TPU v7x, 32 devices: a whole 2x2x4 slice. The times are simulated.
32 devices in a mesh: dp: 8 (over z, x), mp: 4 (over y, core).
Axes of the slice: x: 2, y: 2, z: 4, core: 2. Of those that a mesh axis runs over, the one named last changes fastest.
Arguments:
- tokens: bfloat16 [16384, 768], P('dp'), may hold values from -6 to 6
- segment_ids: int32 [16384], P('dp'), may hold values from 0 to 1, as said below
- slot_valid: int32 [2048], P(('dp', 'mp')), may hold values from 0 to 1
- ln1_gain: bfloat16 [768], P('dp'), may hold values from 0.5 to 1.5
- ln1_bias: bfloat16 [768], P('dp'), may hold values from -1 to 1
- w_qkv: bfloat16 [3, 768, 768], P(None, 'dp', 'mp'), may hold values from -0.21875 to 0.21875
- w_out: bfloat16 [768, 768], P('mp', 'dp'), may hold values from -0.375 to 0.375
- ln2_gain: bfloat16 [768], P('dp'), may hold values from 0.5 to 1.5
- ln2_bias: bfloat16 [768], P('dp'), may hold values from -1 to 1
- w_up: bfloat16 [768, 3072], P('dp', 'mp'), may hold values from -0.21875 to 0.21875
- w_down: bfloat16 [3072, 768], P('mp', 'dp'), may hold values from -0.15625 to 0.15625
- class_tokens: bfloat16 [2048, 768], P(('dp', 'mp')), may hold values from -6 to 6
- image_gain: float32 [768], replicated, may hold values from 0.5 to 1.5
- image_bias: float32 [768], replicated, may hold values from -1.5 to 1.5
- image_proj: bfloat16 [768, 768], replicated, may hold values from -0.21875 to 0.21875
Outputs:
- loss: float32 [], replicated
- block_out: bfloat16 [16384, 768], P('dp')
- token_grad: float32 [16384, 768], P('dp')
- ln1_gain_grad: float32 [768], P('dp')
- ln1_bias_grad: float32 [768], P('dp')
- qkv_grad: float32 [3, 768, 768], P(None, 'dp', 'mp')
- out_grad: float32 [768, 768], P('mp', 'dp')
- ln2_gain_grad: float32 [768], P('dp')
- ln2_bias_grad: float32 [768], P('dp')
- up_grad: float32 [768, 3072], P('dp', 'mp')
- down_grad: float32 [3072, 768], P('mp', 'dp')
Inputs may be any that keep to these rules, and one draw needn't show every extreme that they name: `segment_ids`: in each aligned run of 16 positions the ids are 0 and then 1, each present at least once.
All inputs are finite; a program needn't handle non-finite values.
Results may differ from a plain program's by a relative error of at most 0.012.
The roundings to bfloat16 on the way count: a program that leaves them out, or rounds other values in their place, can miss the bound.
Values may be sent and summed in bfloat16 or wider, within the bound.
A program may use at most 192 MiB of HBM per device.

v0:
```python
import jax
import jax.numpy as jnp
from jax import lax
from jax.sharding import PartitionSpec as P

HEAD_DIM = 64
SEQ_LEN = 16


norm_epsilon = 1e-05
unit_epsilon = 1e-06
logit_scale = 50.0
masked_score = -1e30
tile_rows = 128


def layer_norm(values, gain_vec, bias_vec):
    centred = values - jnp.mean(values, axis=-1, keepdims=True)
    spread = jnp.mean(centred * centred, axis=-1, keepdims=True)
    return centred * lax.rsqrt(spread + norm_epsilon) * gain_vec + bias_vec


def unit_rows(values):
    return values * lax.rsqrt(jnp.sum(values * values, axis=-1, keepdims=True) + unit_epsilon)


def exact_gelu(values):
    return jax.nn.gelu(values, approximate=False)


def end_positions(segment_block):
    count = segment_block.shape[0] // SEQ_LEN
    grid_ids = segment_block.reshape(count, SEQ_LEN)
    first_len = jnp.sum((grid_ids == 0).astype(jnp.int32), axis=1)
    starts = jnp.arange(count, dtype=jnp.int32) * SEQ_LEN
    return jnp.stack([starts + first_len - 1, starts + SEQ_LEN - 1], axis=1).reshape(2 * count)


def contract_rows(left, right):
    return lax.dot_general(
        left, right, (((1,), (1,)), ((), ())), preferred_element_type=jnp.float32
    )


def contract_cols(left, right):
    return lax.dot_general(
        left, right, (((0,), (0,)), ((), ())), preferred_element_type=jnp.float32
    )


def attention_mask(segment_ids, blocks):
    grid_ids = segment_ids.reshape(blocks, tile_rows)
    places = jnp.arange(tile_rows)
    same_sequence = places[:, None] // SEQ_LEN == places[None, :] // SEQ_LEN
    causal = places[:, None] >= places[None, :]
    return (grid_ids[:, :, None] == grid_ids[:, None, :]) & (same_sequence & causal)[None]


def on_device(
    tokens,
    segment_ids,
    slot_valid,
    ln1_gain,
    ln1_bias,
    w_qkv,
    w_out,
    ln2_gain,
    ln2_bias,
    w_up,
    w_down,
    class_tokens,
    image_gain,
    image_bias,
    image_proj,
):
    score_scale = HEAD_DIM ** (-0.5)
    gathered = (
        lax.all_gather(ln1_gain, "dp", axis=0, tiled=True),
        lax.all_gather(ln1_bias, "dp", axis=0, tiled=True),
        lax.all_gather(w_qkv, "dp", axis=1, tiled=True),
        lax.all_gather(w_out, "dp", axis=1, tiled=True),
        lax.all_gather(ln2_gain, "dp", axis=0, tiled=True),
        lax.all_gather(ln2_bias, "dp", axis=0, tiled=True),
        lax.all_gather(w_up, "dp", axis=0, tiled=True),
        lax.all_gather(w_down, "dp", axis=1, tiled=True),
    )
    row_values = tokens.astype(jnp.float32)
    token_count = tokens.shape[0]
    blocks = token_count // tile_rows
    head_local = gathered[2].shape[2] // HEAD_DIM
    normed = layer_norm(
        row_values, gathered[0].astype(jnp.float32), gathered[1].astype(jnp.float32)
    ).astype(jnp.bfloat16)
    projected = jnp.einsum(
        "rd,cde->cre", normed, gathered[2], preferred_element_type=jnp.float32
    ).astype(jnp.bfloat16)
    split = projected.reshape(3, blocks, tile_rows, head_local, HEAD_DIM)
    query_heads, key_heads, value_heads = (split[0], split[1], split[2])
    allowed = attention_mask(segment_ids, blocks)[:, None]
    scores = (
        jnp.einsum("bqhc,bkhc->bhqk", query_heads, key_heads, preferred_element_type=jnp.float32)
        * score_scale
    )
    scores = jnp.where(allowed, scores, masked_score)
    row_lse = jax.nn.logsumexp(scores, axis=-1, keepdims=True)
    probs_fwd = jnp.exp(scores - row_lse)
    mixed = jnp.einsum(
        "bhqk,bkhc->bqhc",
        probs_fwd.astype(jnp.bfloat16),
        value_heads,
        preferred_element_type=jnp.float32,
    )
    mixed = mixed.reshape(token_count, head_local * HEAD_DIM).astype(jnp.bfloat16)
    attended = lax.psum(jnp.dot(mixed, gathered[3], preferred_element_type=jnp.float32), "mp")
    hidden = row_values + attended
    normed_two = layer_norm(
        hidden, gathered[4].astype(jnp.float32), gathered[5].astype(jnp.float32)
    ).astype(jnp.bfloat16)
    upper = jnp.dot(normed_two, gathered[6], preferred_element_type=jnp.float32)
    active = exact_gelu(upper).astype(jnp.bfloat16)
    branch = lax.psum(jnp.dot(active, gathered[7], preferred_element_type=jnp.float32), "mp")
    result = hidden + branch
    ends = end_positions(segment_ids)
    slot_local = slot_valid.shape[0]
    mp_rank = lax.axis_index("mp")
    row_first = lax.axis_index("dp") * ends.shape[0]
    own_offset = mp_rank * slot_local
    pooled = result[ends]
    text_unit = unit_rows(pooled).astype(jnp.bfloat16)
    own_text = lax.dynamic_slice_in_dim(text_unit, own_offset, slot_local, 0)
    image_normed = layer_norm(class_tokens.astype(jnp.float32), image_gain, image_bias).astype(
        jnp.bfloat16
    )
    image_unit = unit_rows(
        jnp.dot(image_normed, image_proj, preferred_element_type=jnp.float32)
    ).astype(jnp.bfloat16)
    all_text, all_image, all_valid = (
        lax.all_gather(own_text, ("dp", "mp"), axis=0, tiled=True),
        lax.all_gather(image_unit, ("dp", "mp"), axis=0, tiled=True),
        lax.all_gather(slot_valid.astype(jnp.bfloat16), ("dp", "mp"), axis=0, tiled=True),
    )
    live = all_valid > 0
    slot_total = all_valid.shape[0]
    row_index = row_first + jnp.arange(text_unit.shape[0], dtype=jnp.int32)
    row_live = live[row_index]
    row_logits = logit_scale * contract_rows(text_unit, all_image)
    text_lse = jax.nn.logsumexp(jnp.where(live[None, :], row_logits, masked_score), axis=1)
    matched = jnp.take_along_axis(row_logits, row_index[:, None], axis=1)[:, 0]
    image_logits = logit_scale * contract_rows(image_unit, all_text)
    image_lse = jax.nn.logsumexp(jnp.where(live[None, :], image_logits, masked_score), axis=1)
    own_live = slot_valid > 0
    own_matched = lax.dynamic_slice_in_dim(matched, own_offset, slot_local)
    own_text_lse = lax.dynamic_slice_in_dim(text_lse, own_offset, slot_local)
    partial_loss = 0.5 * jnp.sum(
        jnp.where(own_live, own_text_lse - own_matched, 0.0)
        + jnp.where(own_live, image_lse - own_matched, 0.0)
    )
    loss = lax.psum(partial_loss, ("dp", "mp")) / slot_total
    all_image_lse = lax.all_gather(image_lse, ("dp", "mp"), axis=0, tiled=True)
    pair_live = row_live[:, None] & live[None, :]
    spread = jnp.exp(row_logits - text_lse[:, None]) + jnp.exp(row_logits - all_image_lse[None, :])
    columns = jnp.arange(slot_total, dtype=jnp.int32)
    target = (columns[None, :] == row_index[:, None]) & row_live[:, None]
    grad_logits = jnp.where(pair_live, 0.5 * spread, 0.0) - target.astype(jnp.float32)
    cosine_grad = (logit_scale * grad_logits).astype(jnp.bfloat16)
    unit_grad = jnp.dot(cosine_grad, all_image, preferred_element_type=jnp.float32)
    unit_out, unit_pull = jax.vjp(unit_rows, pooled)
    pooled_grad = unit_pull(unit_grad)[0]
    result_grad = jnp.zeros_like(result).at[ends].set(pooled_grad)
    again = (
        lax.all_gather(ln1_gain, "dp", axis=0, tiled=True),
        lax.all_gather(ln1_bias, "dp", axis=0, tiled=True),
        lax.all_gather(w_qkv, "dp", axis=1, tiled=True),
        lax.all_gather(w_out, "dp", axis=1, tiled=True),
        lax.all_gather(ln2_gain, "dp", axis=0, tiled=True),
        lax.all_gather(ln2_bias, "dp", axis=0, tiled=True),
        lax.all_gather(w_up, "dp", axis=0, tiled=True),
        lax.all_gather(w_down, "dp", axis=1, tiled=True),
    )
    branch_grad = result_grad.astype(jnp.bfloat16)
    down_local = contract_cols(active, branch_grad)
    active_grad = contract_rows(branch_grad, again[7])
    gelu_out, gelu_pull = jax.vjp(exact_gelu, upper)
    upper_grad = gelu_pull(active_grad)[0].astype(jnp.bfloat16)
    up_local = contract_cols(normed_two, upper_grad)
    normed_two_grad = lax.psum(contract_rows(upper_grad, again[6]), "mp")
    norm_two_out, norm_two_pull = jax.vjp(
        layer_norm, hidden, again[4].astype(jnp.float32), again[5].astype(jnp.float32)
    )
    hidden_part, gain_two_grad, bias_two_grad = norm_two_pull(normed_two_grad)
    hidden_grad = result_grad + hidden_part
    attended_grad = hidden_grad.astype(jnp.bfloat16)
    out_local = contract_cols(mixed, attended_grad)
    mixed_grad = contract_rows(attended_grad, again[3]).astype(jnp.bfloat16)
    mixed_grad = mixed_grad.reshape(blocks, tile_rows, head_local, HEAD_DIM)
    scores_again = (
        jnp.einsum("bqhc,bkhc->bhqk", query_heads, key_heads, preferred_element_type=jnp.float32)
        * score_scale
    )
    scores_again = jnp.where(allowed, scores_again, masked_score)
    probs_back = jnp.exp(scores_again - row_lse)
    probs_grad = jnp.einsum(
        "bqhc,bkhc->bhqk", mixed_grad, value_heads, preferred_element_type=jnp.float32
    )
    value_grad = jnp.einsum(
        "bhqk,bqhc->bkhc",
        probs_back.astype(jnp.bfloat16),
        mixed_grad,
        preferred_element_type=jnp.float32,
    )
    centre = jnp.sum(probs_grad * probs_back, axis=-1, keepdims=True)
    score_grad = (probs_back * (probs_grad - centre)).astype(jnp.bfloat16)
    query_grad = (
        jnp.einsum("bhqk,bkhc->bqhc", score_grad, key_heads, preferred_element_type=jnp.float32)
        * score_scale
    )
    key_grad = (
        jnp.einsum("bhqk,bqhc->bkhc", score_grad, query_heads, preferred_element_type=jnp.float32)
        * score_scale
    )
    proj_grad = (
        jnp.stack([query_grad, key_grad, value_grad])
        .reshape(3, token_count, head_local * HEAD_DIM)
        .astype(jnp.bfloat16)
    )
    qkv_local = jnp.einsum("rd,cre->cde", normed, proj_grad, preferred_element_type=jnp.float32)
    normed_grad = lax.psum(
        jnp.einsum("cre,cde->rd", proj_grad, again[2], preferred_element_type=jnp.float32), "mp"
    )
    norm_one_out, norm_one_pull = jax.vjp(
        layer_norm, row_values, again[0].astype(jnp.float32), again[1].astype(jnp.float32)
    )
    rows_part, gain_one_grad, bias_one_grad = norm_one_pull(normed_grad)
    token_grad = hidden_grad + rows_part
    summed = (
        lax.psum_scatter(gain_one_grad, "dp", scatter_dimension=0, tiled=True),
        lax.psum_scatter(bias_one_grad, "dp", scatter_dimension=0, tiled=True),
        lax.psum_scatter(qkv_local, "dp", scatter_dimension=1, tiled=True),
        lax.psum_scatter(out_local, "dp", scatter_dimension=1, tiled=True),
        lax.psum_scatter(gain_two_grad, "dp", scatter_dimension=0, tiled=True),
        lax.psum_scatter(bias_two_grad, "dp", scatter_dimension=0, tiled=True),
        lax.psum_scatter(up_local, "dp", scatter_dimension=0, tiled=True),
        lax.psum_scatter(down_local, "dp", scatter_dimension=1, tiled=True),
    )
    return (
        loss,
        result.astype(jnp.bfloat16),
        token_grad,
        summed[0],
        summed[1],
        summed[2],
        summed[3],
        summed[4],
        summed[5],
        summed[6],
        summed[7],
    )


def solution(mesh):
    placed = (
        P("dp", None),
        P("dp"),
        P(("dp", "mp")),
        P("dp"),
        P("dp"),
        P(None, "dp", "mp"),
        P("mp", "dp"),
        P("dp"),
        P("dp"),
        P("dp", "mp"),
        P("mp", "dp"),
        P(("dp", "mp"), None),
        P(),
        P(),
        P(),
    )
    return jax.shard_map(
        on_device,
        mesh=mesh,
        in_specs=placed,
        out_specs=(
            P(),
            P("dp", None),
            P("dp", None),
            P("dp"),
            P("dp"),
            P(None, "dp", "mp"),
            P("mp", "dp"),
            P("dp"),
            P("dp"),
            P("dp", "mp"),
            P("mp", "dp"),
        ),
        check_vma=False,
    )
```

profile of v0, /device:TPU:0, one launch (start us, length us, event | category | flops | bytes accessed | tf_op | source)
XLA Modules:
  0.0 992.5 jit_solution(5415597537768030256)
XLA Ops:
  13.5 23.3 %all-reduce.12 = (bf16[768]{0:T(1024)(128)(2,1)S(1)}, bf16[768]{0:T(1024)(128)(2,1)S(1)}, bf16[768]{0:T(1024)(128)(2,1)S(1)}, bf16[768]{0:T(1024)(128)(2,1)S(1)}) all-reduce(bf16[768]{0:T(1024)(128)(2,1)S(1)} %dynamic-update-slice.2, bf16[768]{0:T(1024)(128)(2,1)S(1)} %dynamic-update-slice.1, ...), channel_id=1, replica_groups=mesh['dp'=8,'mp'=4] {'dp'}, use_global_device_ids=true, to_apply=%add.2 | all-reduce | flops 3072 | bytes 12288
  42.9 35.3 %all_gather.45 = bf16[3,768,192]{2,0,1:T(4,128)(2,1)S(1)} all-gather(bf16[3,96,192]{2,0,1:T(4,128)(2,1)S(1)} %copy.61), channel_id=1, replica_groups=mesh['dp'=8,'mp'=4] {'dp'}, dimensions={1}, use_global_device_ids=true | all-gather | bytes 995328 | tf_op jit(solution)/shard_map/all_gather | solution.py:80
  90.5 31.1 %all_gather.46 = bf16[192,768]{0,1:T(8,128)(2,1)S(1)} all-gather(bf16[192,96]{0,1:T(8,128)(2,1)S(1)} %copy.68), channel_id=1, replica_groups=mesh['dp'=8,'mp'=4] {'dp'}, dimensions={1}, use_global_device_ids=true | all-gather | bytes 331776 | tf_op jit(solution)/shard_map/all_gather | solution.py:81
  126.8 117.9 %all-reduce.18.cloned.1.call-done = f32[2048,768]{1,0:T(8,128)} async-done(((f32[2048,768]{1,0:T(8,128)}), f32[2048,768]{1,0:T(8,128)}) %all-reduce.18.cloned.1.call-update) | async-done | bytes 6291472 | tf_op jit(solution)/shard_map/psum | solution.py:114
  254.2 18.7 %multiply_convert_fusion = (bf16[2048,768]{1,0:T(8,128)(2,1)}, f32[2048,768]{1,0:T(8,128)}, f32[2048,768]{1,0:T(8,128)}) fusion(bf16[2048,768]{1,0:T(8,128)(2,1)} %add_convert_fusion.1, bf16[768,768]{1,0:T(8,128)(2,1)} %all-gather.5.cloned.1.call-done), kind=kOutput, calls=%fused_computation.27 | convolution fusion | flops 2518155264 | bytes 20054016 | tf_op jit(solution)/shard_map/dot_general | solution.py:119
  272.9 7.5 fusion.108
  284.8 123.2 %all-reduce.20.cloned.1.call-done = f32[2048,768]{1,0:T(8,128)} async-done(((f32[2048,768]{1,0:T(8,128)}), f32[2048,768]{1,0:T(8,128)}) %all-reduce.20.cloned.1.call-update) | async-done | bytes 6291472 | tf_op jit(solution)/shard_map/psum | solution.py:121
  408.0 9.2 fusion.103
  423.5 40.1 %all-reduce = bf16[2048]{0:T(1024)(128)(2,1)S(1)} all-reduce(bf16[2048]{0:T(1024)(128)(2,1)S(1)} %dynamic-update-slice), channel_id=1, replica_groups=mesh['dp'=8,'mp'=4] {'dp','mp'}, use_global_device_ids=true, to_apply=%add | all-reduce | flops 2048 | bytes 8192
  465.7 4.4 select_reduce_fusion
  470.1 4.5 gather_fusion.2
  476.7 6.2 all-gather.11.cloned.1.call-done
  487.7 38.2 %all-reduce.10 = (f32[]{:T(128)}, f32[2048]{0:T(1024)S(1)}) all-reduce(f32[]{:T(128)S(6)} %mul.314, f32[2048]{0:T(1024)S(1)} %get-tuple-element.72), channel_id=1, replica_groups=mesh['dp'=8,'mp'=4] {'dp','mp'}, use_global_device_ids=true, to_apply=%region_18.19 | all-reduce | flops 2049 | bytes 16392 | tf_op jit(solution)/shard_map/psum | solution.py:158
  525.8 5.4 multiply_reduce_fusion.4
  531.3 5.2 scatter_custom_fusion
  536.5 11.1 %add_convert_fusion = bf16[2048,768]{1,0:T(8,128)(2,1)S(1)} fusion(f32[2048,768]{1,0:T(8,128)} %get-tuple-element.66, f32[2048,768]{1,0:T(8,128)} %get-tuple-element.80, bf16[768,768]{0,1:T(8,128)(2,1)} %all-gather.7.cloned.1.call-done, f32[2048,768]{1,0:T(8,128)} %scatter_custom_fusion), kind=kOutput, calls=%fused_computation.26 | convolution fusion | flops 2439512064 | bytes 23199744 | tf_op jit(solution)/shard_map/dot_general | solution.py:40
  549.3 4.5 fusion.109
  554.1 120.4 %all-reduce.22.cloned.1.call-done = f32[2048,768]{1,0:T(8,128)} async-done(((f32[2048,768]{1,0:T(8,128)}), f32[2048,768]{1,0:T(8,128)}) %all-reduce.22.cloned.1.call-update) | async-done | bytes 6291472 | tf_op jit(solution)/shard_map/psum | solution.py:186
  674.5 5.8 multiply_reduce_fusion
  680.9 6.0 fusion.102
  711.4 7.2 convolution_bitcast_fusion
  719.4 4.9 fusion.34
  727.1 4.7 reshape.481
  731.8 8.0 fusion.28
  740.1 7.1 fusion.110
  748.5 19.9 %reduce-scatter.15.cloned.1.call-done = f32[96,192]{1,0:T(8,128)} async-done(((f32[768,192]{1,0:T(8,128)}), f32[96,192]{1,0:T(8,128)}) %reduce-scatter.15.cloned.1.call-update) | async-done | bytes 73744
  770.0 68.6 %all-reduce.24.cloned.1.call-done = f32[2048,768]{1,0:T(8,128)} async-done(((f32[2048,768]{1,0:T(8,128)}), f32[2048,768]{1,0:T(8,128)}) %all-reduce.24.cloned.1.call-update) | async-done | bytes 6291472 | tf_op jit(solution)/shard_map/psum | solution.py:227
  838.6 4.8 fusion.101
  848.6 37.7 %all-reduce.11 = (f32[768]{0:T(1024)S(1)}, f32[768]{0:T(1024)S(1)}, f32[768]{0:T(1024)S(1)}, f32[768]{0:T(1024)S(1)}) all-reduce(f32[768]{0:T(1024)S(1)} %get-tuple-element.46, f32[768]{0:T(1024)S(1)} %get-tuple-element.49, f32[768]{0:T(1024)S(1)} %get-tuple-element.44, ...), channel_id=2, replica_groups=mesh['dp'=8,'mp'=4] {'dp'}, use_global_device_ids=true, to_apply=%region_29.30.clone | all-reduce | flops 3072 | bytes 24576
  888.6 8.8 add_add_fusion.2
  899.3 12.0 %reduce-scatter.11.cloned.1.call-done = f32[768,96]{0,1:T(8,128)} async-done(((f32[768,768]{0,1:T(8,128)}), f32[768,96]{0,1:T(8,128)}) %reduce-scatter.11.cloned.1.call-update) | async-done | bytes 294928 | tf_op jit(solution)/shard_map/reduce_scatter | solution.py:243
  911.4 72.4 %reduce-scatter.9.cloned.1.call-done = f32[96,768]{1,0:T(8,128)} async-done(((f32[768,768]{1,0:T(8,128)}), f32[96,768]{1,0:T(8,128)}) %reduce-scatter.9.cloned.1.call-update) | async-done | bytes 294928 | tf_op jit(solution)/shard_map/reduce_scatter | solution.py:242
  (219 shorter events, 97.9 us)
Async XLA Ops:
  8.0 273.6 %copy-start = (bf16[768,768]{1,0:T(8,128)(2,1)S(1)}, bf16[768,768]{1,0:T(8,128)(2,1)}, u32[]{:S(2)}) copy-start(bf16[768,768]{1,0:T(8,128)(2,1)} %param.29) | copy-start | bytes 3538948
  8.0 34.8 %copy-start.18 = (bf16[3,96,192]{2,1,0:T(8,128)(2,1)S(1)}, bf16[3,96,192]{2,1,0:T(8,128)(2,1)}, u32[]{:S(2)}) copy-start(bf16[3,96,192]{2,1,0:T(8,128)(2,1)} %param.20) | copy-start | bytes 331780
  8.0 236.7 %all-reduce.18.cloned.1.call-start = ((), (), s32[]{:S(2)}) async-start(), calls=%async_computation.4 | async-start | bytes 12582912 | tf_op jit(solution)/shard_map/psum | solution.py:114
  36.8 47.7 %copy-start.26 = (f32[768]{0:T(1024)}, f32[768]{0:T(1024)S(1)}, u32[]{:S(2)}) copy-start(f32[768]{0:T(1024)S(1)} %convert_element_type.93) | copy-start | bytes 9220
  36.9 47.7 %copy-start.31 = (f32[768]{0:T(1024)}, f32[768]{0:T(1024)S(1)}, u32[]{:S(2)}) copy-start(f32[768]{0:T(1024)S(1)} %convert_element_type.94) | copy-start | bytes 9220
  39.2 45.3 %copy-start.16 = (f32[2048]{0:T(1024)}, f32[2048]{0:T(1024)S(1)}, u32[]{:S(2)}) copy-start(f32[2048]{0:T(1024)S(1)} %broadcast_multiply_fusion.1) | copy-start | bytes 24580
  42.8 41.7 %copy-start.24 = (f32[2048]{0:T(1024)}, f32[2048]{0:T(1024)S(1)}, u32[]{:S(2)}) copy-start(f32[2048]{0:T(1024)S(1)} %fusion.82) | copy-start | bytes 24580
  125.4 128.8 %all-gather.5.cloned.1.call-start = ((), (), s32[]{:S(2)}) async-start(), calls=%async_computation.5 | async-start | bytes 1327104 | tf_op jit(solution)/shard_map/all_gather | solution.py:84
  126.0 146.9 %all-gather.7.cloned.1.call-start = ((), (), s32[]{:S(2)}) async-start(), calls=%async_computation.6 | async-start | bytes 1327104 | tf_op jit(solution)/shard_map/all_gather | solution.py:85
  126.6 281.5 %all-reduce.20.cloned.1.call-start = ((), (), s32[]{:S(2)}) async-start(), calls=%async_computation.7 | async-start | bytes 12582912 | tf_op jit(solution)/shard_map/psum | solution.py:121
  126.8 123.2 %copy-start.28 = (f32[768]{0:T(1024)}, f32[768]{0:T(1024)S(1)}, u32[]{:S(2)}) copy-start(f32[768]{0:T(1024)S(1)} %convert_element_type.102) | copy-start | bytes 9220
  250.0 22.9 %copy-start.21 = (f32[2048]{0:T(1024)}, f32[2048]{0:T(1024)S(1)}, u32[]{:S(2)}) copy-start(f32[2048]{0:T(1024)S(1)} %multiply_reduce_fusion.2) | copy-start | bytes 24580
  280.4 185.3 %all-gather.9.cloned.1.call-start = ((), (), s32[]{:S(2)}) async-start(), calls=%async_computation.8 | async-start | bytes 3244032 | tf_op jit(solution)/shard_map/all_gather | solution.py:139
  283.5 199.4 %all-gather.11.cloned.1.call-start = ((), (), s32[]{:S(2)}) async-start(), calls=%async_computation.9 | async-start | bytes 3244032 | tf_op jit(solution)/shard_map/all_gather | solution.py:138
  417.3 6.0 copy-start.33
  421.5 61.5 %copy-start.14 = (bf16[64,768]{1,0:T(8,128)(2,1)S(1)}, bf16[64,768]{1,0:T(8,128)(2,1)}, u32[]{:S(2)}) copy-start(bf16[64,768]{1,0:T(8,128)(2,1)} %multiply_convert_fusion.7) | copy-start | bytes 294916
  423.2 251.3 %all-reduce.22.cloned.1.call-start = ((), (), s32[]{:S(2)}) async-start(), calls=%async_computation.10 | async-start | bytes 12582912 | tf_op jit(solution)/shard_map/psum | solution.py:186
  536.5 12.8 %copy-start.34 = (bf16[768,768]{1,0:T(8,128)(2,1)S(1)}, bf16[768,768]{1,0:T(8,128)(2,1)}, u32[]{:S(2)}) copy-start(bf16[768,768]{1,0:T(8,128)(2,1)} %all-gather.5.cloned.1.call-done) | copy-start | bytes 3538948
  553.8 120.7 %copy-start.29 = (f32[768]{0:T(1024)S(1)}, f32[768]{0:T(1024)}, u32[]{:S(2)}) copy-start(f32[768]{0:T(1024)} %copy-done.28) | copy-start | bytes 9220
  553.8 126.5 %copy-start.22 = (f32[2048]{0:T(1024)S(1)}, f32[2048]{0:T(1024)}, u32[]{:S(2)}) copy-start(f32[2048]{0:T(1024)} %copy-done.21) | copy-start | bytes 24580
  553.9 214.5 %reduce-scatter.15.cloned.1.call-start = ((), (), s32[]{:S(2)}) async-start(), calls=%async_computation.15 | async-start | bytes 884736
  674.5 6.4 copy-start.7
  674.5 12.4 %slice-start = ((s8[6291456]{0:T(1024)(128)(4,1)}), s8[4194304]{0:T(1024)(128)(4,1)S(1)}, s32[]{:S(2)}) async-start(s8[6291456]{0:T(1024)(128)(4,1)} %bitcast.123), calls=%async_computation.16 | async-start | bytes 8388608
  680.9 6.0 slice-start.1
  690.8 11.4 %copy-start.3 = (f32[2048,768]{1,0:T(8,128)}, f32[2048,768]{1,0:T(8,128)S(1)}, u32[]{:S(2)}) copy-start(f32[2048,768]{1,0:T(8,128)S(1)} %add_add_fusion.3) | copy-start | bytes 18874372
  690.8 6.2 copy-start.12
  705.4 133.2 %all-reduce.24.cloned.1.call-start = ((), (), s32[]{:S(2)}) async-start(), calls=%async_computation.11 | async-start | bytes 12582912 | tf_op jit(solution)/shard_map/psum | solution.py:227
  718.7 178.7 %reduce-scatter.13.cloned.1.call-start = ((), (), s32[]{:S(2)}) async-start(), calls=%async_computation.14 | async-start | bytes 2211840
  731.8 179.6 %reduce-scatter.11.cloned.1.call-start = ((), (), s32[]{:S(2)}) async-start(), calls=%async_computation.13 | async-start | bytes 2654208 | tf_op jit(solution)/shard_map/reduce_scatter | solution.py:243
  739.8 243.9 %reduce-scatter.9.cloned.1.call-start = ((), (), s32[]{:S(2)}) async-start(), calls=%async_computation.12 | async-start | bytes 2654208 | tf_op jit(solution)/shard_map/reduce_scatter | solution.py:242
  747.2 96.2 %copy-start.20 = (f32[2048]{0:T(1024)S(1)}, f32[2048]{0:T(1024)}, u32[]{:S(2)}) copy-start(f32[2048]{0:T(1024)} %copy-done.19) | copy-start | bytes 24580
  888.6 95.2 %copy-start.1 = (bf16[768,768]{1,0:T(8,128)(2,1)S(1)}, bf16[768,768]{1,0:T(8,128)(2,1)}, u32[]{:S(2)}) copy-start(bf16[768,768]{1,0:T(8,128)(2,1)} %param.29) | copy-start | bytes 3538948
  (18 other events, 34.6 us)
Sparse Core Ops, SparseCore 0:
  125.5 119.2 all-reduce.17
  280.5 127.4 all-reduce.19
  554.0 120.5 all-reduce.21
  718.8 119.7 all-reduce.23
Sparse Core Ops, SparseCore 1:
  128.0 40.9 all-gather.4
  171.1 39.8 all-gather.6
  284.3 100.7 all-gather.8
  423.3 59.6 all-gather.10
  705.5 62.8 reduce-scatter.14
  772.3 66.4 reduce-scatter.12
  842.7 68.6 reduce-scatter.10
  915.3 68.4 reduce-scatter.8
where the time goes:
time: 1000 us; the launch traced here: 992 us
  waiting for transfers between devices  542 us (54%)
  blocking collectives  206 us (21%)
  matrix products  102 us (10%)
  other arithmetic  69.3 us (7%)
  local copies, waits for them, and re-layouts  51.3 us (5%)
  between operations  20.4 us (2%)
    psum x1, waiting for transfers between devices, on_device(): lax.psum(jnp.dot(active, gathered[7], preferred_element_type=jnp.float32)...  123 us
    psum x1, waiting for transfers between devices, on_device(): normed_two_grad = lax.psum(contract_rows(upper_grad, again[6]), 'mp')  120 us
    psum x1, waiting for transfers between devices, on_device(): lax.psum(jnp.dot(mixed, gathered[3], preferred_element_type=jnp.float32),...  118 us
    unnamed x3, blocking collectives  101 us
    reduce_scatter x1, waiting for transfers between devices, on_device(): lax.psum_scatter(up_local, 'dp', scatter_dimension=0, tiled=True)  72.4 us
    psum x1, waiting for transfers between devices, on_device(): lax.psum(jnp.einsum('cre,cde->rd', proj_grad, again[2], preferred_element...  68.6 us
    psum x1, blocking collectives, on_device(): loss = lax.psum(partial_loss, ('dp', 'mp')) / slot_total  38.2 us
    all_gather x1, blocking collectives, on_device(): lax.all_gather(w_qkv, 'dp', axis=1, tiled=True)  35.3 us
  transfers between devices with their start and end apart: 12, of which 8 were waited for; matrix products, arithmetic and copies ran while one was open for 12% of the time, Pallas kernels for 0%

commit v1 on v0

v1 whole, which is shorter than its diff:
```python
import jax
import jax.numpy as jnp
from jax import lax
from jax.sharding import PartitionSpec as P

HEAD_DIM = 64
SEQ_LEN = 16
norm_epsilon = 1e-05
unit_epsilon = 1e-06
logit_scale = 50.0
tile_rows = 128
f32, bf16 = jnp.float32, jnp.bfloat16


def standardise(values):
    centred = values - jnp.mean(values, axis=-1, keepdims=True)
    rstd = lax.rsqrt(jnp.mean(centred * centred, axis=-1, keepdims=True) + norm_epsilon)
    return centred * rstd, rstd


def norm_pull(grad, hat, rstd, gain):
    scaled = grad * gain
    first = jnp.mean(scaled, axis=-1, keepdims=True)
    second = jnp.mean(scaled * hat, axis=-1, keepdims=True)
    return rstd * (scaled - first - hat * second)


def inverse_norm(values):
    return lax.rsqrt(jnp.sum(values * values, axis=-1, keepdims=True) + unit_epsilon)


def nn(left, right):
    return lax.dot_general(left, right, (((1,), (0,)), ((), ())), preferred_element_type=f32)


def nt(left, right):
    return lax.dot_general(left, right, (((1,), (1,)), ((), ())), preferred_element_type=f32)


def tn(left, right):
    return lax.dot_general(left, right, (((0,), (0,)), ((), ())), preferred_element_type=f32)


def phi(values):
    return 0.5 * lax.erfc(-values * (0.5**0.5))


def make(dp_size, mp_size):
    def on_device(
        tokens,
        segment_ids,
        slot_valid,
        ln1_gain,
        ln1_bias,
        w_qkv,
        w_out,
        ln2_gain,
        ln2_bias,
        w_up,
        w_down,
        class_tokens,
        image_gain,
        image_bias,
        image_proj,
    ):
        both = ("dp", "mp")
        dp_rank, mp_rank = lax.axis_index("dp"), lax.axis_index("mp")
        depth = w_up.shape[0]
        width = depth * dp_size
        head_cols = w_out.shape[0]
        heads = head_cols // HEAD_DIM
        rows = tokens.shape[0] // mp_size
        seqs = rows // SEQ_LEN
        slots = slot_valid.shape[0]
        slot_total = slots * dp_size * mp_size

        packed = jnp.stack(
            [jnp.concatenate([w_qkv[0], w_qkv[1], w_qkv[2], w_out.T], axis=1), w_up, w_down.T]
        )
        norms = jnp.stack([ln1_gain, ln1_bias, ln2_gain, ln2_bias])
        image_hat, _ = standardise(class_tokens.astype(f32))
        image_normed = (image_hat * image_gain + image_bias).astype(bf16)
        image_raw = nn(image_normed, image_proj)
        image_unit = (image_raw * inverse_norm(image_raw)).astype(bf16)

        weights = lax.all_gather(packed, both, axis=0).reshape(dp_size, mp_size, 3, depth, -1)
        weights = weights.transpose(2, 1, 0, 3, 4).reshape(3, mp_size, width, -1)
        vectors = lax.all_gather(norms, "dp", axis=1, tiled=True).astype(f32)
        all_image = lax.all_gather(image_unit, both, axis=0, tiled=True)
        all_valid = lax.all_gather(slot_valid.astype(bf16), both, axis=0, tiled=True) > 0

        own = lax.dynamic_slice_in_dim(tokens, mp_rank * rows, rows, 0).astype(f32)
        ids = lax.dynamic_slice_in_dim(segment_ids, mp_rank * rows, rows, 0)
        grid_ids = ids.reshape(seqs, SEQ_LEN)
        first_len = jnp.sum((grid_ids == 0).astype(jnp.int32), axis=1)
        starts = jnp.arange(seqs, dtype=jnp.int32) * SEQ_LEN
        ends = jnp.stack([starts + first_len - 1, starts + SEQ_LEN - 1], axis=1).reshape(2 * seqs)
        place = (ends[:, None] == jnp.arange(rows)[None, :]).astype(bf16)

        hat_one, rstd_one = standardise(own)
        normed = (hat_one * vectors[0] + vectors[1]).astype(bf16)
        attn = weights[0]
        qkv = jnp.einsum("rd,mde->mre", normed, attn[:, :, : 3 * head_cols], preferred_element_type=f32)
        qkv = qkv.astype(bf16).reshape(mp_size, rows, 3, heads, HEAD_DIM)
        blocks = rows // tile_rows
        split = qkv.reshape(mp_size, blocks, tile_rows, 3, heads, HEAD_DIM)
        query, key, value = split[:, :, :, 0], split[:, :, :, 1], split[:, :, :, 2]
        tile_ids = ids.reshape(blocks, tile_rows)
        spots = jnp.arange(tile_rows)
        allowed = (
            (tile_ids[:, :, None] == tile_ids[:, None, :])
            & (spots[:, None] // SEQ_LEN == spots[None, :] // SEQ_LEN)[None]
            & (spots[:, None] >= spots[None, :])[None]
        )[None, :, None]
        scale = HEAD_DIM**-0.5
        scores = jnp.einsum("mbqhc,mbkhc->mbhqk", query, key, preferred_element_type=f32) * scale
        scores = jnp.where(allowed, scores, -1e30)
        probs = jax.nn.softmax(scores, axis=-1)
        mixed = jnp.einsum("mbhqk,mbkhc->mbqhc", probs.astype(bf16), value, preferred_element_type=f32)
        mixed = mixed.astype(bf16).reshape(mp_size, rows, head_cols)
        out_t = attn[:, :, 3 * head_cols :]
        attended = jnp.einsum("mre,mde->rd", mixed, out_t, preferred_element_type=f32)
        hidden = own + attended

        def feed(rows_in):
            hat, rstd = standardise(rows_in)
            normed_two = (hat * vectors[2] + vectors[3]).astype(bf16)
            upper = jnp.einsum("rd,mdf->mrf", normed_two, weights[1], preferred_element_type=f32)
            active = (upper * phi(upper)).astype(bf16)
            branch = jnp.einsum("mrf,mdf->rd", active, weights[2], preferred_element_type=f32)
            return hat, rstd, normed_two, upper, active, rows_in + branch

        block_out = feed(hidden)[-1].astype(bf16)
        hidden_ends = hidden[ends]
        hat_two, rstd_two, normed_two, upper, active, pooled = feed(hidden_ends)

        scale_back = inverse_norm(pooled)
        text = (pooled * scale_back).astype(bf16)
        logits = logit_scale * nt(text, all_image)
        live = slot_valid > 0
        weight = jnp.exp(logits)
        row_sum = jnp.sum(jnp.where(all_valid[None, :], weight, 0.0), axis=1)
        col_part = jnp.sum(jnp.where(live[:, None], weight, 0.0), axis=0)
        row_index = (dp_rank * mp_size + mp_rank) * slots + jnp.arange(slots)
        target = jnp.arange(slot_total)[None, :] == row_index[:, None]
        matched = jnp.sum(jnp.where(target, logits, 0.0), axis=1)
        row_part = jnp.sum(jnp.where(live, jnp.log(row_sum) - 2.0 * matched, 0.0))
        sums = lax.psum(jnp.concatenate([col_part, row_part[None]]), both)
        col_sum = sums[:slot_total]
        loss = 0.5 * (sums[slot_total] + jnp.sum(jnp.where(all_valid, jnp.log(col_sum), 0.0))) / slot_total
        pair = live[:, None] & all_valid[None, :]
        spread = 0.5 * weight * (1.0 / row_sum[:, None] + 1.0 / col_sum[None, :])
        grad_logits = jnp.where(pair, spread, 0.0) - (target & live[:, None]).astype(f32)
        cosine_grad = (logit_scale * grad_logits).astype(bf16)
        unit_grad = nn(cosine_grad, all_image)
        along = jnp.sum(unit_grad * pooled, axis=-1, keepdims=True)
        pooled_grad = scale_back * unit_grad - pooled * (scale_back * scale_back * scale_back * along)

        branch_grad = pooled_grad.astype(bf16)
        down_local = jnp.einsum("rd,mrf->mdf", branch_grad, active, preferred_element_type=f32)
        active_grad = jnp.einsum("rd,mdf->mrf", branch_grad, weights[2], preferred_element_type=f32)
        slope = phi(upper) + upper * jnp.exp(-0.5 * upper * upper) * (1.0 / (2.0 * jnp.pi) ** 0.5)
        upper_grad = (active_grad * slope).astype(bf16)
        up_local = jnp.einsum("rd,mrf->mdf", normed_two, upper_grad, preferred_element_type=f32)
        normed_two_grad = jnp.einsum("mrf,mdf->rd", upper_grad, weights[1], preferred_element_type=f32)
        gain_two = jnp.sum(normed_two_grad * hat_two, axis=0)
        bias_two = jnp.sum(normed_two_grad, axis=0)
        hidden_grad = pooled_grad + norm_pull(normed_two_grad, hat_two, rstd_two, vectors[2])

        attended_grad = hidden_grad.astype(bf16)
        mixed_ends = mixed[:, ends]
        out_local = jnp.einsum("rd,mre->mde", attended_grad, mixed_ends, preferred_element_type=f32)
        mixed_grad = jnp.einsum("rd,mde->mre", attended_grad, out_t, preferred_element_type=f32).astype(bf16)
        mixed_grad = mixed_grad.reshape(mp_size, 2 * seqs, heads, HEAD_DIM)
        query_ends, keys, values = qkv[:, ends, 0], qkv[:, :, 1], qkv[:, :, 2]
        spot = jnp.arange(rows)
        allowed_ends = (
            (ids[ends][:, None] == ids[None, :])
            & (ends[:, None] // SEQ_LEN == spot[None, :] // SEQ_LEN)
            & (ends[:, None] >= spot[None, :])
        )[None, None]
        again = jnp.einsum("mqhc,mkhc->mhqk", query_ends, keys, preferred_element_type=f32) * scale
        probs_ends = jax.nn.softmax(jnp.where(allowed_ends, again, -1e30), axis=-1)
        probs_grad = jnp.einsum("mqhc,mkhc->mhqk", mixed_grad, values, preferred_element_type=f32)
        value_grad = jnp.einsum("mhqk,mqhc->mkhc", probs_ends.astype(bf16), mixed_grad, preferred_element_type=f32)
        centre = jnp.sum(probs_grad * probs_ends, axis=-1, keepdims=True)
        score_grad = (probs_ends * (probs_grad - centre)).astype(bf16)
        query_grad = jnp.einsum("mhqk,mkhc->mqhc", score_grad, keys, preferred_element_type=f32) * scale
        key_grad = jnp.einsum("mhqk,mqhc->mkhc", score_grad, query_ends, preferred_element_type=f32) * scale
        query_grad = query_grad.astype(bf16).reshape(mp_size, 2 * seqs, head_cols)
        query_grad = jnp.einsum("er,mec->mrc", place, query_grad, preferred_element_type=f32).astype(bf16)
        proj_grad = jnp.concatenate(
            [
                query_grad,
                key_grad.astype(bf16).reshape(mp_size, rows, head_cols),
                value_grad.astype(bf16).reshape(mp_size, rows, head_cols),
            ],
            axis=-1,
        )
        qkv_local = jnp.einsum("rd,mre->mde", normed, proj_grad, preferred_element_type=f32)
        normed_grad = jnp.einsum("mre,mde->rd", proj_grad, attn[:, :, : 3 * head_cols], preferred_element_type=f32)
        gain_one = jnp.sum(normed_grad * hat_one, axis=0)
        bias_one = jnp.sum(normed_grad, axis=0)
        token_grad = norm_pull(normed_grad, hat_one, rstd_one, vectors[0])
        token_grad = token_grad.at[ends].add(hidden_grad)

        local = jnp.stack([jnp.concatenate([qkv_local, out_local], axis=-1), up_local, down_local])
        local = local.reshape(3, mp_size, dp_size, depth, -1).transpose(2, 1, 0, 3, 4)
        local = local.reshape(dp_size * mp_size, 3, depth, -1)
        summed = lax.psum_scatter(local, both, scatter_dimension=0, tiled=False)
        vector_local = lax.psum(jnp.stack([gain_one, bias_one, gain_two, bias_two]), both)
        vector_own = lax.dynamic_slice_in_dim(vector_local, dp_rank * depth, depth, 1)

        block_out = lax.all_gather(block_out, "mp", axis=0, tiled=True)
        token_grad = lax.all_gather(token_grad, "mp", axis=0, tiled=True)
        qkv_grad = summed[0, :, : 3 * head_cols].reshape(depth, 3, head_cols).transpose(1, 0, 2)
        return (
            loss,
            block_out,
            token_grad,
            vector_own[0],
            vector_own[1],
            qkv_grad,
            summed[0, :, 3 * head_cols :].T,
            vector_own[2],
            vector_own[3],
            summed[1],
            summed[2].T,
        )

    return on_device


def solution(mesh):
    placed = (
        P("dp", None),
        P("dp"),
        P(("dp", "mp")),
        P("dp"),
        P("dp"),
        P(None, "dp", "mp"),
        P("mp", "dp"),
        P("dp"),
        P("dp"),
        P("dp", "mp"),
        P("mp", "dp"),
        P(("dp", "mp"), None),
        P(),
        P(),
        P(),
    )
    return jax.shard_map(
        make(mesh.shape["dp"], mesh.shape["mp"]),
        mesh=mesh,
        in_specs=placed,
        out_specs=(
            P(),
            P("dp", None),
            P("dp", None),
            P("dp"),
            P("dp"),
            P(None, "dp", "mp"),
            P("mp", "dp"),
            P("dp"),
            P("dp"),
            P("dp", "mp"),
            P("mp", "dp"),
        ),
        check_vma=False,
    )
```

time: 1000 us -> 630 us (0.63)
  waiting for transfers between devices: 542 us -> 251 us
  blocking collectives: 206 us -> 144 us
  other arithmetic: 69.3 us -> 39.1 us
  local copies, waits for them, and re-layouts: 51.3 us -> 80.2 us
  matrix products: 102 us -> 88.2 us
    psum x4 -> x0, waiting for transfers between devices: 430 us -> none  [the longest x1 123 us: on_device(): lax.psum(jnp.dot(active, gathered[7], preferred_element_type=jnp.float32)...]
    reduce_scatter x2 -> x1, waiting for transfers between devices: 84.4 us -> 221 us  [on_device(): summed = lax.psum_scatter(local, both, scatter_dimension=0, tiled=False)]
    unnamed x3 -> x1, blocking collectives: 101 us -> 43.3 us
    all_gather x2 -> x1, blocking collectives: 66.4 us -> 20.4 us  [on_device(): vectors = lax.all_gather(norms, 'dp', axis=1, tiled=True).astype(f32)]
    psum x1 -> x2, blocking collectives: 38.2 us -> 80.6 us  [the longest x1 41.2 us: on_device(): lax.psum(jnp.stack([gain_one, bias_one, gain_two, bias_two]), both)]
    reduce_sum x15 -> x8, other arithmetic: 35.4 us -> 5.62 us  [the longest x4 3.07 us: standardise(): jnp.mean(centred * centred, axis=-1, keepdims=True) + norm_epsilon]
    all_gather x4, waiting for transfers between devices: 6.28 us -> 30.7 us  [the longest x1 30.6 us: on_device(): lax.all_gather(packed, both, axis=0).reshape(dp_size, mp_size, 3, depth, -1)]
    unnamed x14 -> x5, waiting for transfers between devices: 21.1 us -> 0.08 us
  transfers between devices with their start and end apart: 12 -> 5, of which waited for: 8 -> 2; matrix products, arithmetic and copies ran while one was open for 12% -> 30% of each run, Pallas kernels for 0% -> 0%
where the time goes in v1:
time: 630 us; the launch traced here: 621 us
  waiting for transfers between devices  251 us (40%)
  blocking collectives  144 us (23%)
  matrix products  88.2 us (14%)
  local copies, waits for them, and re-layouts  80.2 us (13%)
  other arithmetic  39.1 us (6%)
  between operations  17.4 us (3%)
    reduce_scatter x1, waiting for transfers between devices, on_device(): summed = lax.psum_scatter(local, both, scatter_dimension=0, tiled=False)  221 us
    unnamed x1, blocking collectives  43.3 us
    psum x1, blocking collectives, on_device(): lax.psum(jnp.stack([gain_one, bias_one, gain_two, bias_two]), both)  41.2 us
    psum x1, blocking collectives, on_device(): sums = lax.psum(jnp.concatenate([col_part, row_part[None]]), both)  39.3 us
    all_gather x1, waiting for transfers between devices, on_device(): lax.all_gather(packed, both, axis=0).reshape(dp_size, mp_size, 3, depth, -1)  30.6 us
    dot_general x2, matrix products, feed(): jnp.einsum('mrf,mdf->rd', active, weights[2], preferred_element_type=f32)  27.2 us
    all_gather x1, blocking collectives, on_device(): vectors = lax.all_gather(norms, 'dp', axis=1, tiled=True).astype(f32)  20.4 us
    unnamed x123, local copies, waits for them, and re-layouts  14.3 us
  transfers between devices with their start and end apart: 5, of which 2 were waited for; matrix products, arithmetic and copies ran while one was open for 30% of the time, Pallas kernels for 0%

profile of v1, /device:TPU:0, one launch (start us, length us, event | category | flops | bytes accessed | tf_op | source)
XLA Modules:
  0.0 620.9 jit_solution(10369757935309103214)
XLA Ops:
  21.0 43.3 %all-reduce.1 = bf16[2048]{0:T(1024)(128)(2,1)S(1)} all-reduce(bf16[2048]{0:T(1024)(128)(2,1)S(1)} %dynamic-update-slice), channel_id=1, replica_groups=mesh['dp'=8,'mp'=4] {'dp','mp'}, use_global_device_ids=true, to_apply=%add.1 | all-reduce | flops 2048 | bytes 8192
  64.8 20.4 %all-gather.1 = bf16[8,96,4]{1,2,0:T(4,128)(2,1)S(1)} all-gather(bf16[1,96,4]{1,2,0:T(4,128)(2,1)S(1)} %maximum_bitcast_fusion.2), channel_id=1, replica_groups=mesh['dp'=8,'mp'=4] {'dp'}, dimensions={0}, use_global_device_ids=true | all-gather | bytes 6912 | tf_op jit(solution)/shard_map/all_gather | solution.py:88
  87.2 30.6 %all-gather.13.cloned.1.call-done = bf16[96,96,768]{2,1,0:T(8,128)(2,1)} async-done(((bf16[3,96,768]{2,1,0:T(8,128)(2,1)}), bf16[96,96,768]{2,1,0:T(8,128)(2,1)}) %all-gather.13.cloned.1.call-update) | async-done | bytes 14155792 | tf_op jit(solution)/shard_map/all_gather | solution.py:86
  117.9 8.2 %fusion.187 = (bf16[1,4,8,96,768]{4,3,0,1,2:T(8,128)(2,1)S(1)}, bf16[1,4,8,96,768]{4,3,0,1,2:T(8,128)(2,1)}, bf16[1,4,8,96,768]{4,3,0,1,2:T(8,128)(2,1)S(1)}) fusion(bf16[3,4,8,96,768]{4,3,0,1,2:T(8,128)(2,1)} %bitcast.253), kind=kLoop, calls=%fused_computation.310 | loop fusion | bytes 28311552 | tf_op jit(solution)/shard_map/slice | solution.py:128
  126.0 2.5 copy.149
  129.0 4.3 fusion.26
  135.4 2.5 fusion.188
  143.3 4.4 fusion.190
  150.3 3.3 convolution_bitcast_fusion.3
  153.7 3.0 copy.150
  157.1 2.8 multiply_reduce_fusion.6
  161.5 24.5 %fusion.43 = bf16[512,768]{1,0:T(8,128)(2,1)} fusion(f32[512,768]{1,0:T(8,128)} %get-tuple-element.112, bf16[4,768,768]{2,1,0:T(8,128)(2,1)} %bitcast.267, bf16[4,768,768]{2,1,0:T(8,128)(2,1)} %bitcast.245, f32[768]{0:T(1024)S(1)} %get-tuple-element.78, f32[768]{0:T(1024)S(1)} %get-tuple-element.77, f32[512]{0:T(512)} %add_rsqrt_fusion, f32[512]{0:T(512)} %copy-done.35), kind=kOutput, calls=%fused_computation.67 | convolution fusion | flops 4936826880 | bytes 11806720 | tf_op jit(solution)/shard_map/mrf,mdf->rd/dot_general | solution.py:130
  186.1 3.9 select_reduce_fusion.2
  193.0 39.3 %psum.14 = f32[2049]{0:T(1024)} all-reduce(f32[2049]{0:T(1024)} %pad_maximum_fusion.5), channel_id=1, replica_groups=mesh['dp'=8,'mp'=4] {'dp','mp'}, use_global_device_ids=true, to_apply=%region_15.16 | all-reduce | flops 2049 | bytes 16392 | tf_op jit(solution)/shard_map/psum | solution.py:148
  233.8 3.1 multiply_reduce_fusion.4
  238.4 4.7 fusion.59
  245.5 2.7 fusion.65
  249.9 5.4 copy.155
  255.3 3.8 gather_fusion.2
  260.9 3.3 fusion.191
  270.1 3.3 fusion.41
  279.1 7.1 %convolution_bitcast_fusion = f32[4,768,576]{1,2,0:T(8,128)} fusion(bf16[4,512,192]{1,2,0:T(8,128)(2,1)} %bitcast.288, bf16[4,512,192]{1,2,0:T(8,128)(2,1)S(1)} %bitcast.274, bf16[4,512,192]{1,2,0:T(8,128)(2,1)} %copy-done.15, f32[768]{0:T(1024)S(1)} %copy-done.40, f32[768]{0:T(1024)S(1)} %copy-done.22, f32[512]{0:T(512)S(1)} %copy-done.30, ...), kind=kOutput, calls=%fused_computation.40 | convolution fusion | flops 1821376512 | bytes 10233860 | tf_op jit(solution)/shard_map/rd,mre->mde/dot_general | solution.py:200
  286.3 8.4 %pad_maximum_fusion = f32[4,768,768]{1,2,0:T(8,128)} fusion(f32[4,768,192]{1,2,0:T(8,128)S(1)} %convolution_bitcast_fusion.1, f32[4,768,576]{1,2,0:T(8,128)} %convolution_bitcast_fusion), kind=kLoop, calls=%fused_computation.9 | loop fusion | flops 2359296 | bytes 18874368 | tf_op jit(solution)/shard_map/concatenate | solution.py:207
  294.7 9.7 %copy.164 = f32[4,768,768]{2,1,0:T(8,128)} copy(f32[4,768,768]{1,2,0:T(8,128)} %pad_maximum_fusion) | data formatting | bytes 18874368 | tf_op jit(solution)/shard_map/concatenate | solution.py:207
  304.5 6.1 fusion.184
  310.5 5.9 fusion.122
  316.4 8.6 %maximum_bitcast_fusion = f32[8,4,3,96,768]{4,3,0,1,2:T(8,128)S(1)} fusion(f32[1,4,8,96,768]{4,3,2,1,0:T(8,128)} %bitcast.254, f32[1,4,8,96,768]{4,3,2,1,0:T(8,128)} %bitcast.252, f32[1,4,8,96,768]{4,3,2,1,0:T(8,128)S(1)} %bitcast.251), kind=kLoop, calls=%fused_computation.7 | loop fusion | flops 14155776 | bytes 56623104 | tf_op jit(solution)/shard_map/transpose | solution.py:208
  325.0 9.6 %copy.165 = f32[8,4,3,96,768]{4,3,2,1,0:T(8,128)} copy(f32[8,4,3,96,768]{4,3,0,1,2:T(8,128)S(1)} %maximum_bitcast_fusion) | data formatting | bytes 56623104 | tf_op jit(solution)/shard_map/transpose | solution.py:208
  337.2 41.2 %psum.15 = f32[4,768]{1,0:T(4,128)S(1)} all-reduce(f32[4,768]{1,0:T(4,128)S(1)} %pad_maximum_fusion.6), channel_id=1, replica_groups=mesh['dp'=8,'mp'=4] {'dp','mp'}, use_global_device_ids=true, to_apply=%region_32.33 | all-reduce | flops 3072 | bytes 24576 | tf_op jit(solution)/shard_map/psum | solution.py:211
  379.1 220.7 %reduce-scatter.2.cloned.1.call-done = f32[1,3,96,768]{3,2,1,0:T(8,128)} async-done(((f32[32,3,96,768]{3,2,1,0:T(8,128)}), f32[1,3,96,768]{3,2,1,0:T(8,128)}) %reduce-scatter.2.cloned.1.call-update) | async-done | bytes 884752 | tf_op jit(solution)/shard_map/reduce_scatter | solution.py:210
  605.4 3.9 copy.194
  610.3 2.7 copy.195
  (228 shorter events, 60.1 us)
Async XLA Ops:
  7.2 6.1 copy-start
  7.2 8.3 %copy-start.44 = (s32[64]{0:T(128)S(1)}, s32[64]{0:T(128)}, u32[]{:S(2)}) copy-start(s32[64]{0:T(128)} %param.17) | copy-start | bytes 772
  7.2 57.6 %copy-start.45 = (bf16[96]{0:T(256)(128)(2,1)S(1)}, bf16[96]{0:T(256)(128)(2,1)}, u32[]{:S(2)}) copy-start(bf16[96]{0:T(256)(128)(2,1)} %param.23) | copy-start | bytes 580
  7.2 57.6 %copy-start.46 = (bf16[96]{0:T(256)(128)(2,1)S(1)}, bf16[96]{0:T(256)(128)(2,1)}, u32[]{:S(2)}) copy-start(bf16[96]{0:T(256)(128)(2,1)} %param.22) | copy-start | bytes 580
  7.2 57.6 %copy-start.47 = (bf16[96]{0:T(256)(128)(2,1)S(1)}, bf16[96]{0:T(256)(128)(2,1)}, u32[]{:S(2)}) copy-start(bf16[96]{0:T(256)(128)(2,1)} %param.19) | copy-start | bytes 580
  7.2 57.6 %copy-start.48 = (bf16[96]{0:T(256)(128)(2,1)S(1)}, bf16[96]{0:T(256)(128)(2,1)}, u32[]{:S(2)}) copy-start(bf16[96]{0:T(256)(128)(2,1)} %param.18) | copy-start | bytes 580
  7.2 110.6 %all-gather.13.cloned.1.call-start = ((), (), s32[]{:S(2)}) async-start(), calls=%async_computation.5 | async-start | bytes 14598144 | tf_op jit(solution)/shard_map/all_gather | solution.py:86
  11.1 175.0 %all-gather.7.cloned.1.call-start = ((), (), s32[]{:S(2)}) async-start(), calls=%async_computation.1 | async-start | bytes 3244032 | tf_op jit(solution)/shard_map/all_gather | solution.py:89
  15.4 363.7 %all-gather.9.cloned.1.call-start = ((), (), s32[]{:S(2)}) async-start(), calls=%async_computation.2 | async-start | bytes 3932160 | tf_op jit(solution)/shard_map/all_gather | solution.py:214
  17.2 108.8 %copy-start.37 = (s32[64]{0:T(128)}, s32[64]{0:T(128)S(1)}, u32[]{:S(2)}) copy-start(s32[64]{0:T(128)S(1)} %reshape.521) | copy-start | bytes 772
  19.2 109.8 %copy-start.19 = (f32[512]{0:T(512)}, f32[512]{0:T(512)S(1)}, u32[]{:S(2)}) copy-start(f32[512]{0:T(512)S(1)} %broadcast_multiply_fusion.3) | copy-start | bytes 6148
  20.7 108.3 %copy-start.28 = (f32[512]{0:T(512)}, f32[512]{0:T(512)S(1)}, u32[]{:S(2)}) copy-start(f32[512]{0:T(512)S(1)} %add_rsqrt_fusion.1) | copy-start | bytes 6148
  85.4 43.6 %copy-start.21 = (f32[768]{0:T(1024)}, f32[768]{0:T(1024)S(1)}, u32[]{:S(2)}) copy-start(f32[768]{0:T(1024)S(1)} %get-tuple-element.80) | copy-start | bytes 9220
  85.4 43.6 %copy-start.39 = (f32[768]{0:T(1024)}, f32[768]{0:T(1024)S(1)}, u32[]{:S(2)}) copy-start(f32[768]{0:T(1024)S(1)} %get-tuple-element.79) | copy-start | bytes 9220
  85.4 40.6 %copy-start.43 = (s32[64]{0:T(128)}, s32[64]{0:T(128)S(1)}, u32[]{:S(2)}) copy-start(s32[64]{0:T(128)S(1)} %get-tuple-element.101) | copy-start | bytes 772
  85.5 62.3 %copy-start.36 = (s32[1024]{0:T(1024)}, s32[1024]{0:T(1024)S(1)}, u32[]{:S(2)}) copy-start(s32[1024]{0:T(1024)S(1)} %pad_clamp_fusion) | copy-start | bytes 12292
  150.1 6.6 %copy-start.25 = (f32[64]{0:T(128)}, f32[64]{0:T(128)S(1)}, u32[]{:S(2)}) copy-start(f32[64]{0:T(128)S(1)} %broadcast_multiply_fusion.7) | copy-start | bytes 772
  150.3 6.4 %copy-start.32 = (f32[64]{0:T(128)}, f32[64]{0:T(128)S(1)}, u32[]{:S(2)}) copy-start(f32[64]{0:T(128)S(1)} %add_rsqrt_fusion.5) | copy-start | bytes 772
  186.0 193.1 %all-gather.11.cloned.1.call-start = ((), (), s32[]{:S(2)}) async-start(), calls=%async_computation.3 | async-start | bytes 7864320 | tf_op jit(solution)/shard_map/all_gather | solution.py:215
  232.4 6.0 copy-start.12
  233.7 9.4 %slice-start = ((s8[4718592]{0:T(1024)(128)(4,1)}), s8[4194304]{0:T(1024)(128)(4,1)S(1)}, s32[]{:S(2)}) async-start(s8[4718592]{0:T(1024)(128)(4,1)} %bitcast.246), calls=%async_computation.6 | async-start | bytes 8388608
  238.3 7.0 %copy-start.16 = (f32[64,768]{1,0:T(8,128)}, f32[64,768]{1,0:T(8,128)S(1)}, u32[]{:S(2)}) copy-start(f32[64,768]{1,0:T(8,128)S(1)} %multiply_subtract_fusion) | copy-start | bytes 589828
  268.4 5.0 copy-start.49
  276.8 323.0 %reduce-scatter.2.cloned.1.call-start = ((), (), s32[]{:S(2)}) async-start(), calls=%async_computation.4 | async-start | bytes 29196288 | tf_op jit(solution)/shard_map/reduce_scatter | solution.py:210
  294.7 9.7 %copy-start.9 = (bf16[4,64,768]{2,1,0:T(8,128)(2,1)S(1)}, bf16[4,64,768]{2,1,0:T(8,128)(2,1)}, u32[]{:S(2)}) copy-start(bf16[4,64,768]{2,1,0:T(8,128)(2,1)} %copy-done.8) | copy-start | bytes 1179652
  294.7 9.7 %copy-start.27 = (f32[64]{0:T(128)S(1)}, f32[64]{0:T(128)}, u32[]{:S(2)}) copy-start(f32[64]{0:T(128)} %copy-done.25) | copy-start | bytes 772
  294.7 9.7 %copy-start.34 = (f32[64]{0:T(128)S(1)}, f32[64]{0:T(128)}, u32[]{:S(2)}) copy-start(f32[64]{0:T(128)} %copy-done.32) | copy-start | bytes 772
  304.4 6.1 copy-start.13
  304.4 6.1 copy-start.17
  304.4 12.0 %slice-start.2 = ((s8[9437184]{0:T(1024)(128)(4,1)}), s8[4194304]{0:T(1024)(128)(4,1)S(1)}, s32[]{:S(2)}) async-start(s8[9437184]{0:T(1024)(128)(4,1)} %bitcast.249), calls=%async_computation.8 | async-start | bytes 8388608
  304.5 12.0 %slice-start.3 = ((s8[9437184]{0:T(1024)(128)(4,1)}), s8[4194304]{0:T(1024)(128)(4,1)S(1)}, s32[]{:S(2)}) async-start(s8[9437184]{0:T(1024)(128)(4,1)} %bitcast.249), calls=%async_computation.9 | async-start | bytes 8388608
  310.5 5.9 slice-start.4
  (31 other events, 76.1 us)
Sparse Core Ops, SparseCore 0:
  11.6 106.2 all-gather.12
  121.3 57.1 all-gather.6
  186.1 27.7 all-gather.8
  276.9 47.4 all-gather.10
  334.8 264.9 reduce-scatter.1

commit v2 on v1

--- a/solution.py
+++ b/solution.py
@@ -2,6 +2,9 @@
 import jax.numpy as jnp
 from jax import lax
 from jax.sharding import PartitionSpec as P
+import functools
+from jax.experimental import pallas as pl
+from jax.experimental.pallas import tpu as pltpu
 
 HEAD_DIM = 64
 SEQ_LEN = 16
@@ -43,6 +46,811 @@
 
 def phi(values):
     return 0.5 * lax.erfc(-values * (0.5**0.5))
+
+
+MESH = pl.DeviceIdType.MESH
+VMEM, DMA = pltpu.VMEM, pltpu.SemaphoreType.DMA
+CUT = 48
+LATE = 48
+
+
+def loop(count, body):
+    lax.fori_loop(0, count, lambda i, carry: (body(i), carry)[1], 0)
+
+
+def rows_of(index, size):
+    return pl.ds(pl.multiple_of(index * size, size), size)
+
+
+def split_three(values):
+    first = values.astype(bf16)
+    rest = values - first.astype(f32)
+    second = rest.astype(bf16)
+    return first, second, (rest - second.astype(f32)).astype(bf16)
+
+
+def pick(place, values):
+    return sum(nn(place, part) for part in split_three(values))
+
+
+def spread_rows(place, values):
+    return sum(tn(place, part) for part in split_three(values))
+
+
+def half_erf(values):
+    return 0.5 + 0.5 * lax.erf(values * (0.5**0.5))
+
+
+def layer_kernel(slot_total, *refs):
+    (packed, small, classes, image_gain, image_bias, image_proj, tokens, ids) = refs[:8]
+    (loss_out, block_out, token_out, attn_out, up_out, down_out, vec_out) = refs[8:15]
+    (w_attn, w_up, w_down, images, smalls, x_ref, a_ref, qkv, hidden, a_two, active, stage_out, image_own, vecs) = refs[15:29]
+    (mask_ref, place_ref, member_ref, h_ends, ends_two, ends_grad, u_ends, g_all, s_all, weight_ref, valid_ref) = refs[29:40]
+    (sum_own, sum_buf, sum_got, d_attn, d_qkv) = refs[40:45]
+    (grad_down, grad_up, ffn_one, ffn_three, attn_send, attn_acc, attn_core, one_p, one_q, two_p, two_q, three_a) = refs[45:57]
+    (vec_buf, vec_got, stage_grad, grad_got) = refs[57:61]
+    gsems = refs[61:96]
+    (s_local, s_bo, s_boc, s_send, s_a2, s_dm, s_sum, s_sums, s_f1, s_f3, s_core, s_1p, s_1q, s_2p, s_2q, s_3, s_v, s_vs, s_tg, s_exs) = refs[96:116]
+
+    dp = lax.axis_index("dp")
+    mp = lax.axis_index("mp")
+    z = lax.div(dp, 2)
+    x = lax.rem(dp, 2)
+    y = lax.div(mp, 2)
+    c = lax.rem(mp, 2)
+    xd, ym, cm = 2 * z + (1 - x), 2 * (1 - y) + c, 2 * y + (1 - c)
+    zt = [lax.rem(z + j, 4) for j in range(4)]
+    zs = [lax.rem(z + 4 - j, 4) for j in range(4)]
+    X, Y, C, YC = (xd, mp), (dp, ym), (dp, cm), (dp, 3 - mp)
+    Z = [(2 * zt[j] + x, mp) for j in range(4)]
+    xy = 2 * y + x
+    Q = []
+    for j in range(1, 4):
+        other = lax.rem(xy + j, 4)
+        Q.append((2 * z + lax.rem(other, 2), 2 * lax.div(other, 2) + c))
+    G = [(dp, lax.rem(mp + j, 4)) for j in range(4)]
+
+    far_xy = (2 * z + (1 - x), 2 * (1 - y) + c)
+    peers = [X, Y, C, YC, far_xy] + Z[1:]
+    barrier = pltpu.get_barrier_semaphore()
+    for peer in peers:
+        pl.semaphore_signal(barrier, inc=1, device_id=peer, device_id_type=MESH)
+    pl.semaphore_wait(barrier, len(peers))
+
+    def remote(src, dst, send_sem, recv_sem, device):
+        copy = pltpu.make_async_remote_copy(
+            src_ref=src, dst_ref=dst, send_sem=send_sem, recv_sem=recv_sem, device_id=device, device_id_type=MESH
+        )
+        copy.start()
+        return copy
+
+    def arrived(ref, recv_sem, send_sem):
+        pltpu.make_async_remote_copy(
+            src_ref=ref, dst_ref=ref, send_sem=send_sem, recv_sem=recv_sem, device_id=X, device_id_type=MESH
+        ).wait_recv()
+
+    def gather_steps(src, out, rows, cut, sems):
+        zr, x0, y1, y0, x1, cr, sd = sems
+        first = (0, cut) if cut else (0, rows)
+        second = (cut, rows - cut) if cut else None
+        full = (0, rows)
+
+        def piece(d, m, span):
+            return out.at[m, pl.ds(pl.multiple_of(d * rows + span[0], 16), span[1])]
+
+        def send(src_ref, dst_ref, sem, device):
+            remote(src_ref, dst_ref, sd.at[0], sem, device)
+
+        def got(ref, sem):
+            arrived(ref, sem, sd.at[0])
+
+        def step0():
+            for j in range(1, 4):
+                send(src, piece(dp, mp, full), zr.at[j], Z[j])
+            send(src.at[pl.ds(*first)], piece(dp, mp, first), x0.at[0], X)
+            if second:
+                send(src.at[pl.ds(*second)], piece(dp, mp, second), y1.at[0], Y)
+            send(src.at[pl.ds(*first)], piece(dp, mp, first), y0.at[0], Y)
+            if second:
+                send(src.at[pl.ds(*second)], piece(dp, mp, second), x1.at[0], X)
+            send(src, piece(dp, mp, full), cr.at[0], C)
+            pltpu.make_async_copy(src, piece(dp, mp, full), sd.at[0]).start()
+            yield
+
+        def step1():
+            for j in range(1, 4):
+                d = 2 * zs[j] + x
+                block = piece(d, mp, full)
+                got(block, zr.at[j])
+                one = piece(d, mp, first)
+                send(one, one, x0.at[j], X)
+                if second:
+                    two = piece(d, mp, second)
+                    send(two, two, y1.at[j], Y)
+                send(one, one, y0.at[j], Y)
+                if second:
+                    send(two, two, x1.at[j], X)
+                send(block, block, cr.at[0], C)
+                yield
+
+        def step2():
+            for j in range(4):
+                one = piece(2 * zs[j] + (1 - x), mp, first)
+                got(one, x0.at[j])
+                send(one, one, y0.at[4 + j], Y)
+                send(one, one, cr.at[0], C)
+                if second:
+                    two = piece(2 * zs[j] + x, ym, second)
+                    got(two, y1.at[j])
+                    send(two, two, x1.at[4 + j], X)
+                    send(two, two, cr.at[0], C)
+                yield
+
+        def step3():
+            for i in range(2):
+                for j in range(4):
+                    one = piece(2 * zs[j] + (x if i == 0 else 1 - x), ym, first)
+                    got(one, y0.at[4 * i + j])
+                    send(one, one, cr.at[0], C)
+                    if second:
+                        two = piece(2 * zs[j] + (1 - x), (mp if i == 0 else ym), second)
+                        got(two, x1.at[4 * i + j])
+                        send(two, two, cr.at[0], C)
+                    yield
+
+        def step4():
+            half = out.at[pl.ds(0, 2)]
+            pltpu.make_async_copy(half, half, cr.at[0]).wait()
+            pltpu.make_async_copy(out, out, sd.at[0]).wait()
+            yield
+
+        return [step0, step1, step2, step3, step4]
+
+    depth = packed.shape[1]
+    slots = classes.shape[0]
+    kinds = {
+        "S": gather_steps(small, smalls, 16, 0, gsems[0:7]),
+        "A": gather_steps(packed.at[0], w_attn, depth, CUT, gsems[7:14]),
+        "U": gather_steps(packed.at[1], w_up, depth, CUT, gsems[14:21]),
+        "D": gather_steps(packed.at[2], w_down, depth, CUT, gsems[21:28]),
+        "I": gather_steps(image_own, images, slots, slots // 2, gsems[28:35]),
+    }
+
+    def run(*steps):
+        for name in steps:
+            for _ in kinds[name[0]][int(name[1])]():
+                pass
+
+    def blend(steps, chunks):
+        chunks = list(chunks)
+        micro = [kinds[name[0]][int(name[1])] for name in steps]
+        count = sum((1, 3, 4, 8, 1)[int(name[1])] for name in steps)
+        done, at = 0, 0
+        for step in micro:
+            for _ in step():
+                at += 1
+                while done < len(chunks) and done * count < at * len(chunks):
+                    chunks[done]()
+                    done += 1
+        for chunk in chunks[done:]:
+            chunk()
+
+    lane = lax.broadcasted_iota(jnp.int32, (128, 128), 1)
+    sub = lax.broadcasted_iota(jnp.int32, (128, 128), 0)
+    low = lax.broadcasted_iota(jnp.int32, (1, 128), 1) < 64
+    token_rows = x_ref.shape[0]
+    tiles = token_rows // 128
+    end_count = h_ends.shape[0]
+
+    def keep_low(values):
+        return jnp.where(low, values, jnp.zeros_like(values))
+
+    def keep_high(values):
+        return jnp.where(low, jnp.zeros_like(values), values)
+
+    def masks():
+        slot_row = lax.broadcasted_iota(jnp.int32, (end_count, 128), 0)
+        parts, spots = [], []
+        best = jnp.full((end_count, 1), -1, jnp.int32)
+        for b in range(tiles):
+            caption = 2 * (8 * b + lax.shift_right_logical(lax.broadcasted_iota(jnp.int32, (1, 128), 1), 4)) + ids[mp, pl.ds(b, 1), :]
+            column = jnp.sum(jnp.where(lane == sub, caption, 0), axis=1, keepdims=True)
+            mask_ref[b] = jnp.where((column == caption) & (sub >= lane), 0.0, -1e30)
+            member = slot_row == caption
+            spot = lax.broadcasted_iota(jnp.int32, (end_count, 128), 1) + 128 * b
+            best = jnp.maximum(best, jnp.max(jnp.where(member, spot, -1), axis=1, keepdims=True))
+            member_ref[:, 128 * b : 128 * (b + 1)] = jnp.where(member, 0.0, -1e30)
+            spots.append(spot)
+        for b in range(tiles):
+            place_ref[:, 128 * b : 128 * (b + 1)] = (spots[b] == best).astype(f32).astype(bf16)
+
+    def image_tower():
+        hat, _ = standardise(classes[...].astype(f32))
+        raw = nn((hat * image_gain[...] + image_bias[...]).astype(bf16), image_proj[...])
+        image_own[...] = (raw * inverse_norm(raw)).astype(bf16)
+
+    def small_vectors():
+        halves = []
+        for w in range(2):
+            halves.append(sum(smalls[0, 64 * w + 16 * d : 64 * w + 16 * (d + 1), :].astype(f32) for d in range(4)))
+        for v in range(4):
+            for w in range(2):
+                for t in range(3):
+                    at = 384 * w + 128 * t
+                    vecs[v : v + 1, at : at + 128] = halves[w][3 * v + t : 3 * v + t + 1, :]
+        for m in range(4):
+            for pair in range(4):
+                both = sum(smalls[m, 32 * pair + 16 * d : 32 * pair + 16 * (d + 1), :].astype(f32) for d in range(2))
+                valid_ref[m : m + 1, 128 * pair : 128 * (pair + 1)] = both[12:13, :]
+
+    def first_norm():
+        def body(b):
+            rows = rows_of(b, 128)
+            values = x_ref[rows, :].astype(f32)
+            hat, _ = standardise(values)
+            a_ref[rows, :] = (hat * vecs[0:1, :] + vecs[1:2, :]).astype(bf16)
+            hidden[rows, :] = values
+
+        loop(tiles, body)
+
+    def soft(scores):
+        top = jnp.max(scores, axis=-1, keepdims=True)
+        raised = jnp.exp(scores - top)
+        return raised * (1.0 / jnp.sum(raised, axis=-1, keepdims=True))
+
+    scale = HEAD_DIM**-0.5
+
+    def attention(m):
+        def body(b):
+            rows = rows_of(b, 128)
+            made = nn(a_ref[rows, :], w_attn[m]).astype(bf16)
+            q01, k01, v01, qv, ko = (made[:, 128 * i : 128 * (i + 1)] for i in range(5))
+            mask = mask_ref[b]
+            p0 = soft(nt(keep_low(q01), k01) * scale + mask).astype(bf16)
+            p1 = soft(nt(keep_high(q01), k01) * scale + mask).astype(bf16)
+            p2 = soft(nt(keep_low(qv), ko) * scale + mask).astype(bf16)
+            o01 = jnp.where(low, nn(p0, v01), nn(p1, v01)).astype(bf16)
+            o2 = keep_high(nn(p2, qv)).astype(bf16)
+            qkv[m, rows, 0:512] = made[:, 0:512]
+            qkv[m, rows, 512:640] = keep_low(ko) + o2
+            qkv[m, rows, 640:768] = o01
+            hidden[rows, :] += nt(o2, w_attn[m, :, 512:640]) + nt(o01, w_attn[m, :, 640:768])
+
+        loop(tiles, body)
+
+    def second_norm():
+        def body(b):
+            rows = rows_of(b, 128)
+            hat, _ = standardise(hidden[rows, :])
+            a_two[rows, :] = (hat * vecs[2:3, :] + vecs[3:4, :]).astype(bf16)
+
+        loop(tiles, body)
+        place = place_ref[...]
+        ends = pick(place, hidden[...])
+        h_ends[...] = ends
+        hat, _ = standardise(ends)
+        ends_two[mp] = (hat * vecs[2:3, :] + vecs[3:4, :]).astype(bf16)
+
+    def ends_up(m):
+        u_ends[m] = nn(ends_two[mp], w_up[m])
+
+    def full_up(m):
+        def body(b):
+            rows = rows_of(b, 128)
+            upper = nn(a_two[rows, :], w_up[m])
+            active[m, rows, :] = (upper * half_erf(upper)).astype(bf16)
+
+        loop(tiles, body)
+
+    def slope_of(upper):
+        return half_erf(upper) + upper * jnp.exp(-0.5 * upper * upper) * (1.0 / (2.0 * jnp.pi) ** 0.5)
+
+    def group_up():
+        def body(i):
+            upper = nn(ends_two[i], w_up[mp])
+            rows = rows_of(i, end_count)
+            g_all[rows, :] = (upper * half_erf(upper)).astype(bf16)
+            s_all[rows, :] = slope_of(upper)
+
+        loop(4, body)
+
+    def full_down(b):
+        rows = slice(128 * b, 128 * (b + 1))
+        hidden_down = hidden[rows, :]
+
+        def body(m, total):
+            return total + nt(active[m, rows, :], w_down[m])
+
+        stage_out[rows, :] = lax.fori_loop(0, 4, body, hidden_down).astype(bf16)
+
+    own_tokens = pltpu.make_async_copy(tokens.at[rows_of(mp, token_rows)], x_ref, s_local.at[0])
+    own_tokens.start()
+    run("S0", "A0", "U0")
+    image_tower()
+    masks()
+    run("S1", "A1", "D0", "I0", "S2", "A2", "U1", "S3", "S4")
+    own_tokens.wait()
+    small_vectors()
+    first_norm()
+    run("D1", "A3", "A4")
+    blend(("U2", "I1", "D2", "U3", "I2"), [functools.partial(attention, m) for m in range(4)])
+    second_norm()
+    swaps = [remote(ends_two.at[mp], ends_two.at[mp], s_exs.at[j - 1], s_a2.at[j - 1], G[j]) for j in range(1, 4)]
+    run("U4")
+    blend(("D3", "I3"), [functools.partial(full_up, m) for m in range(4)])
+    loop(4, ends_up)
+    for swap in swaps:
+        swap.wait()
+    group_up()
+    run("D4", "I4")
+
+    pooled = h_ends[...]
+    for m in range(4):
+        upper = u_ends[m]
+        pooled = pooled + nt((upper * half_erf(upper)).astype(bf16), w_down[m])
+    scale_back = inverse_norm(pooled)
+    text = (pooled * scale_back).astype(bf16)
+    own_valid = small[12:13, :].astype(f32)
+    own_valid = jnp.max(
+        jnp.where(
+            lax.rem(lax.broadcasted_iota(jnp.int32, (slots, 128), 1), slots)
+            == lax.broadcasted_iota(jnp.int32, (slots, 128), 0),
+            own_valid,
+            0.0,
+        ),
+        axis=1,
+        keepdims=True,
+    )
+    live = own_valid > 0.0
+    place_col = lax.broadcasted_iota(jnp.int32, (slots, 512), 1)
+    place_row = lax.broadcasted_iota(jnp.int32, (slots, 512), 0)
+
+    def target_of(m):
+        return (place_col == place_row + dp * slots) & (mp == m)
+
+    row_sum = jnp.zeros((slots, 1), f32)
+    matched = jnp.zeros((slots, 1), f32)
+    for m in range(4):
+        logits = logit_scale * nt(text, images[m])
+        weight = jnp.exp(logits)
+        matched = matched + jnp.sum(jnp.where(target_of(m), logits, 0.0), axis=1, keepdims=True)
+        seen = jnp.where(valid_ref[m : m + 1, :] > 0.0, weight, 0.0)
+        weight_ref[m] = seen
+        row_sum = row_sum + jnp.sum(seen, axis=1, keepdims=True)
+        columns = jnp.sum(jnp.where(live, weight, 0.0), axis=0, keepdims=True)
+        for part in range(4):
+            sum_own[4 * m + part : 4 * m + part + 1, :] = columns[:, 128 * part : 128 * (part + 1)]
+    row_part = jnp.sum(jnp.where(live, jnp.log(row_sum) - 2.0 * matched, 0.0), axis=0, keepdims=True)
+    sum_own[16:24, :] = jnp.broadcast_to(row_part, (8, 128))
+
+    swap = remote(sum_own, sum_got.at[0], s_sums.at[0], s_sum.at[0], C)
+    full_down(0)
+    swap.wait()
+    sum_buf[0] = sum_own[...] + sum_got[0]
+    swaps = [remote(sum_buf.at[0], sum_got.at[1 + xy], s_sums.at[j], s_sum.at[j], Q[j - 1]) for j in range(1, 4)]
+    sum_got[1 + xy] = sum_buf[0]
+    full_down(1)
+    for swap in swaps:
+        swap.wait()
+    sum_buf[1] = (sum_got[1] + sum_got[2]) + (sum_got[3] + sum_got[4])
+    swaps = [remote(sum_buf.at[1], sum_got.at[5 + z], s_sums.at[3 + j], s_sum.at[3 + j], Z[j]) for j in range(1, 4)]
+    sum_got[5 + z] = sum_buf[1]
+    full_down(2)
+    for swap in swaps:
+        swap.wait()
+    sums = (sum_got[5] + sum_got[6]) + (sum_got[7] + sum_got[8])
+
+    total = sums[16:17, 0:1]
+    unit_grad = jnp.zeros((slots, text.shape[1]), f32)
+    for m in range(4):
+        columns = jnp.concatenate([sums[4 * m + part : 4 * m + part + 1, :] for part in range(4)], axis=1)
+        seen = valid_ref[m : m + 1, :] > 0.0
+        total = total + jnp.sum(jnp.where(seen, jnp.log(columns), 0.0), axis=1, keepdims=True)
+        spread = 0.5 * weight_ref[m] * (1.0 / row_sum + 1.0 / columns)
+        grad = jnp.where(seen & live, spread, 0.0) - jnp.where(target_of(m) & live, 1.0, 0.0)
+        unit_grad = unit_grad + nn((logit_scale * grad).astype(bf16), images[m])
+    loss_out[...] = jnp.broadcast_to(total * (0.5 / slot_total), (8, 128))
+    along = jnp.sum(unit_grad * pooled, axis=-1, keepdims=True)
+    pooled_grad = scale_back * unit_grad - pooled * (scale_back * scale_back * scale_back * along)
+    branch_grad = pooled_grad.astype(bf16)
+    ends_grad[mp] = branch_grad
+    swaps = [remote(ends_grad.at[mp], ends_grad.at[mp], s_exs.at[2 + j], s_dm.at[j - 1], G[j]) for j in range(1, 4)]
+
+    full_down(3)
+    own_rows = rows_of(mp, token_rows)
+    far_rows = rows_of(ym, token_rows)
+    out_swaps = [
+        remote(stage_out, block_out.at[own_rows], s_bo.at[0], s_bo.at[1], Y),
+        remote(stage_out, block_out.at[own_rows], s_bo.at[2], s_bo.at[3], C),
+    ]
+    keep_out = pltpu.make_async_copy(stage_out, block_out.at[own_rows], s_local.at[1])
+    keep_out.start()
+
+    two_grad = jnp.zeros_like(pooled)
+    for m in range(4):
+        upper_grad = (nn(branch_grad, w_down[m]) * slope_of(u_ends[m])).astype(bf16)
+        two_grad = two_grad + nt(upper_grad, w_up[m])
+    hat_two, rstd_two = standardise(h_ends[...])
+    vec_buf[0] = jnp.zeros_like(vec_buf[0])
+    vec_buf[0, 2:3, :] = jnp.sum(two_grad * hat_two, axis=0, keepdims=True)
+    vec_buf[0, 3:4, :] = jnp.sum(two_grad, axis=0, keepdims=True)
+    hidden_grad = pooled_grad + norm_pull(two_grad, hat_two, rstd_two, vecs[2:3, :])
+    attended_grad = hidden_grad.astype(bf16)
+    h_ends[...] = hidden_grad
+
+    for swap in swaps:
+        swap.wait()
+    group_grad = ends_grad[...].reshape(4 * end_count, -1)
+    upper_grad = (nn(group_grad, w_down[mp]) * s_all[...]).astype(bf16)
+    s_all_grad = upper_grad
+    grad_down[...] = tn(group_grad, g_all[...]).astype(bf16)
+
+    def block(z_, x_):
+        return pl.ds(pl.multiple_of((2 * z_ + x_) * depth, 16), depth)
+
+    ffn = [grad_down, grad_up]
+
+    def ffn_start(k):
+        for j in (2, 1, 3, 0):
+            remote(ffn[k].at[block(zt[j], 1 - x)], ffn_one.at[k, j], s_send.at[k], s_f1.at[k, j], X)
+
+    def ffn_add(k, out):
+        for j in (2, 1, 3, 0):
+            arrived(ffn_one.at[k, j], s_f1.at[k, j], s_send.at[k])
+            mine = block(zt[j], x)
+            summed = ffn[k][mine, :].astype(f32) + ffn_one[k, j].astype(f32)
+            if j:
+                ffn[k][mine, :] = summed.astype(bf16)
+                remote(ffn[k].at[mine], ffn_three.at[k, j - 1], s_send.at[k], s_f3.at[k, j - 1], Z[j])
+            else:
+                out[...] = summed
+
+    def ffn_end(k, out):
+        for j in range(1, 4):
+            arrived(ffn_three.at[k, j - 1], s_f3.at[k, j - 1], s_send.at[k])
+        out[...] = out[...] + ffn_three[k, 0].astype(f32) + ffn_three[k, 1].astype(f32) + ffn_three[k, 2].astype(f32)
+        sent = ffn[k].at[pl.ds(0, 7 * depth)]
+        pltpu.make_async_copy(sent, sent, s_send.at[k]).wait()
+
+    ffn_start(0)
+    grad_up[...] = tn(ends_two[...].reshape(4 * end_count, -1), s_all_grad).astype(bf16)
+    ffn_start(1)
+
+    d_attn[...] = jnp.zeros_like(d_attn)
+
+    def attention_back(m):
+        place = place_ref[...]
+        member = member_ref[...]
+        k01, v01, qv, ko = (qkv[m, :, 128 * i : 128 * (i + 1)] for i in range(1, 5))
+        q_e = nn(place, qkv[m, :, 0:128]).astype(bf16)
+        q2_e = keep_low(nn(place, qv)).astype(bf16)
+        do01 = nn(attended_grad, w_attn[m, :, 640:768]).astype(bf16)
+        do2 = keep_high(nn(attended_grad, w_attn[m, :, 512:640])).astype(bf16)
+
+        def head(query, keys, values, outer):
+            probs = soft(nt(query, keys) * scale + member)
+            probs_grad = nt(outer, values)
+            centre = jnp.sum(probs_grad * probs, axis=-1, keepdims=True)
+            return probs.astype(bf16), (probs * (probs_grad - centre)).astype(bf16)
+
+        p0, ds0 = head(keep_low(q_e), k01, v01, keep_low(do01))
+        p1, ds1 = head(keep_high(q_e), k01, v01, keep_high(do01))
+        p2, ds2 = head(q2_e, ko, qv, do2)
+        dq01 = (jnp.where(low, nn(ds0, k01), nn(ds1, k01)) * scale).astype(bf16)
+        dq2 = keep_low(nn(ds2, ko) * scale).astype(bf16)
+        d_qkv[m, :, 0:128] = tn(place, dq01).astype(bf16)
+        d_qkv[m, :, 128:256] = (jnp.where(low, tn(ds0, q_e), tn(ds1, q_e)) * scale).astype(bf16)
+        d_qkv[m, :, 256:384] = jnp.where(low, tn(p0, do01), tn(p1, do01)).astype(bf16)
+        d_qkv[m, :, 384:512] = jnp.where(low, tn(place, dq2), tn(p2, do2)).astype(bf16)
+        d_qkv[m, :, 512:640] = keep_low(tn(ds2, q2_e) * scale).astype(bf16)
+
+    def token_back(m):
+        def body(b):
+            rows = rows_of(b, 128)
+            d_attn[rows, :] += nt(d_qkv[m, rows, 0:640], w_attn[m, :, 0:640])
+
+        loop(tiles, body)
+
+    for m in range(4):
+        attention_back(m)
+        token_back(m)
+        if m == 1:
+            ffn_add(0, down_out)
+    ffn_add(1, up_out)
+
+    vec_buf[0, 0:2, :] = jnp.zeros((2, vec_buf.shape[2]), f32)
+
+    def token_end(b):
+        rows = rows_of(b, 128)
+        hat, rstd = standardise(x_ref[rows, :].astype(f32))
+        grad = d_attn[rows, :]
+        vec_buf[0, 0:1, :] += jnp.sum(grad * hat, axis=0, keepdims=True)
+        vec_buf[0, 1:2, :] += jnp.sum(grad, axis=0, keepdims=True)
+        d_attn[rows, :] = norm_pull(grad, hat, rstd, vecs[0:1, :])
+
+    loop(tiles, token_end)
+    stage_grad[...] = (d_attn[...] + spread_rows(place_ref[...], h_ends[...])).astype(bf16)
+    grad_swaps = [
+        remote(stage_grad, token_out.at[own_rows], s_tg.at[0], s_tg.at[1], Y),
+        remote(stage_grad, token_out.at[own_rows], s_tg.at[2], s_tg.at[3], C),
+    ]
+    keep_grad = pltpu.make_async_copy(stage_grad, token_out.at[own_rows], s_local.at[2])
+    keep_grad.start()
+
+    def attn_grad(m):
+        made = tn(a_ref[...], d_qkv[m, :, 0:640])
+        o_e = nn(place_ref[...], qkv[m, :, 512:768]).astype(bf16)
+        outer = tn(attended_grad, o_e)
+        last = jnp.where(low, made[:, 512:640], outer[:, 0:128])
+        return jnp.concatenate([made[:, 0:512], last, outer[:, 128:256]], axis=1)
+
+    def pair_y(d):
+        return y if d == 0 else 1 - y
+
+    def pair_x(d):
+        return x if d == 0 else 1 - x
+
+    first, second = pl.ds(0, LATE), pl.ds(LATE, depth - LATE)
+
+    def half_rows(d):
+        return d * 8 * depth
+
+    def part(d, z_, x_, span):
+        start = half_rows(d) + (2 * z_ + x_) * depth + span.start
+        return attn_acc.at[pl.ds(pl.multiple_of(start, 16), span.size)]
+
+    whole = pl.ds(0, depth)
+    core_swaps = []
+    for d in (1, 0):
+        attn_send[d] = attn_grad(2 * pair_y(d) + (1 - c)).astype(bf16)
+        core_swaps.append(remote(attn_send.at[d], attn_core.at[d], s_exs.at[6 + d], s_core.at[d], C))
+    vec_swaps = [remote(vec_buf.at[0], vec_got.at[0], s_vs.at[0], s_v.at[0], C)]
+    for i, d in enumerate((1, 0)):
+        made = attn_grad(2 * pair_y(d) + c)
+        core_swaps[i].wait()
+        attn_acc[half_rows(d) : half_rows(d + 1), :] = (made + attn_core[d].astype(f32)).astype(bf16)
+        for j in range(4):
+            remote(part(d, zt[j], 1 - x, second), one_q.at[4 * d + j], s_send.at[2], s_1q.at[4 * d + j], X)
+        if d:
+            for e in (1, 0):
+                for j in range(4):
+                    remote(part(1, zt[j], pair_x(e), first), one_p.at[4 * e + j], s_send.at[2], s_1p.at[4 * e + j], Y)
+            ffn_end(0, down_out)
+            vec_swaps[0].wait()
+            vec_buf[1] = vec_buf[0] + vec_got[0]
+            vec_swaps.append(remote(vec_buf.at[1], vec_got.at[1], s_vs.at[1], s_v.at[1], Y))
+
+    def add(ref, got):
+        ref[...] = (ref[...].astype(f32) + got.astype(f32)).astype(bf16)
+
+    ffn_end(1, up_out)
+    vec_swaps[1].wait()
+    vec_buf[2] = vec_buf[1] + vec_got[1]
+    vec_swaps.append(remote(vec_buf.at[2], vec_got.at[2], s_vs.at[2], s_v.at[2], X))
+    for e in (1, 0):
+        for j in range(4):
+            i = 4 * e + j
+            arrived(one_p.at[i], s_1p.at[i], s_send.at[2])
+            spot = part(0, zt[j], pair_x(e), first)
+            add(spot, one_p[i])
+            if e:
+                remote(spot, two_p.at[j], s_send.at[2], s_2p.at[j], X)
+            arrived(one_q.at[i], s_1q.at[i], s_send.at[2])
+            spot = part(e, zt[j], x, second)
+            add(spot, one_q[i])
+            if e:
+                remote(spot, two_q.at[j], s_send.at[2], s_2q.at[j], Y)
+    vec_swaps[2].wait()
+    vec_buf[3] = vec_buf[2] + vec_got[2]
+    for j in range(1, 4):
+        vec_swaps.append(remote(vec_buf.at[3], vec_got.at[3 + z], s_vs.at[2 + j], s_v.at[2 + j], Z[j]))
+    vec_got[3 + z] = vec_buf[3]
+    for j in (2, 1, 3, 0):
+        arrived(two_p.at[j], s_2p.at[j], s_send.at[2])
+        add(part(0, zt[j], x, first), two_p[j])
+        arrived(two_q.at[j], s_2q.at[j], s_send.at[2])
+        add(part(0, zt[j], x, second), two_q[j])
+        spot = part(0, zt[j], x, whole)
+        if j:
+            remote(spot, three_a.at[j - 1], s_send.at[2], s_3.at[j - 1], Z[j])
+        else:
+            attn_out[...] = spot[...].astype(f32)
+    out_swaps[0].wait()
+    on = remote(block_out.at[far_rows], block_out.at[far_rows], s_boc.at[0], s_boc.at[1], C)
+    grad_swaps[0].wait()
+    on_grad = remote(token_out.at[far_rows], token_out.at[far_rows], s_boc.at[2], s_boc.at[3], C)
+    for j in range(1, 4):
+        arrived(three_a.at[j - 1], s_3.at[j - 1], s_send.at[2])
+    attn_out[...] = attn_out[...] + three_a[0].astype(f32) + three_a[1].astype(f32) + three_a[2].astype(f32)
+    for swap in vec_swaps[3:]:
+        swap.wait()
+    vec_out[...] = (vec_got[3] + vec_got[4]) + (vec_got[5] + vec_got[6])
+    sent = attn_acc.at[pl.ds(0, 15 * depth)]
+    pltpu.make_async_copy(sent, sent, s_send.at[2]).wait()
+    out_swaps[1].wait()
+    grad_swaps[1].wait()
+    on.wait()
+    on_grad.wait()
+    keep_out.wait()
+    keep_grad.wait()
+
+
+def layer(slot_total, packed, small, classes, image_gain, image_bias, image_proj, tokens, ids):
+    width, depth, slots = packed.shape[2], packed.shape[1], classes.shape[0]
+    rows = tokens.shape[0] // 4
+
+    def gather_sems():
+        return [DMA((4,)), DMA((4,)), DMA((4,)), DMA((8,)), DMA((8,)), DMA((1,)), DMA((1,))]
+
+    here, there = pl.BlockSpec(memory_space=VMEM), pl.BlockSpec(memory_space=pltpu.HBM)
+    square = VMEM((4, width, width), bf16)
+    scratch = [
+        square,
+        square,
+        square,
+        VMEM((4, 8 * slots, width), bf16),
+        VMEM((4, 128, 128), bf16),
+        VMEM((rows, width), bf16),
+        VMEM((rows, width), bf16),
+        VMEM((4, rows, width), bf16),
+        VMEM((rows, width), f32),
+        VMEM((rows, width), bf16),
+        VMEM((4, rows, width), bf16),
+        VMEM((rows, width), bf16),
+        VMEM((slots, width), bf16),
+        VMEM((8, width), f32),
+        VMEM((rows // 128, 128, 128), f32),
+        VMEM((slots, rows), bf16),
+        VMEM((slots, rows), f32),
+        VMEM((slots, width), f32),
+        VMEM((4, slots, width), bf16),
+        VMEM((4, slots, width), bf16),
+        VMEM((4, slots, width), f32),
+        VMEM((4 * slots, width), bf16),
+        VMEM((4 * slots, width), f32),
+        VMEM((4, slots, 8 * slots), f32),
+        VMEM((8, 8 * slots), f32),
+        VMEM((24, 128), f32),
+        VMEM((2, 24, 128), f32),
+        VMEM((9, 24, 128), f32),
+        VMEM((rows, width), f32),
+        VMEM((4, rows, 640), bf16),
+        VMEM((width, width), bf16),
+        VMEM((width, width), bf16),
+        VMEM((2, 4, depth, width), bf16),
+        VMEM((2, 3, depth, width), bf16),
+        VMEM((2, width, width), bf16),
+        VMEM((2 * width, width), bf16),
+        VMEM((2, width, width), bf16),
+        VMEM((8, LATE, width), bf16),
+        VMEM((8, depth - LATE, width), bf16),
+        VMEM((4, LATE, width), bf16),
+        VMEM((4, depth - LATE, width), bf16),
+        VMEM((3, depth, width), bf16),
+        VMEM((4, 8, width), f32),
+        VMEM((7, 8, width), f32),
+        VMEM((rows, width), bf16),
+        VMEM((8, 128), f32),
+    ]
+    for _ in range(5):
+        scratch += gather_sems()
+    scratch += [
+        DMA((3,)),
+        DMA((4,)),
+        DMA((4,)),
+        DMA((3,)),
+        DMA((3,)),
+        DMA((3,)),
+        DMA((7,)),
+        DMA((7,)),
+        DMA((2, 4)),
+        DMA((2, 3)),
+        DMA((2,)),
+        DMA((8,)),
+        DMA((8,)),
+        DMA((4,)),
+        DMA((4,)),
+        DMA((3,)),
+        DMA((6,)),
+        DMA((6,)),
+        DMA((4,)),
+        DMA((8,)),
+    ]
+    return pl.pallas_call(
+        functools.partial(layer_kernel, slot_total),
+        out_shape=[
+            jax.ShapeDtypeStruct((8, 128), f32),
+            jax.ShapeDtypeStruct((4 * rows, width), bf16),
+            jax.ShapeDtypeStruct((4 * rows, width), bf16),
+            jax.ShapeDtypeStruct((depth, width), f32),
+            jax.ShapeDtypeStruct((depth, width), f32),
+            jax.ShapeDtypeStruct((depth, width), f32),
+            jax.ShapeDtypeStruct((8, width), f32),
+        ],
+        in_specs=[here] * 6 + [there, here],
+        out_specs=[here, there, there, here, here, here, here],
+        scratch_shapes=scratch,
+        compiler_params=pltpu.CompilerParams(
+            collective_id=1, has_side_effects=True, vmem_limit_bytes=63 * 2**20
+        ),
+        cost_estimate=pl.CostEstimate(flops=30 * 10**9, bytes_accessed=40 * 10**6, transcendentals=10**7),
+        name="layer",
+    )(packed, small, classes, image_gain, image_bias, image_proj, tokens, ids)
+
+
+def on_kernel(
+    tokens,
+    segment_ids,
+    slot_valid,
+    ln1_gain,
+    ln1_bias,
+    w_qkv,
+    w_out,
+    ln2_gain,
+    ln2_bias,
+    w_up,
+    w_down,
+    class_tokens,
+    image_gain,
+    image_bias,
+    image_proj,
+):
+    dp_rank = lax.axis_index("dp")
+    depth, slots = w_up.shape[0], slot_valid.shape[0]
+    out_t = w_out.T
+    query, key, value = w_qkv[0], w_qkv[1], w_qkv[2]
+    attn = jnp.concatenate(
+        [
+            query[:, :128],
+            key[:, :128],
+            value[:, :128],
+            query[:, 128:],
+            value[:, 128:],
+            key[:, 128:],
+            out_t[:, 128:],
+            out_t[:, :128],
+        ],
+        axis=1,
+    )
+    packed = jnp.stack([attn, w_up, w_down.T])
+    norms = jnp.stack([ln1_gain, ln1_bias, ln2_gain, ln2_bias])
+    norms = jnp.where(
+        (jnp.arange(4) == lax.rem(dp_rank, 4))[None, :, None], norms[:, None, :], jnp.zeros((), bf16)
+    ).reshape(12, 128)
+    valid = jnp.where(
+        (jnp.arange(2) == lax.rem(dp_rank, 2))[:, None], slot_valid.astype(bf16)[None, :], jnp.zeros((), bf16)
+    ).reshape(1, 128)
+    small = jnp.concatenate([norms, valid, jnp.zeros((3, 128), bf16)], axis=0)
+    loss, block_out, token_grad, own_attn, own_up, own_down, vectors = layer(
+        slots * 32,
+        packed,
+        small,
+        class_tokens,
+        image_gain[None],
+        image_bias[None],
+        image_proj,
+        tokens,
+        segment_ids.reshape(4, 4, 128),
+    )
+    pick_cols = lambda *spans: jnp.concatenate([own_attn[:, a:b] for a, b in spans], axis=1)
+    qkv_grad = jnp.stack(
+        [pick_cols((0, 128), (384, 448)), pick_cols((128, 256), (512, 576)), pick_cols((256, 384), (448, 512))]
+    )
+    out_grad = pick_cols((640, 768), (576, 640)).T
+    vectors = lax.dynamic_slice_in_dim(vectors, dp_rank * depth, depth, 1)
+    return (
+        loss[0, 0],
+        block_out,
+        token_grad.astype(f32),
+        vectors[0],
+        vectors[1],
+        qkv_grad,
+        out_grad,
+        vectors[2],
+        vectors[3],
+        own_up,
+        own_down.T,
+    )
 
 
 def make(dp_size, mp_size):
@@ -249,8 +1057,9 @@
         P(),
         P(),
     )
+    sizes = (mesh.shape["dp"], mesh.shape["mp"])
     return jax.shard_map(
-        make(mesh.shape["dp"], mesh.shape["mp"]),
+        on_kernel if sizes == (8, 4) else make(*sizes),
         mesh=mesh,
         in_specs=placed,
         out_specs=(

time: 630 us -> 217 us (0.34); the launches traced: 621 us -> 216 us
  waiting for transfers between devices: 251 us -> 0 us
  Pallas kernels: 0 us -> 195 us
  blocking collectives: 144 us -> 0 us
  matrix products: 88.2 us -> 0 us
  local copies, waits for them, and re-layouts: 80.2 us -> 11.1 us
  other arithmetic: 39.1 us -> 10 us
  between operations: 17.4 us -> 0.77 us
    reduce_scatter x1 -> x0, waiting for transfers between devices: 221 us -> none  [on_device(): summed = lax.psum_scatter(local, both, scatter_dimension=0, tiled=False)]
    pallas_call x0 -> x1, Pallas kernels: none -> 195 us  [layer(): pl.pallas_call(functools.partial(layer_kernel, slot_total), out_shape=[ja...]
    dot_general x23 -> x0, matrix products: 84.9 us -> none  [the longest x2 27.2 us: feed(): jnp.einsum('mrf,mdf->rd', active, weights[2], preferred_element_type=f32)]
    psum x2 -> x0, blocking collectives: 80.6 us -> none  [the longest x1 41.2 us: on_device(): lax.psum(jnp.stack([gain_one, bias_one, gain_two, bias_two]), both)]
    unnamed x1 -> x0, blocking collectives: 43.3 us -> none
    all_gather x4 -> x0, waiting for transfers between devices: 30.7 us -> none  [the longest x1 30.6 us: on_device(): lax.all_gather(packed, both, axis=0).reshape(dp_size, mp_size, 3, depth, -1)]
    all_gather x1 -> x0, blocking collectives: 20.4 us -> none  [on_device(): vectors = lax.all_gather(norms, 'dp', axis=1, tiled=True).astype(f32)]
    slice x9 -> x11, local copies, waits for them, and re-layouts: 18.9 us -> 1.32 us  [the longest x1 1.19 us: on_kernel(): loss[0, 0]]
  transfers between devices with their start and end apart: 5 -> 0, of which waited for: 2 -> 0; matrix products, arithmetic and copies ran while one was open for 30% -> 0% of each run, Pallas kernels for 0% -> 0%
where the time goes in v2:
time: 217 us; the launch traced here: 216 us
  Pallas kernels  195 us (90%)
  local copies, waits for them, and re-layouts  11.1 us (5%)
  other arithmetic  10 us (5%)
    pallas_call x1, Pallas kernels, layer(): pl.pallas_call(functools.partial(layer_kernel, slot_total), out_shape=[ja...  195 us
    convert_element_type x1, other arithmetic, on_kernel(): token_grad.astype(f32)  5.23 us
    unnamed x13, local copies, waits for them, and re-layouts  4.74 us

profile of v2, /device:TPU:0, one launch (start us, length us, event | category | flops | bytes accessed | tf_op | source)
XLA Modules:
  0.0 216.4 jit_solution(6942180249305822115)
XLA Ops:
  0.6 0.9 slice_bitcast_fusion
  1.6 0.9 copy.26
  2.5 0.1 concatenate.18
  2.6 1.8 pad_maximum_fusion.refs_0_
  4.4 0.7 convert_element_type.6
  5.1 0.1 broadcast_select_fusion.1
  5.1 0.1 select_n.28
  5.2 0.7 pad_maximum_fusion.2
  5.9 0.1 broadcast_select_fusion
  6.0 0.1 select_n.26
  6.1 0.1 pad.13.clone
  6.2 0.7 maximum_maximum_fusion.refs_1_
  6.9 1.3 broadcast_in_dim.60.refs_3_
  8.1 1.3 broadcast_in_dim.61.refs_4_
  9.4 194.5 %layer.1 = (f32[8,128]{1,0:T(8,128)}, bf16[2048,768]{1,0:T(8,128)(2,1)}, bf16[2048,768]{1,0:T(8,128)(2,1)}, f32[96,768]{1,0:T(8,128)}, f32[96,768]{1,0:T(8,128)}, /*index=5*/f32[96,768]{1,0:T(8,128)}, f32[8,768]{1,0:T(8,128)}) custom-call(bf16[3,96,768]{2,1,0:T(8,128)(2,1)} %pad_maximum_fusion.refs_0_, bf16[16,128]{1,0:T(8,128)(2,1)} %maximum_maximum_fusion.refs_1_, ...), custom_call_target="tpu_custom_call" | custom-call | flops 30000001024 | bytes 40000000 | tf_op jit(solution)/shard_map/layer/pallas_call | solution.py:759
  203.9 1.2 slice.83
  205.1 0.0 copy-start.1
  205.1 0.0 copy-start
  205.1 5.2 %convert_element_type.7 = f32[2048,768]{1,0:T(8,128)} convert(bf16[2048,768]{1,0:T(8,128)(2,1)} %get-tuple-element.20) | non-fusion elementwise | flops 1572864 | bytes 9437184 | tf_op jit(solution)/shard_map/convert_element_type | solution.py:844
  210.4 0.8 constant_dynamic-slice_fusion
  211.1 0.5 slice_bitcast_fusion.3
  211.7 0.0 copy-done.1
  211.7 0.1 fusion.1
  211.8 0.7 pad_maximum_fusion.1
  212.6 0.7 copy.27
  213.3 0.0 copy-done
  213.3 0.0 copy-start.3
  213.3 1.7 copy.31
  215.0 0.0 copy-done.3
  215.0 0.7 copy.32
  215.7 0.0 copy-done.2
  215.7 0.7 copy.33
  (16 shorter events, 0.1 us)
Async XLA Ops:
  205.1 6.5 %copy-start.1 = (f32[96,768]{1,0:T(8,128)S(1)}, f32[96,768]{1,0:T(8,128)}, u32[]{:S(2)}) copy-start(f32[96,768]{1,0:T(8,128)} %get-tuple-element.22) | copy-start | bytes 884740
  205.1 8.2 %copy-start = (bf16[2048,768]{1,0:T(8,128)(2,1)S(1)}, bf16[2048,768]{1,0:T(8,128)(2,1)}, u32[]{:S(2)}) copy-start(bf16[2048,768]{1,0:T(8,128)(2,1)} %get-tuple-element.65) | copy-start | bytes 9437188
  213.3 1.7 copy-start.3
  213.3 2.4 %copy-start.2 = (f32[96,768]{1,0:T(8,128)S(1)}, f32[96,768]{1,0:T(8,128)}, u32[]{:S(2)}) copy-start(f32[96,768]{1,0:T(8,128)} %get-tuple-element.24) | copy-start | bytes 884740

commit v3 on v2

--- a/solution.py
+++ b/solution.py
@@ -51,7 +51,6 @@
 MESH = pl.DeviceIdType.MESH
 VMEM, DMA = pltpu.VMEM, pltpu.SemaphoreType.DMA
 CUT = 48
-LATE = 48
 
 
 def loop(count, body):
@@ -82,15 +81,16 @@
 
 
 def layer_kernel(slot_total, *refs):
-    (packed, small, classes, image_gain, image_bias, image_proj, tokens, ids) = refs[:8]
-    (loss_out, block_out, token_out, attn_out, up_out, down_out, vec_out) = refs[8:15]
-    (w_attn, w_up, w_down, images, smalls, x_ref, a_ref, qkv, hidden, a_two, active, stage_out, image_own, vecs) = refs[15:29]
-    (mask_ref, place_ref, member_ref, h_ends, ends_two, ends_grad, u_ends, g_all, s_all, weight_ref, valid_ref) = refs[29:40]
-    (sum_own, sum_buf, sum_got, d_attn, d_qkv) = refs[40:45]
-    (grad_down, grad_up, ffn_one, ffn_three, attn_send, attn_acc, attn_core, one_p, one_q, two_p, two_q, three_a) = refs[45:57]
-    (vec_buf, vec_got, stage_grad, grad_got) = refs[57:61]
-    gsems = refs[61:96]
-    (s_local, s_bo, s_boc, s_send, s_a2, s_dm, s_sum, s_sums, s_f1, s_f3, s_core, s_1p, s_1q, s_2p, s_2q, s_3, s_v, s_vs, s_tg, s_exs) = refs[96:116]
+    (w_qkv, w_out, up_own, down_own, norms, valid_own, classes, image_gain, image_bias, image_proj, tokens, ids) = refs[:12]
+    (loss_out, block_out, token_out, attn_out, up_out, down_out, vec_out) = refs[12:19]
+    (w_attn, w_up, w_down, images, smalls, x_ref, a_ref, qkv, hidden, a_two, active, stage_out, image_own, vecs) = refs[19:33]
+    (mask_ref, place_ref, member_ref, h_ends, ends_two, ends_grad, u_ends, g_all, s_all, weight_ref, valid_ref) = refs[33:44]
+    (sum_own, sum_buf, sum_got, d_attn, d_far) = refs[44:49]
+    (grad_down, grad_up, grad_attn, step_x, step_z, attn_send, attn_core, ends_back) = refs[49:57]
+    (vec_buf, vec_got, stage_grad, attn_own, small_own, far_mix) = refs[57:63]
+    gsems = refs[63:91]
+    isems = refs[91:100]
+    (s_local, s_bo, s_on, s_send, s_a2, s_dm, s_dh, s_sum, s_sums, s_x, s_z, s_core, s_v, s_vs, s_tg, s_exs) = refs[100:116]
 
     dp = lax.axis_index("dp")
     mp = lax.axis_index("mp")
@@ -103,15 +103,14 @@
     zs = [lax.rem(z + 4 - j, 4) for j in range(4)]
     X, Y, C, YC = (xd, mp), (dp, ym), (dp, cm), (dp, 3 - mp)
     Z = [(2 * zt[j] + x, mp) for j in range(4)]
-    xy = 2 * y + x
-    Q = []
-    for j in range(1, 4):
-        other = lax.rem(xy + j, 4)
-        Q.append((2 * z + lax.rem(other, 2), 2 * lax.div(other, 2) + c))
+    here = 4 * x + mp
+    PLANE = []
+    for j in range(1, 8):
+        other = lax.rem(here + j, 8)
+        PLANE.append((2 * z + lax.div(other, 4), lax.rem(other, 4)))
     G = [(dp, lax.rem(mp + j, 4)) for j in range(4)]
 
-    far_xy = (2 * z + (1 - x), 2 * (1 - y) + c)
-    peers = [X, Y, C, YC, far_xy] + Z[1:]
+    peers = PLANE + Z[1:]
     barrier = pltpu.get_barrier_semaphore()
     for peer in peers:
         pl.semaphore_signal(barrier, inc=1, device_id=peer, device_id_type=MESH)
@@ -206,14 +205,105 @@
 
         return [step0, step1, step2, step3, step4]
 
-    depth = packed.shape[1]
+    depth = up_own.shape[0]
     slots = classes.shape[0]
+
+    def image_steps():
+        near, cross, core, near_sent, core_sent, up_got, down_got, up_sent, down_sent = isems
+
+        def at(d, m, start=0, size=slots):
+            return images.at[m, pl.ds(pl.multiple_of(d * slots + start, 16), size)]
+
+        def plane(z_, i):
+            return images.at[2 * i + c, pl.ds(pl.multiple_of(2 * z_ * slots, 16), 2 * slots)]
+
+        def to_core(ref):
+            remote(ref, ref, core_sent.at[0], core.at[0], C)
+
+        half = slots // 2
+
+        def step0():
+            remote(image_own, at(dp, mp), near_sent.at[0], near.at[0], X)
+            remote(image_own, at(dp, mp), near_sent.at[0], near.at[1], Y)
+            remote(image_own, at(dp, mp), core_sent.at[0], core.at[0], C)
+            pltpu.make_async_copy(image_own, at(dp, mp), s_local.at[5]).start()
+            yield
+
+        def step1():
+            arrived(at(xd, mp), near.at[0], near_sent.at[0])
+            remote(at(xd, mp, 0, half), at(xd, mp, 0, half), near_sent.at[0], cross.at[0], Y)
+            to_core(at(xd, mp))
+            arrived(at(dp, ym), near.at[1], near_sent.at[0])
+            remote(at(dp, ym, half, half), at(dp, ym, half, half), near_sent.at[0], cross.at[1], X)
+            to_core(at(dp, ym))
+            yield
+
+        def up(i, t):
+            ref = plane(z - t, i)
+            return pltpu.make_async_remote_copy(
+                src_ref=ref, dst_ref=ref, send_sem=up_sent.at[t, i], recv_sem=up_got.at[t, i],
+                device_id=(2 * (z + 1) + x, mp), device_id_type=MESH,
+            )
+
+        def down(i, t):
+            ref = plane(z + t, i)
+            return pltpu.make_async_remote_copy(
+                src_ref=ref, dst_ref=ref, send_sem=down_sent.at[t, i], recv_sem=down_got.at[t, i],
+                device_id=(2 * (z - 1) + x, mp), device_id_type=MESH,
+            )
+
+        def step2():
+            arrived(at(xd, ym, 0, half), cross.at[0], near_sent.at[0])
+            arrived(at(xd, ym, half, half), cross.at[1], near_sent.at[0])
+            to_core(at(xd, ym))
+            pltpu.make_async_copy(image_own, at(dp, mp), s_local.at[5]).wait()
+            for i in range(2):
+                pl.when(z < 3)(lambda i=i: up(i, 0).start())
+                pl.when(z > 0)(lambda i=i: down(i, 0).start())
+            yield
+
+        def step3():
+            for t in range(1, 4):
+                for i in range(2):
+
+                    def from_below(i=i, t=t):
+                        ref = plane(z - t, i)
+                        arrived(ref, up_got.at[t - 1, i], near_sent.at[0])
+                        if t < 3:
+                            pl.when(z < 3)(lambda: up(i, t).start())
+                        to_core(ref)
+
+                    def from_above(i=i, t=t):
+                        ref = plane(z + t, i)
+                        arrived(ref, down_got.at[t - 1, i], near_sent.at[0])
+                        if t < 3:
+                            pl.when(z > 0)(lambda: down(i, t).start())
+                        to_core(ref)
+
+                    pl.when(z >= t)(from_below)
+                    pl.when(z + t <= 3)(from_above)
+                    yield
+
+        def step4():
+            halves = images.at[pl.ds(0, 2)]
+            pltpu.make_async_copy(halves, halves, core.at[0]).wait()
+            pltpu.make_async_copy(halves, halves, core_sent.at[0]).wait()
+            three = images.at[0, pl.ds(0, 3 * slots)]
+            pltpu.make_async_copy(three, three, near_sent.at[0]).wait()
+            for t in range(3):
+                for i in range(2):
+                    pl.when((z >= t) & (z < 3))(lambda i=i, t=t: up(i, t).wait_send())
+                    pl.when((z + t <= 3) & (z > 0))(lambda i=i, t=t: down(i, t).wait_send())
+            yield
+
+        return [step0, step1, step2, step3, step4]
+
     kinds = {
-        "S": gather_steps(small, smalls, 16, 0, gsems[0:7]),
-        "A": gather_steps(packed.at[0], w_attn, depth, CUT, gsems[7:14]),
-        "U": gather_steps(packed.at[1], w_up, depth, CUT, gsems[14:21]),
-        "D": gather_steps(packed.at[2], w_down, depth, CUT, gsems[21:28]),
-        "I": gather_steps(image_own, images, slots, slots // 2, gsems[28:35]),
+        "S": gather_steps(small_own, smalls, 16, 0, gsems[0:7]),
+        "A": gather_steps(attn_own, w_attn, depth, CUT, gsems[7:14]),
+        "U": gather_steps(up_own, w_up, depth, CUT, gsems[14:21]),
+        "D": gather_steps(down_own, w_down, depth, CUT, gsems[21:28]),
+        "I": image_steps(),
     }
 
     def run(*steps):
@@ -224,7 +314,7 @@
     def blend(steps, chunks):
         chunks = list(chunks)
         micro = [kinds[name[0]][int(name[1])] for name in steps]
-        count = sum((1, 3, 4, 8, 1)[int(name[1])] for name in steps)
+        count = sum((1, 3, 4, 8, 1)[int(name[1])] if name[0] != "I" else (1, 1, 1, 6, 1)[int(name[1])] for name in steps)
         done, at = 0, 0
         for step in micro:
             for _ in step():
@@ -238,7 +328,7 @@
     lane = lax.broadcasted_iota(jnp.int32, (128, 128), 1)
     sub = lax.broadcasted_iota(jnp.int32, (128, 128), 0)
     low = lax.broadcasted_iota(jnp.int32, (1, 128), 1) < 64
-    token_rows = x_ref.shape[0]
+    token_rows = hidden.shape[0]
     tiles = token_rows // 128
     end_count = h_ends.shape[0]
 
@@ -248,25 +338,47 @@
     def keep_high(values):
         return jnp.where(low, jnp.zeros_like(values), values)
 
-    def masks():
+    def pack_own():
+        rows = lax.broadcasted_iota(jnp.int32, (depth, depth), 0)
+        eye = (rows == lax.broadcasted_iota(jnp.int32, (depth, depth), 1)).astype(f32).astype(bf16)
+        out_t = nt(eye, w_out[...]).astype(bf16)
+        query, key, value = w_qkv[0], w_qkv[1], w_qkv[2]
+        attn_own[:, 0:128] = query[:, 0:128]
+        attn_own[:, 128:256] = key[:, 0:128]
+        attn_own[:, 256:384] = value[:, 0:128]
+        attn_own[:, 384:512] = jnp.concatenate([query[:, 128:192], value[:, 128:192]], axis=1)
+        attn_own[:, 512:640] = jnp.concatenate([key[:, 128:192], out_t[:, 128:192]], axis=1)
+        attn_own[:, 640:768] = out_t[:, 0:128]
+
+    def pack_small():
+        shift = lax.broadcasted_iota(jnp.int32, (depth, 384), 1) - lax.broadcasted_iota(jnp.int32, (depth, 384), 0)
+        made = nn(norms[...], (shift == depth * lax.rem(dp, 4)).astype(f32).astype(bf16))
+        shift = lax.broadcasted_iota(jnp.int32, (slots, 128), 1) - lax.broadcasted_iota(jnp.int32, (slots, 128), 0)
+        flags = jnp.broadcast_to(valid_own[...].astype(f32), (8, slots)).astype(bf16)
+        flags = nn(flags, (shift == slots * lax.rem(dp, 2)).astype(f32).astype(bf16))
+        parts = [made[v : v + 1, 128 * t : 128 * (t + 1)] for v in range(4) for t in range(3)]
+        small_own[...] = jnp.concatenate(parts + [flags[0:4, :]], axis=0).astype(bf16)
+
+    def masks(g):
         slot_row = lax.broadcasted_iota(jnp.int32, (end_count, 128), 0)
-        parts, spots = [], []
+        spots = []
         best = jnp.full((end_count, 1), -1, jnp.int32)
         for b in range(tiles):
-            caption = 2 * (8 * b + lax.shift_right_logical(lax.broadcasted_iota(jnp.int32, (1, 128), 1), 4)) + ids[mp, pl.ds(b, 1), :]
+            sequence = 8 * b + lax.shift_right_logical(lax.broadcasted_iota(jnp.int32, (1, 128), 1), 4)
+            caption = 2 * sequence + ids[ym if g else mp, pl.ds(b, 1), :]
             column = jnp.sum(jnp.where(lane == sub, caption, 0), axis=1, keepdims=True)
-            mask_ref[b] = jnp.where((column == caption) & (sub >= lane), 0.0, -1e30)
+            mask_ref[tiles * g + b] = jnp.where((column == caption) & (sub >= lane), 0.0, -1e30)
             member = slot_row == caption
             spot = lax.broadcasted_iota(jnp.int32, (end_count, 128), 1) + 128 * b
             best = jnp.maximum(best, jnp.max(jnp.where(member, spot, -1), axis=1, keepdims=True))
-            member_ref[:, 128 * b : 128 * (b + 1)] = jnp.where(member, 0.0, -1e30)
+            member_ref[g, :, 128 * b : 128 * (b + 1)] = jnp.where(member, 0.0, -1e30)
             spots.append(spot)
         for b in range(tiles):
-            place_ref[:, 128 * b : 128 * (b + 1)] = (spots[b] == best).astype(f32).astype(bf16)
+            place_ref[g, :, 128 * b : 128 * (b + 1)] = (spots[b] == best).astype(f32).astype(bf16)
 
     def image_tower():
         hat, _ = standardise(classes[...].astype(f32))
-        raw = nn((hat * image_gain[...] + image_bias[...]).astype(bf16), image_proj[...])
+        raw = nn((hat * image_gain[...].reshape(1, -1) + image_bias[...].reshape(1, -1)).astype(bf16), image_proj[...])
         image_own[...] = (raw * inverse_norm(raw)).astype(bf16)
 
     def small_vectors():
@@ -283,13 +395,14 @@
                 both = sum(smalls[m, 32 * pair + 16 * d : 32 * pair + 16 * (d + 1), :].astype(f32) for d in range(2))
                 valid_ref[m : m + 1, 128 * pair : 128 * (pair + 1)] = both[12:13, :]
 
-    def first_norm():
+    def first_norm(g):
         def body(b):
-            rows = rows_of(b, 128)
+            rows = rows_of(tiles * g + b, 128)
             values = x_ref[rows, :].astype(f32)
             hat, _ = standardise(values)
             a_ref[rows, :] = (hat * vecs[0:1, :] + vecs[1:2, :]).astype(bf16)
-            hidden[rows, :] = values
+            if g == 0:
+                hidden[rows, :] = values
 
         loop(tiles, body)
 
@@ -300,23 +413,37 @@
 
     scale = HEAD_DIM**-0.5
 
+    def project(m, g):
+        def body(b):
+            rows = rows_of(2 * g + b, 256)
+            qkv[m, rows, :] = nn(a_ref[rows, :], w_attn[m]).astype(bf16)
+
+        loop(2, body)
+
     def attention(m):
-        def body(b):
-            rows = rows_of(b, 128)
-            made = nn(a_ref[rows, :], w_attn[m]).astype(bf16)
-            q01, k01, v01, qv, ko = (made[:, 128 * i : 128 * (i + 1)] for i in range(5))
-            mask = mask_ref[b]
-            p0 = soft(nt(keep_low(q01), k01) * scale + mask).astype(bf16)
-            p1 = soft(nt(keep_high(q01), k01) * scale + mask).astype(bf16)
-            p2 = soft(nt(keep_low(qv), ko) * scale + mask).astype(bf16)
-            o01 = jnp.where(low, nn(p0, v01), nn(p1, v01)).astype(bf16)
-            o2 = keep_high(nn(p2, qv)).astype(bf16)
-            qkv[m, rows, 0:512] = made[:, 0:512]
-            qkv[m, rows, 512:640] = keep_low(ko) + o2
-            qkv[m, rows, 640:768] = o01
-            hidden[rows, :] += nt(o2, w_attn[m, :, 512:640]) + nt(o01, w_attn[m, :, 640:768])
-
-        loop(tiles, body)
+        project(m, 0)
+
+        def body(pair):
+            for b in (2 * pair, 2 * pair + 1):
+                rows = rows_of(b, 128)
+                q01, k01, v01, qv, ko = (qkv[m, rows, 128 * i : 128 * (i + 1)] for i in range(5))
+                mask = mask_ref[b]
+                p0 = soft(nt(keep_low(q01), k01) * scale + mask).astype(bf16)
+                p1 = soft(nt(keep_high(q01), k01) * scale + mask).astype(bf16)
+                p2 = soft(nt(keep_low(qv), ko) * scale + mask).astype(bf16)
+                o01 = jnp.where(low, nn(p0, v01), nn(p1, v01)).astype(bf16)
+                o2 = keep_high(nn(p2, qv)).astype(bf16)
+                qkv[m, rows, 512:640] = keep_low(ko) + o2
+                qkv[m, rows, 640:768] = o01
+
+        loop(tiles // 2, body)
+
+        def attended(b):
+            rows = rows_of(b, 256)
+            mixed = jnp.concatenate([keep_high(qkv[m, rows, 512:640]), qkv[m, rows, 640:768]], axis=1)
+            hidden[rows, :] += nt(mixed, w_attn[m, :, 512:768])
+
+        loop(2, attended)
 
     def second_norm():
         def body(b):
@@ -325,7 +452,7 @@
             a_two[rows, :] = (hat * vecs[2:3, :] + vecs[3:4, :]).astype(bf16)
 
         loop(tiles, body)
-        place = place_ref[...]
+        place = place_ref[0]
         ends = pick(place, hidden[...])
         h_ends[...] = ends
         hat, _ = standardise(ends)
@@ -336,11 +463,11 @@
 
     def full_up(m):
         def body(b):
-            rows = rows_of(b, 128)
+            rows = rows_of(b, 256)
             upper = nn(a_two[rows, :], w_up[m])
             active[m, rows, :] = (upper * half_erf(upper)).astype(bf16)
 
-        loop(tiles, body)
+        loop(tiles // 2, body)
 
     def slope_of(upper):
         return half_erf(upper) + upper * jnp.exp(-0.5 * upper * upper) * (1.0 / (2.0 * jnp.pi) ** 0.5)
@@ -355,34 +482,46 @@
         loop(4, body)
 
     def full_down(b):
-        rows = slice(128 * b, 128 * (b + 1))
-        hidden_down = hidden[rows, :]
+        rows = slice(256 * b, 256 * (b + 1))
 
         def body(m, total):
             return total + nt(active[m, rows, :], w_down[m])
 
-        stage_out[rows, :] = lax.fori_loop(0, 4, body, hidden_down).astype(bf16)
-
-    own_tokens = pltpu.make_async_copy(tokens.at[rows_of(mp, token_rows)], x_ref, s_local.at[0])
-    own_tokens.start()
-    run("S0", "A0", "U0")
+        stage_out[rows, :] = lax.fori_loop(0, 4, body, hidden[rows, :]).astype(bf16)
+
+    token_copies = []
+    for g in range(2):
+        wanted = tokens.at[rows_of(ym if g else mp, token_rows)]
+        token_copies.append(pltpu.make_async_copy(wanted, x_ref.at[pl.ds(g * token_rows, token_rows)], s_local.at[g]))
+        token_copies[g].start()
+    pack_small()
+    run("S0")
+    pack_own()
+    run("A0")
     image_tower()
-    masks()
-    run("S1", "A1", "D0", "I0", "S2", "A2", "U1", "S3", "S4")
-    own_tokens.wait()
+    run("I0", "U0")
+    masks(0)
+    masks(1)
+    run("S1", "A1", "D0", "I1", "S2", "A2", "I2", "U1", "S3", "S4")
     small_vectors()
-    first_norm()
+    for g in range(2):
+        token_copies[g].wait()
+        first_norm(g)
     run("D1", "A3", "A4")
-    blend(("U2", "I1", "D2", "U3", "I2"), [functools.partial(attention, m) for m in range(4)])
+    blend(("U2", "I3", "D2", "U3"), [functools.partial(attention, m) for m in range(4)])
     second_norm()
     swaps = [remote(ends_two.at[mp], ends_two.at[mp], s_exs.at[j - 1], s_a2.at[j - 1], G[j]) for j in range(1, 4)]
     run("U4")
-    blend(("D3", "I3"), [functools.partial(full_up, m) for m in range(4)])
+    blend(
+        ("D3",),
+        [functools.partial(full_up, m) for m in range(4)] + [functools.partial(project, m, 1) for m in range(4)],
+    )
     loop(4, ends_up)
+    run("I4")
     for swap in swaps:
         swap.wait()
     group_up()
-    run("D4", "I4")
+    run("D4")
 
     pooled = h_ends[...]
     for m in range(4):
@@ -390,7 +529,7 @@
         pooled = pooled + nt((upper * half_erf(upper)).astype(bf16), w_down[m])
     scale_back = inverse_norm(pooled)
     text = (pooled * scale_back).astype(bf16)
-    own_valid = small[12:13, :].astype(f32)
+    own_valid = small_own[12:13, :].astype(f32)
     own_valid = jnp.max(
         jnp.where(
             lax.rem(lax.broadcasted_iota(jnp.int32, (slots, 128), 1), slots)
@@ -423,22 +562,20 @@
     row_part = jnp.sum(jnp.where(live, jnp.log(row_sum) - 2.0 * matched, 0.0), axis=0, keepdims=True)
     sum_own[16:24, :] = jnp.broadcast_to(row_part, (8, 128))
 
-    swap = remote(sum_own, sum_got.at[0], s_sums.at[0], s_sum.at[0], C)
+    swaps = [remote(sum_own, sum_got.at[here], s_sums.at[j - 1], s_sum.at[j - 1], PLANE[j - 1]) for j in range(1, 8)]
+    sum_got[here] = sum_own[...]
     full_down(0)
-    swap.wait()
-    sum_buf[0] = sum_own[...] + sum_got[0]
-    swaps = [remote(sum_buf.at[0], sum_got.at[1 + xy], s_sums.at[j], s_sum.at[j], Q[j - 1]) for j in range(1, 4)]
-    sum_got[1 + xy] = sum_buf[0]
+    for swap in swaps:
+        swap.wait()
+    sum_buf[...] = ((sum_got[0] + sum_got[1]) + (sum_got[2] + sum_got[3])) + (
+        (sum_got[4] + sum_got[5]) + (sum_got[6] + sum_got[7])
+    )
+    swaps = [remote(sum_buf, sum_got.at[8 + z], s_sums.at[6 + j], s_sum.at[6 + j], Z[j]) for j in range(1, 4)]
+    sum_got[8 + z] = sum_buf[...]
     full_down(1)
     for swap in swaps:
         swap.wait()
-    sum_buf[1] = (sum_got[1] + sum_got[2]) + (sum_got[3] + sum_got[4])
-    swaps = [remote(sum_buf.at[1], sum_got.at[5 + z], s_sums.at[3 + j], s_sum.at[3 + j], Z[j]) for j in range(1, 4)]
-    sum_got[5 + z] = sum_buf[1]
-    full_down(2)
-    for swap in swaps:
-        swap.wait()
-    sums = (sum_got[5] + sum_got[6]) + (sum_got[7] + sum_got[8])
+    sums = (sum_got[8] + sum_got[9]) + (sum_got[10] + sum_got[11])
 
     total = sums[16:17, 0:1]
     unit_grad = jnp.zeros((slots, text.shape[1]), f32)
@@ -449,21 +586,20 @@
         spread = 0.5 * weight_ref[m] * (1.0 / row_sum + 1.0 / columns)
         grad = jnp.where(seen & live, spread, 0.0) - jnp.where(target_of(m) & live, 1.0, 0.0)
         unit_grad = unit_grad + nn((logit_scale * grad).astype(bf16), images[m])
-    loss_out[...] = jnp.broadcast_to(total * (0.5 / slot_total), (8, 128))
+    loss_out[...] = total * (0.5 / slot_total)
     along = jnp.sum(unit_grad * pooled, axis=-1, keepdims=True)
     pooled_grad = scale_back * unit_grad - pooled * (scale_back * scale_back * scale_back * along)
     branch_grad = pooled_grad.astype(bf16)
     ends_grad[mp] = branch_grad
     swaps = [remote(ends_grad.at[mp], ends_grad.at[mp], s_exs.at[2 + j], s_dm.at[j - 1], G[j]) for j in range(1, 4)]
 
-    full_down(3)
     own_rows = rows_of(mp, token_rows)
     far_rows = rows_of(ym, token_rows)
     out_swaps = [
         remote(stage_out, block_out.at[own_rows], s_bo.at[0], s_bo.at[1], Y),
         remote(stage_out, block_out.at[own_rows], s_bo.at[2], s_bo.at[3], C),
     ]
-    keep_out = pltpu.make_async_copy(stage_out, block_out.at[own_rows], s_local.at[1])
+    keep_out = pltpu.make_async_copy(stage_out, block_out.at[own_rows], s_local.at[2])
     keep_out.start()
 
     two_grad = jnp.zeros_like(pooled)
@@ -475,57 +611,55 @@
     vec_buf[0, 2:3, :] = jnp.sum(two_grad * hat_two, axis=0, keepdims=True)
     vec_buf[0, 3:4, :] = jnp.sum(two_grad, axis=0, keepdims=True)
     hidden_grad = pooled_grad + norm_pull(two_grad, hat_two, rstd_two, vecs[2:3, :])
-    attended_grad = hidden_grad.astype(bf16)
-    h_ends[...] = hidden_grad
+    ends_back[0] = hidden_grad.astype(bf16)
+    back_swap = remote(ends_back.at[0], ends_back.at[1], s_exs.at[6], s_dh.at[0], Y)
 
     for swap in swaps:
         swap.wait()
     group_grad = ends_grad[...].reshape(4 * end_count, -1)
     upper_grad = (nn(group_grad, w_down[mp]) * s_all[...]).astype(bf16)
-    s_all_grad = upper_grad
     grad_down[...] = tn(group_grad, g_all[...]).astype(bf16)
 
     def block(z_, x_):
         return pl.ds(pl.multiple_of((2 * z_ + x_) * depth, 16), depth)
 
-    ffn = [grad_down, grad_up]
-
-    def ffn_start(k):
+    grads, outs = [grad_down, grad_up, grad_attn], [down_out, up_out, attn_out]
+
+    def sum_start(k):
         for j in (2, 1, 3, 0):
-            remote(ffn[k].at[block(zt[j], 1 - x)], ffn_one.at[k, j], s_send.at[k], s_f1.at[k, j], X)
-
-    def ffn_add(k, out):
-        for j in (2, 1, 3, 0):
-            arrived(ffn_one.at[k, j], s_f1.at[k, j], s_send.at[k])
-            mine = block(zt[j], x)
-            summed = ffn[k][mine, :].astype(f32) + ffn_one[k, j].astype(f32)
-            if j:
-                ffn[k][mine, :] = summed.astype(bf16)
-                remote(ffn[k].at[mine], ffn_three.at[k, j - 1], s_send.at[k], s_f3.at[k, j - 1], Z[j])
-            else:
-                out[...] = summed
-
-    def ffn_end(k, out):
+            remote(grads[k].at[block(zt[j], 1 - x)], step_x.at[k, j], s_send.at[k], s_x.at[k, j], X)
+
+    def sum_add(k, j):
+        arrived(step_x.at[k, j], s_x.at[k, j], s_send.at[k])
+        mine = block(zt[j], x)
+        summed = grads[k][mine, :].astype(f32) + step_x[k, j].astype(f32)
+        if j:
+            grads[k][mine, :] = summed.astype(bf16)
+            remote(grads[k].at[mine], step_z.at[k, j - 1], s_send.at[k], s_z.at[k, j - 1], Z[j])
+        else:
+            outs[k][...] = summed
+
+    def sum_end(k):
         for j in range(1, 4):
-            arrived(ffn_three.at[k, j - 1], s_f3.at[k, j - 1], s_send.at[k])
-        out[...] = out[...] + ffn_three[k, 0].astype(f32) + ffn_three[k, 1].astype(f32) + ffn_three[k, 2].astype(f32)
-        sent = ffn[k].at[pl.ds(0, 7 * depth)]
+            arrived(step_z.at[k, j - 1], s_z.at[k, j - 1], s_send.at[k])
+        outs[k][...] = outs[k][...] + step_z[k, 0].astype(f32) + step_z[k, 1].astype(f32) + step_z[k, 2].astype(f32)
+        sent = grads[k].at[pl.ds(0, 7 * depth)]
         pltpu.make_async_copy(sent, sent, s_send.at[k]).wait()
 
-    ffn_start(0)
-    grad_up[...] = tn(ends_two[...].reshape(4 * end_count, -1), s_all_grad).astype(bf16)
-    ffn_start(1)
-
-    d_attn[...] = jnp.zeros_like(d_attn)
-
-    def attention_back(m):
-        place = place_ref[...]
-        member = member_ref[...]
-        k01, v01, qv, ko = (qkv[m, :, 128 * i : 128 * (i + 1)] for i in range(1, 5))
-        q_e = nn(place, qkv[m, :, 0:128]).astype(bf16)
+    sum_start(0)
+    grad_up[...] = tn(ends_two[...].reshape(4 * end_count, -1), upper_grad).astype(bf16)
+    sum_start(1)
+
+    def attention_back(m, g, mix=False):
+        place = place_ref[g]
+        member = member_ref[g]
+        ends_row = ends_back[g]
+        span = slice(token_rows * g, token_rows * (g + 1))
+        k01, v01, qv, ko = (qkv[m, span, 128 * i : 128 * (i + 1)] for i in range(1, 5))
+        q_e = nn(place, qkv[m, span, 0:128]).astype(bf16)
         q2_e = keep_low(nn(place, qv)).astype(bf16)
-        do01 = nn(attended_grad, w_attn[m, :, 640:768]).astype(bf16)
-        do2 = keep_high(nn(attended_grad, w_attn[m, :, 512:640])).astype(bf16)
+        do01 = nn(ends_row, w_attn[m, :, 640:768]).astype(bf16)
+        do2 = keep_high(nn(ends_row, w_attn[m, :, 512:640])).astype(bf16)
 
         def head(query, keys, values, outer):
             probs = soft(nt(query, keys) * scale + member)
@@ -538,146 +672,127 @@
         p2, ds2 = head(q2_e, ko, qv, do2)
         dq01 = (jnp.where(low, nn(ds0, k01), nn(ds1, k01)) * scale).astype(bf16)
         dq2 = keep_low(nn(ds2, ko) * scale).astype(bf16)
-        d_qkv[m, :, 0:128] = tn(place, dq01).astype(bf16)
-        d_qkv[m, :, 128:256] = (jnp.where(low, tn(ds0, q_e), tn(ds1, q_e)) * scale).astype(bf16)
-        d_qkv[m, :, 256:384] = jnp.where(low, tn(p0, do01), tn(p1, do01)).astype(bf16)
-        d_qkv[m, :, 384:512] = jnp.where(low, tn(place, dq2), tn(p2, do2)).astype(bf16)
-        d_qkv[m, :, 512:640] = keep_low(tn(ds2, q2_e) * scale).astype(bf16)
-
-    def token_back(m):
+        if g == 1 and mix:
+            far_mix[:, 0:128] = nn(p2, qv).astype(bf16)
+            far_mix[:, 128:256] = jnp.where(low, nn(p0, v01), nn(p1, v01)).astype(bf16)
+        d_ref = d_far if g else active
+        d_ref[m, :, 0:128] = tn(place, dq01).astype(bf16)
+        d_ref[m, :, 128:256] = (jnp.where(low, tn(ds0, q_e), tn(ds1, q_e)) * scale).astype(bf16)
+        d_ref[m, :, 256:384] = jnp.where(low, tn(p0, do01), tn(p1, do01)).astype(bf16)
+        d_ref[m, :, 384:512] = jnp.where(low, tn(place, dq2), tn(p2, do2)).astype(bf16)
+        d_ref[m, :, 512:640] = keep_low(tn(ds2, q2_e) * scale).astype(bf16)
+
+    def token_back(g):
+        d_ref = d_far if g else active
+
         def body(b):
-            rows = rows_of(b, 128)
-            d_attn[rows, :] += nt(d_qkv[m, rows, 0:640], w_attn[m, :, 0:640])
+            rows = rows_of(b, 256)
+            total = jnp.zeros((256, d_attn.shape[1]), f32)
+            for m in range(4):
+                total = total + nt(d_ref[m, rows, 0:640], w_attn[m, :, 0:640])
+            d_attn[rows_of(2 * g + b, 256), :] = total
+
+        loop(2, body)
+
+    def attn_grad(m):
+        ends_mix = nn(place_ref[0], qkv[m, 0:token_rows, 512:768]).astype(bf16)
+        outer = tn(ends_back[0], ends_mix) + tn(ends_back[1], far_mix[...])
+
+        def made(start, stop):
+            span = slice(start, stop)
+            return tn(a_ref[0:token_rows, :], active[m, :, span]) + tn(a_ref[token_rows:, :], d_far[m, :, span])
+
+        last = jnp.where(low, made(512, 640), outer[:, 0:128])
+        return jnp.concatenate([made(0, 512), last, outer[:, 128:256]], axis=1)
+
+    steps = iter([(k, j) for k in range(3) for j in range(4)])
+
+    def sum_some(count):
+        for _ in range(count):
+            k, i = next(steps)
+            sum_add(k, (2, 1, 3, 0)[i])
+
+    back_swap.wait()
+    m = 2 * y + (1 - c)
+    attention_back(m, 0, True)
+    attention_back(m, 1, True)
+    sum_some(1)
+    attn_send[...] = attn_grad(m).astype(bf16)
+    core_swap = remote(attn_send, attn_core, s_exs.at[7], s_core.at[0], C)
+    sum_some(1)
+    m = 2 * y + c
+    attention_back(m, 0, True)
+    attention_back(m, 1, True)
+    sum_some(1)
+    made = attn_grad(m)
+    core_swap.wait()
+    grad_attn[...] = (made + attn_core[...].astype(f32)).astype(bf16)
+    sum_start(2)
+    sum_some(1)
+    for i in range(2):
+        for g in range(2):
+            attention_back(2 * (1 - y) + i, g)
+            sum_some(1)
+    def token_end(g):
+        def body(b):
+            rows = rows_of(tiles * g + b, 128)
+            hat, rstd = standardise(x_ref[rows, :].astype(f32))
+            grad = d_attn[rows, :]
+            if g == 0:
+                vec_buf[0, 0:1, :] += jnp.sum(grad * hat, axis=0, keepdims=True)
+                vec_buf[0, 1:2, :] += jnp.sum(grad, axis=0, keepdims=True)
+            d_attn[rows, :] = norm_pull(grad, hat, rstd, vecs[0:1, :])
 
         loop(tiles, body)
-
-    for m in range(4):
-        attention_back(m)
-        token_back(m)
-        if m == 1:
-            ffn_add(0, down_out)
-    ffn_add(1, up_out)
-
-    vec_buf[0, 0:2, :] = jnp.zeros((2, vec_buf.shape[2]), f32)
-
-    def token_end(b):
-        rows = rows_of(b, 128)
-        hat, rstd = standardise(x_ref[rows, :].astype(f32))
-        grad = d_attn[rows, :]
-        vec_buf[0, 0:1, :] += jnp.sum(grad * hat, axis=0, keepdims=True)
-        vec_buf[0, 1:2, :] += jnp.sum(grad, axis=0, keepdims=True)
-        d_attn[rows, :] = norm_pull(grad, hat, rstd, vecs[0:1, :])
-
-    loop(tiles, token_end)
-    stage_grad[...] = (d_attn[...] + spread_rows(place_ref[...], h_ends[...])).astype(bf16)
-    grad_swaps = [
-        remote(stage_grad, token_out.at[own_rows], s_tg.at[0], s_tg.at[1], Y),
-        remote(stage_grad, token_out.at[own_rows], s_tg.at[2], s_tg.at[3], C),
+        span = slice(token_rows * g, token_rows * (g + 1))
+        stage_grad[span, :] = (d_attn[span, :] + tn(place_ref[g], ends_back[g])).astype(bf16)
+
+    grad_swaps, keep_grads, vec_swaps = [], [], []
+    for g in range(2):
+        token_back(g)
+        sum_some(1)
+        if g == 0:
+            out_swaps[0].wait()
+            on = remote(block_out.at[far_rows], block_out.at[far_rows], s_on.at[0], s_on.at[1], C)
+        token_end(g)
+        if g == 0:
+            for j in range(1, 8):
+                vec_swaps.append(
+                    remote(vec_buf.at[0], vec_got.at[here], s_vs.at[j - 1], s_v.at[j - 1], PLANE[j - 1])
+                )
+            vec_got[here] = vec_buf[0]
+        ref = stage_grad.at[pl.ds(token_rows * g, token_rows)]
+        spot = token_out.at[far_rows if g else own_rows]
+        grad_swaps.append(remote(ref, spot, s_tg.at[2 * g], s_tg.at[2 * g + 1], C))
+        keep_grads.append(pltpu.make_async_copy(ref, spot, s_local.at[3 + g]))
+        keep_grads[g].start()
+        sum_some(1)
+    for swap in vec_swaps:
+        swap.wait()
+    vec_buf[1] = ((vec_got[0] + vec_got[1]) + (vec_got[2] + vec_got[3])) + (
+        (vec_got[4] + vec_got[5]) + (vec_got[6] + vec_got[7])
+    )
+    vec_swaps = [
+        remote(vec_buf.at[1], vec_got.at[8 + z], s_vs.at[6 + j], s_v.at[6 + j], Z[j]) for j in range(1, 4)
     ]
-    keep_grad = pltpu.make_async_copy(stage_grad, token_out.at[own_rows], s_local.at[2])
-    keep_grad.start()
-
-    def attn_grad(m):
-        made = tn(a_ref[...], d_qkv[m, :, 0:640])
-        o_e = nn(place_ref[...], qkv[m, :, 512:768]).astype(bf16)
-        outer = tn(attended_grad, o_e)
-        last = jnp.where(low, made[:, 512:640], outer[:, 0:128])
-        return jnp.concatenate([made[:, 0:512], last, outer[:, 128:256]], axis=1)
-
-    def pair_y(d):
-        return y if d == 0 else 1 - y
-
-    def pair_x(d):
-        return x if d == 0 else 1 - x
-
-    first, second = pl.ds(0, LATE), pl.ds(LATE, depth - LATE)
-
-    def half_rows(d):
-        return d * 8 * depth
-
-    def part(d, z_, x_, span):
-        start = half_rows(d) + (2 * z_ + x_) * depth + span.start
-        return attn_acc.at[pl.ds(pl.multiple_of(start, 16), span.size)]
-
-    whole = pl.ds(0, depth)
-    core_swaps = []
-    for d in (1, 0):
-        attn_send[d] = attn_grad(2 * pair_y(d) + (1 - c)).astype(bf16)
-        core_swaps.append(remote(attn_send.at[d], attn_core.at[d], s_exs.at[6 + d], s_core.at[d], C))
-    vec_swaps = [remote(vec_buf.at[0], vec_got.at[0], s_vs.at[0], s_v.at[0], C)]
-    for i, d in enumerate((1, 0)):
-        made = attn_grad(2 * pair_y(d) + c)
-        core_swaps[i].wait()
-        attn_acc[half_rows(d) : half_rows(d + 1), :] = (made + attn_core[d].astype(f32)).astype(bf16)
-        for j in range(4):
-            remote(part(d, zt[j], 1 - x, second), one_q.at[4 * d + j], s_send.at[2], s_1q.at[4 * d + j], X)
-        if d:
-            for e in (1, 0):
-                for j in range(4):
-                    remote(part(1, zt[j], pair_x(e), first), one_p.at[4 * e + j], s_send.at[2], s_1p.at[4 * e + j], Y)
-            ffn_end(0, down_out)
-            vec_swaps[0].wait()
-            vec_buf[1] = vec_buf[0] + vec_got[0]
-            vec_swaps.append(remote(vec_buf.at[1], vec_got.at[1], s_vs.at[1], s_v.at[1], Y))
-
-    def add(ref, got):
-        ref[...] = (ref[...].astype(f32) + got.astype(f32)).astype(bf16)
-
-    ffn_end(1, up_out)
-    vec_swaps[1].wait()
-    vec_buf[2] = vec_buf[1] + vec_got[1]
-    vec_swaps.append(remote(vec_buf.at[2], vec_got.at[2], s_vs.at[2], s_v.at[2], X))
-    for e in (1, 0):
-        for j in range(4):
-            i = 4 * e + j
-            arrived(one_p.at[i], s_1p.at[i], s_send.at[2])
-            spot = part(0, zt[j], pair_x(e), first)
-            add(spot, one_p[i])
-            if e:
-                remote(spot, two_p.at[j], s_send.at[2], s_2p.at[j], X)
-            arrived(one_q.at[i], s_1q.at[i], s_send.at[2])
-            spot = part(e, zt[j], x, second)
-            add(spot, one_q[i])
-            if e:
-                remote(spot, two_q.at[j], s_send.at[2], s_2q.at[j], Y)
-    vec_swaps[2].wait()
-    vec_buf[3] = vec_buf[2] + vec_got[2]
-    for j in range(1, 4):
-        vec_swaps.append(remote(vec_buf.at[3], vec_got.at[3 + z], s_vs.at[2 + j], s_v.at[2 + j], Z[j]))
-    vec_got[3 + z] = vec_buf[3]
-    for j in (2, 1, 3, 0):
-        arrived(two_p.at[j], s_2p.at[j], s_send.at[2])
-        add(part(0, zt[j], x, first), two_p[j])
-        arrived(two_q.at[j], s_2q.at[j], s_send.at[2])
-        add(part(0, zt[j], x, second), two_q[j])
-        spot = part(0, zt[j], x, whole)
-        if j:
-            remote(spot, three_a.at[j - 1], s_send.at[2], s_3.at[j - 1], Z[j])
-        else:
-            attn_out[...] = spot[...].astype(f32)
-    out_swaps[0].wait()
-    on = remote(block_out.at[far_rows], block_out.at[far_rows], s_boc.at[0], s_boc.at[1], C)
-    grad_swaps[0].wait()
-    on_grad = remote(token_out.at[far_rows], token_out.at[far_rows], s_boc.at[2], s_boc.at[3], C)
-    for j in range(1, 4):
-        arrived(three_a.at[j - 1], s_3.at[j - 1], s_send.at[2])
-    attn_out[...] = attn_out[...] + three_a[0].astype(f32) + three_a[1].astype(f32) + three_a[2].astype(f32)
-    for swap in vec_swaps[3:]:
+    vec_got[8 + z] = vec_buf[1]
+    sum_end(0)
+    sum_end(1)
+    for swap in vec_swaps:
         swap.wait()
-    vec_out[...] = (vec_got[3] + vec_got[4]) + (vec_got[5] + vec_got[6])
-    sent = attn_acc.at[pl.ds(0, 15 * depth)]
-    pltpu.make_async_copy(sent, sent, s_send.at[2]).wait()
+    vec_out[...] = (vec_got[8] + vec_got[9]) + (vec_got[10] + vec_got[11])
+    sum_end(2)
     out_swaps[1].wait()
-    grad_swaps[1].wait()
     on.wait()
-    on_grad.wait()
     keep_out.wait()
-    keep_grad.wait()
-
-
-def layer(slot_total, packed, small, classes, image_gain, image_bias, image_proj, tokens, ids):
-    width, depth, slots = packed.shape[2], packed.shape[1], classes.shape[0]
-    rows = tokens.shape[0] // 4
+    for swap in grad_swaps + keep_grads:
+        swap.wait()
+
+
+def layer(slot_total, w_qkv, w_out, up_own, down_own, norms, valid, classes, *rest):
+    depth, width = up_own.shape
+    slots = classes.shape[0]
+    rows = rest[3].shape[0] // 4
 
     def gather_sems():
         return [DMA((4,)), DMA((4,)), DMA((4,)), DMA((8,)), DMA((8,)), DMA((1,)), DMA((1,))]
@@ -690,18 +805,18 @@
         square,
         VMEM((4, 8 * slots, width), bf16),
         VMEM((4, 128, 128), bf16),
-        VMEM((rows, width), bf16),
-        VMEM((rows, width), bf16),
-        VMEM((4, rows, width), bf16),
+        VMEM((2 * rows, width), bf16),
+        VMEM((2 * rows, width), bf16),
+        VMEM((4, 2 * rows, width), bf16),
         VMEM((rows, width), f32),
         VMEM((rows, width), bf16),
         VMEM((4, rows, width), bf16),
         VMEM((rows, width), bf16),
         VMEM((slots, width), bf16),
         VMEM((8, width), f32),
-        VMEM((rows // 128, 128, 128), f32),
-        VMEM((slots, rows), bf16),
-        VMEM((slots, rows), f32),
+        VMEM((2 * rows // 128, 128, 128), f32),
+        VMEM((2, slots, rows), bf16),
+        VMEM((2, slots, rows), f32),
         VMEM((slots, width), f32),
         VMEM((4, slots, width), bf16),
         VMEM((4, slots, width), bf16),
@@ -711,55 +826,34 @@
         VMEM((4, slots, 8 * slots), f32),
         VMEM((8, 8 * slots), f32),
         VMEM((24, 128), f32),
-        VMEM((2, 24, 128), f32),
-        VMEM((9, 24, 128), f32),
-        VMEM((rows, width), f32),
+        VMEM((24, 128), f32),
+        VMEM((12, 24, 128), f32),
+        VMEM((2 * rows, width), f32),
         VMEM((4, rows, 640), bf16),
         VMEM((width, width), bf16),
         VMEM((width, width), bf16),
-        VMEM((2, 4, depth, width), bf16),
-        VMEM((2, 3, depth, width), bf16),
-        VMEM((2, width, width), bf16),
-        VMEM((2 * width, width), bf16),
-        VMEM((2, width, width), bf16),
-        VMEM((8, LATE, width), bf16),
-        VMEM((8, depth - LATE, width), bf16),
-        VMEM((4, LATE, width), bf16),
-        VMEM((4, depth - LATE, width), bf16),
-        VMEM((3, depth, width), bf16),
-        VMEM((4, 8, width), f32),
-        VMEM((7, 8, width), f32),
-        VMEM((rows, width), bf16),
-        VMEM((8, 128), f32),
+        VMEM((width, width), bf16),
+        VMEM((3, 4, depth, width), bf16),
+        VMEM((3, 3, depth, width), bf16),
+        VMEM((width, width), bf16),
+        VMEM((width, width), bf16),
+        VMEM((2, slots, width), bf16),
+        VMEM((2, 8, width), f32),
+        VMEM((12, 8, width), f32),
+        VMEM((2 * rows, width), bf16),
+        VMEM((depth, width), bf16),
+        VMEM((16, 128), bf16),
+        VMEM((slots, 256), bf16),
     ]
-    for _ in range(5):
+    for _ in range(4):
         scratch += gather_sems()
-    scratch += [
-        DMA((3,)),
-        DMA((4,)),
-        DMA((4,)),
-        DMA((3,)),
-        DMA((3,)),
-        DMA((3,)),
-        DMA((7,)),
-        DMA((7,)),
-        DMA((2, 4)),
-        DMA((2, 3)),
-        DMA((2,)),
-        DMA((8,)),
-        DMA((8,)),
-        DMA((4,)),
-        DMA((4,)),
-        DMA((3,)),
-        DMA((6,)),
-        DMA((6,)),
-        DMA((4,)),
-        DMA((8,)),
-    ]
+    scratch += [DMA((2,)), DMA((2,)), DMA((1,)), DMA((1,)), DMA((1,)), DMA((3, 2)), DMA((3, 2)), DMA((3, 2)), DMA((3, 2))]
+    scratch += [DMA((6,)), DMA((4,)), DMA((2,)), DMA((3,)), DMA((3,)), DMA((3,)), DMA((1,)), DMA((10,)), DMA((10,))]
+    scratch += [DMA((3, 4)), DMA((3, 3)), DMA((1,)), DMA((10,)), DMA((10,)), DMA((4,)), DMA((8,))]
     return pl.pallas_call(
         functools.partial(layer_kernel, slot_total),
         out_shape=[
-            jax.ShapeDtypeStruct((8, 128), f32),
+            jax.ShapeDtypeStruct((1, 1), f32),
             jax.ShapeDtypeStruct((4 * rows, width), bf16),
             jax.ShapeDtypeStruct((4 * rows, width), bf16),
             jax.ShapeDtypeStruct((depth, width), f32),
@@ -767,7 +861,7 @@
             jax.ShapeDtypeStruct((depth, width), f32),
             jax.ShapeDtypeStruct((8, width), f32),
         ],
-        in_specs=[here] * 6 + [there, here],
+        in_specs=[here] * 10 + [there, here],
         out_specs=[here, there, there, here, here, here, here],
         scratch_shapes=scratch,
         compiler_params=pltpu.CompilerParams(
@@ -775,7 +869,70 @@
         ),
         cost_estimate=pl.CostEstimate(flops=30 * 10**9, bytes_accessed=40 * 10**6, transcendentals=10**7),
         name="layer",
-    )(packed, small, classes, image_gain, image_bias, image_proj, tokens, ids)
+    )(w_qkv, w_out, up_own, down_own, norms, valid, classes, *rest)
+
+
+def finish_kernel(block_in, token_in, attn_in, up_in, down_in, block_out, token_out, qkv_out, out_out, up_out, down_out, narrow, wide, held, sems):
+    parts = narrow.shape[0]
+    rows = narrow.shape[1]
+    loads, saves, keeps = [], [], []
+    for i in range(parts):
+        load = pltpu.make_async_copy(block_in.at[pl.ds(i * rows, rows)], held.at[i], sems.at[1 + 2 * parts + i])
+        load.start()
+        save = pltpu.make_async_copy(held.at[i], block_out.at[pl.ds(i * rows, rows)], sems.at[1 + 3 * parts + i])
+        keeps.append((load, save))
+    for i in range(parts):
+        loads.append(pltpu.make_async_copy(token_in.at[pl.ds(i * rows, rows)], narrow.at[i], sems.at[1 + i]))
+        loads[i].start()
+        saves.append(pltpu.make_async_copy(wide.at[i], token_out.at[pl.ds(i * rows, rows)], sems.at[1 + parts + i]))
+    up_out[...] = up_in[...]
+    down_out[...] = down_in[...]
+    for i, (pair, single) in enumerate(((0, 384), (128, 512), (256, 448))):
+        qkv_out[i] = jnp.concatenate([attn_in[:, pair : pair + 128], attn_in[:, single : single + 64]], axis=1)
+    depth = attn_in.shape[0]
+    row = lax.broadcasted_iota(jnp.int32, (depth, depth), 0)
+    eye = (row == lax.broadcasted_iota(jnp.int32, (depth, depth), 1)).astype(f32).astype(bf16)
+    mixed = jnp.concatenate([attn_in[:, 640:768], attn_in[:, 576:640]], axis=1)
+    out_out[...] = sum(tn(part, eye) for part in split_three(mixed))
+    for i in range(parts):
+        loads[i].wait()
+        wide[i] = narrow[i].astype(f32)
+        saves[i].start()
+    for load, save in keeps:
+        load.wait()
+        save.start()
+    for save in saves:
+        save.wait()
+    for load, save in keeps:
+        save.wait()
+
+
+def finish(block_out, token_grad, own_attn, own_up, own_down):
+    rows, width = token_grad.shape
+    depth = own_up.shape[0]
+    parts = 4
+    here, there = pl.BlockSpec(memory_space=VMEM), pl.BlockSpec(memory_space=pltpu.HBM)
+    return pl.pallas_call(
+        finish_kernel,
+        out_shape=[
+            jax.ShapeDtypeStruct(block_out.shape, bf16),
+            jax.ShapeDtypeStruct((rows, width), f32),
+            jax.ShapeDtypeStruct((3, depth, 192), f32),
+            jax.ShapeDtypeStruct((192, depth), f32),
+            jax.ShapeDtypeStruct((depth, width), f32),
+            jax.ShapeDtypeStruct((depth, width), f32),
+        ],
+        in_specs=[there, there, here, here, here],
+        out_specs=[there, there, here, here, here, here],
+        scratch_shapes=[
+            VMEM((parts, rows // parts, width), bf16),
+            VMEM((parts, rows // parts, width), f32),
+            VMEM((parts, rows // parts, width), bf16),
+            DMA((1 + 4 * parts,)),
+        ],
+        compiler_params=pltpu.CompilerParams(vmem_limit_bytes=63 * 2**20),
+        name="finish",
+    )(block_out, token_grad, own_attn, own_up, own_down)
 
 
 def on_kernel(
@@ -797,51 +954,29 @@
 ):
     dp_rank = lax.axis_index("dp")
     depth, slots = w_up.shape[0], slot_valid.shape[0]
-    out_t = w_out.T
-    query, key, value = w_qkv[0], w_qkv[1], w_qkv[2]
-    attn = jnp.concatenate(
-        [
-            query[:, :128],
-            key[:, :128],
-            value[:, :128],
-            query[:, 128:],
-            value[:, 128:],
-            key[:, 128:],
-            out_t[:, 128:],
-            out_t[:, :128],
-        ],
-        axis=1,
-    )
-    packed = jnp.stack([attn, w_up, w_down.T])
-    norms = jnp.stack([ln1_gain, ln1_bias, ln2_gain, ln2_bias])
-    norms = jnp.where(
-        (jnp.arange(4) == lax.rem(dp_rank, 4))[None, :, None], norms[:, None, :], jnp.zeros((), bf16)
-    ).reshape(12, 128)
-    valid = jnp.where(
-        (jnp.arange(2) == lax.rem(dp_rank, 2))[:, None], slot_valid.astype(bf16)[None, :], jnp.zeros((), bf16)
-    ).reshape(1, 128)
-    small = jnp.concatenate([norms, valid, jnp.zeros((3, 128), bf16)], axis=0)
     loss, block_out, token_grad, own_attn, own_up, own_down, vectors = layer(
         slots * 32,
-        packed,
-        small,
+        w_qkv,
+        w_out,
+        w_up,
+        w_down.T,
+        jnp.stack([ln1_gain, ln1_bias, ln2_gain, ln2_bias]),
+        slot_valid.reshape(1, slots),
         class_tokens,
-        image_gain[None],
-        image_bias[None],
+        image_gain,
+        image_bias,
         image_proj,
         tokens,
         segment_ids.reshape(4, 4, 128),
     )
-    pick_cols = lambda *spans: jnp.concatenate([own_attn[:, a:b] for a, b in spans], axis=1)
-    qkv_grad = jnp.stack(
-        [pick_cols((0, 128), (384, 448)), pick_cols((128, 256), (512, 576)), pick_cols((256, 384), (448, 512))]
+    block_out, token_grad, qkv_grad, out_grad, own_up, own_down = finish(
+        block_out, token_grad, own_attn, own_up, own_down
     )
-    out_grad = pick_cols((640, 768), (576, 640)).T
     vectors = lax.dynamic_slice_in_dim(vectors, dp_rank * depth, depth, 1)
     return (
-        loss[0, 0],
+        loss.reshape(()),
         block_out,
-        token_grad.astype(f32),
+        token_grad,
         vectors[0],
         vectors[1],
         qkv_grad,

time: 217 us -> 188 us (0.87)
  Pallas kernels: 195 us -> 183 us
  local copies, waits for them, and re-layouts: 11.1 us -> 1.31 us
  other arithmetic: 10 us -> 1.28 us
    pallas_call x1, Pallas kernels: 195 us -> 175 us  [layer(): pl.pallas_call(functools.partial(layer_kernel, slot_total), out_shape=[ja...]
    pallas_call x0 -> x1, Pallas kernels: none -> 8.06 us  [finish(): pl.pallas_call(finish_kernel, out_shape=[jax.ShapeDtypeStruct(block_out.s...]
    convert_element_type x2 -> x0, other arithmetic: 5.88 us -> none  [the longest x1 5.23 us: on_kernel(): token_grad.astype(f32)]
    unnamed x13 -> x0, local copies, waits for them, and re-layouts: 4.74 us -> none
    broadcast_in_dim x3 -> x0, local copies, waits for them, and re-layouts: 2.54 us -> none  [the longest x1 1.27 us: on_kernel(): image_gain[None]]
where the time goes in v3:
time: 188 us
  Pallas kernels  183 us (97%)
  between operations  2.41 us (1%)
    pallas_call x1, Pallas kernels, layer(): pl.pallas_call(functools.partial(layer_kernel, slot_total), out_shape=[ja...  175 us
    pallas_call x1, Pallas kernels, finish(): pl.pallas_call(finish_kernel, out_shape=[jax.ShapeDtypeStruct(block_out.s...  8.06 us

profile of v3, /device:TPU:0, one launch (start us, length us, event | category | flops | bytes accessed | tf_op | source)
XLA Modules:
  0.0 188.1 jit_solution(2512541064804858019)
XLA Ops:
  0.6 1.3 pad_maximum_fusion.refs_4_
  1.9 175.1 %layer.1 = (f32[1,1]{1,0:T(1,128)}, bf16[2048,768]{1,0:T(8,128)(2,1)}, bf16[2048,768]{1,0:T(8,128)(2,1)}, f32[96,768]{1,0:T(8,128)}, f32[96,768]{1,0:T(8,128)}, /*index=5*/f32[96,768]{1,0:T(8,128)}, f32[8,768]{1,0:T(8,128)}) custom-call(bf16[3,96,192]{2,1,0:T(8,128)(2,1)} %refs_0_.1, bf16[192,96]{1,0:T(8,128)(2,1)} %refs_1_.1, bf16[96,768]{1,0:T(8,128)(2,1)} %refs_2_.1, ...), custom_call_target="tpu_custom_call" | custom-call | flops 30000001024 | bytes 40000000 | tf_op jit(solution)/shard_map/layer/pallas_call | solution.py:853
  177.0 0.8 constant_dynamic-slice_fusion
  177.8 0.5 slice_bitcast_fusion
  178.3 8.1 %finish.1 = (bf16[2048,768]{1,0:T(8,128)(2,1)}, f32[2048,768]{1,0:T(8,128)}, f32[3,96,192]{2,1,0:T(8,128)}, f32[192,96]{1,0:T(8,128)}, f32[96,768]{1,0:T(8,128)}, /*index=5*/f32[96,768]{1,0:T(8,128)}) custom-call(bf16[2048,768]{1,0:T(8,128)(2,1)} %get-tuple-element.25.block_in, bf16[2048,768]{1,0:T(8,128)(2,1)} %get-tuple-element.26.token_in, ...), custom_call_target="tpu_custom_call" | custom-call | tf_op jit(solution)/shard_map/finish/pallas_call | solution.py:915

commit v4 on v3

--- a/solution.py
+++ b/solution.py
@@ -51,6 +51,7 @@
 MESH = pl.DeviceIdType.MESH
 VMEM, DMA = pltpu.VMEM, pltpu.SemaphoreType.DMA
 CUT = 48
+WINDOW = 3
 
 
 def loop(count, body):
@@ -87,10 +88,10 @@
     (mask_ref, place_ref, member_ref, h_ends, ends_two, ends_grad, u_ends, g_all, s_all, weight_ref, valid_ref) = refs[33:44]
     (sum_own, sum_buf, sum_got, d_attn, d_far) = refs[44:49]
     (grad_down, grad_up, grad_attn, step_x, step_z, attn_send, attn_core, ends_back) = refs[49:57]
-    (vec_buf, vec_got, stage_grad, attn_own, small_own, far_mix) = refs[57:63]
-    gsems = refs[63:91]
-    isems = refs[91:100]
-    (s_local, s_bo, s_on, s_send, s_a2, s_dm, s_dh, s_sum, s_sums, s_x, s_z, s_core, s_v, s_vs, s_tg, s_exs) = refs[100:116]
+    (vec_buf, vec_pack, vec_got, stage_grad, attn_own, small_own, far_mix) = refs[57:64]
+    gsems = refs[64:92]
+    isems = refs[92:101]
+    (s_local, s_bo, s_on, s_send, s_a2, s_dm, s_dh, s_sum, s_sums, s_x, s_z, s_core, s_v, s_vs, s_tg, s_exs) = refs[101:117]
 
     dp = lax.axis_index("dp")
     mp = lax.axis_index("mp")
@@ -593,41 +594,25 @@
     ends_grad[mp] = branch_grad
     swaps = [remote(ends_grad.at[mp], ends_grad.at[mp], s_exs.at[2 + j], s_dm.at[j - 1], G[j]) for j in range(1, 4)]
 
-    own_rows = rows_of(mp, token_rows)
-    far_rows = rows_of(ym, token_rows)
-    out_swaps = [
-        remote(stage_out, block_out.at[own_rows], s_bo.at[0], s_bo.at[1], Y),
-        remote(stage_out, block_out.at[own_rows], s_bo.at[2], s_bo.at[3], C),
-    ]
-    keep_out = pltpu.make_async_copy(stage_out, block_out.at[own_rows], s_local.at[2])
-    keep_out.start()
-
-    two_grad = jnp.zeros_like(pooled)
-    for m in range(4):
+    def two_part(m):
         upper_grad = (nn(branch_grad, w_down[m]) * slope_of(u_ends[m])).astype(bf16)
-        two_grad = two_grad + nt(upper_grad, w_up[m])
-    hat_two, rstd_two = standardise(h_ends[...])
-    vec_buf[0] = jnp.zeros_like(vec_buf[0])
-    vec_buf[0, 2:3, :] = jnp.sum(two_grad * hat_two, axis=0, keepdims=True)
-    vec_buf[0, 3:4, :] = jnp.sum(two_grad, axis=0, keepdims=True)
-    hidden_grad = pooled_grad + norm_pull(two_grad, hat_two, rstd_two, vecs[2:3, :])
-    ends_back[0] = hidden_grad.astype(bf16)
-    back_swap = remote(ends_back.at[0], ends_back.at[1], s_exs.at[6], s_dh.at[0], Y)
-
-    for swap in swaps:
-        swap.wait()
-    group_grad = ends_grad[...].reshape(4 * end_count, -1)
-    upper_grad = (nn(group_grad, w_down[mp]) * s_all[...]).astype(bf16)
-    grad_down[...] = tn(group_grad, g_all[...]).astype(bf16)
+        return nt(upper_grad, w_up[m])
+
+    two_grad = two_part(0) + two_part(1)
 
     def block(z_, x_):
         return pl.ds(pl.multiple_of((2 * z_ + x_) * depth, 16), depth)
 
     grads, outs = [grad_down, grad_up, grad_attn], [down_out, up_out, attn_out]
 
-    def sum_start(k):
-        for j in (2, 1, 3, 0):
-            remote(grads[k].at[block(zt[j], 1 - x)], step_x.at[k, j], s_send.at[k], s_x.at[k, j], X)
+    order = [(k, j) for k in range(3) for j in (2, 1, 3, 0)]
+    sent, added = iter(order), iter(order)
+
+    def sum_start(count):
+        for _ in range(count):
+            k, j = next(sent, (None, None))
+            if k is not None:
+                remote(grads[k].at[block(zt[j], 1 - x)], step_x.at[k, j], s_send.at[k], s_x.at[k, j], X)
 
     def sum_add(k, j):
         arrived(step_x.at[k, j], s_x.at[k, j], s_send.at[k])
@@ -646,9 +631,28 @@
         sent = grads[k].at[pl.ds(0, 7 * depth)]
         pltpu.make_async_copy(sent, sent, s_send.at[k]).wait()
 
-    sum_start(0)
+    def sum_some(count):
+        for _ in range(count):
+            sum_start(1)
+            sum_add(*next(added))
+
+    for swap in swaps:
+        swap.wait()
+    group_grad = ends_grad[...].reshape(4 * end_count, -1)
+    upper_grad = (nn(group_grad, w_down[mp]) * s_all[...]).astype(bf16)
+    grad_down[...] = tn(group_grad, g_all[...]).astype(bf16)
+
+    sum_start(WINDOW)
     grad_up[...] = tn(ends_two[...].reshape(4 * end_count, -1), upper_grad).astype(bf16)
-    sum_start(1)
+
+    two_grad = two_grad + two_part(2) + two_part(3)
+    hat_two, rstd_two = standardise(h_ends[...])
+    vec_buf[...] = jnp.zeros_like(vec_buf)
+    vec_buf[2:3, :] = jnp.sum(two_grad * hat_two, axis=0, keepdims=True)
+    vec_buf[3:4, :] = jnp.sum(two_grad, axis=0, keepdims=True)
+    hidden_grad = pooled_grad + norm_pull(two_grad, hat_two, rstd_two, vecs[2:3, :])
+    ends_back[0] = hidden_grad.astype(bf16)
+    back_swap = remote(ends_back.at[0], ends_back.at[1], s_exs.at[6], s_dh.at[0], Y)
 
     def attention_back(m, g, mix=False):
         place = place_ref[g]
@@ -705,18 +709,19 @@
         last = jnp.where(low, made(512, 640), outer[:, 0:128])
         return jnp.concatenate([made(0, 512), last, outer[:, 128:256]], axis=1)
 
-    steps = iter([(k, j) for k in range(3) for j in range(4)])
-
-    def sum_some(count):
-        for _ in range(count):
-            k, i = next(steps)
-            sum_add(k, (2, 1, 3, 0)[i])
-
     back_swap.wait()
+    own_rows = rows_of(mp, token_rows)
+    far_rows = rows_of(ym, token_rows)
+    out_swaps = [
+        remote(stage_out, block_out.at[own_rows], s_bo.at[0], s_bo.at[1], Y),
+        remote(stage_out, block_out.at[own_rows], s_bo.at[2], s_bo.at[3], C),
+    ]
+    keep_out = pltpu.make_async_copy(stage_out, block_out.at[own_rows], s_local.at[2])
+    keep_out.start()
+
     m = 2 * y + (1 - c)
     attention_back(m, 0, True)
     attention_back(m, 1, True)
-    sum_some(1)
     attn_send[...] = attn_grad(m).astype(bf16)
     core_swap = remote(attn_send, attn_core, s_exs.at[7], s_core.at[0], C)
     sum_some(1)
@@ -727,60 +732,70 @@
     made = attn_grad(m)
     core_swap.wait()
     grad_attn[...] = (made + attn_core[...].astype(f32)).astype(bf16)
-    sum_start(2)
     sum_some(1)
     for i in range(2):
         for g in range(2):
             attention_back(2 * (1 - y) + i, g)
-            sum_some(1)
+    sum_some(1)
+
     def token_end(g):
         def body(b):
             rows = rows_of(tiles * g + b, 128)
             hat, rstd = standardise(x_ref[rows, :].astype(f32))
             grad = d_attn[rows, :]
             if g == 0:
-                vec_buf[0, 0:1, :] += jnp.sum(grad * hat, axis=0, keepdims=True)
-                vec_buf[0, 1:2, :] += jnp.sum(grad, axis=0, keepdims=True)
+                vec_buf[0:1, :] += jnp.sum(grad * hat, axis=0, keepdims=True)
+                vec_buf[1:2, :] += jnp.sum(grad, axis=0, keepdims=True)
             d_attn[rows, :] = norm_pull(grad, hat, rstd, vecs[0:1, :])
 
         loop(tiles, body)
         span = slice(token_rows * g, token_rows * (g + 1))
         stage_grad[span, :] = (d_attn[span, :] + tn(place_ref[g], ends_back[g])).astype(bf16)
 
-    grad_swaps, keep_grads, vec_swaps = [], [], []
+    grad_swaps, keep_grads = [], []
+    out_swaps[0].wait()
+    on = remote(block_out.at[far_rows], block_out.at[far_rows], s_on.at[0], s_on.at[1], C)
     for g in range(2):
         token_back(g)
-        sum_some(1)
-        if g == 0:
-            out_swaps[0].wait()
-            on = remote(block_out.at[far_rows], block_out.at[far_rows], s_on.at[0], s_on.at[1], C)
+        sum_some(g)
         token_end(g)
         if g == 0:
-            for j in range(1, 8):
-                vec_swaps.append(
-                    remote(vec_buf.at[0], vec_got.at[here], s_vs.at[j - 1], s_v.at[j - 1], PLANE[j - 1])
-                )
-            vec_got[here] = vec_buf[0]
+            for v in range(4):
+                for t in range(6):
+                    vec_pack[0, 6 * v + t : 6 * v + t + 1, :] = vec_buf[v : v + 1, 128 * t : 128 * (t + 1)]
+            core_vec = remote(vec_pack.at[0], vec_got.at[0], s_vs.at[0], s_v.at[0], C)
         ref = stage_grad.at[pl.ds(token_rows * g, token_rows)]
         spot = token_out.at[far_rows if g else own_rows]
         grad_swaps.append(remote(ref, spot, s_tg.at[2 * g], s_tg.at[2 * g + 1], C))
         keep_grads.append(pltpu.make_async_copy(ref, spot, s_local.at[3 + g]))
         keep_grads[g].start()
-        sum_some(1)
+        if g == 0:
+            sum_some(1)
+    core_vec.wait()
+    vec_pack[1] = vec_pack[0] + vec_got[0]
+    across = [X, Y, (2 * z + (1 - x), ym)]
+    vec_swaps = [
+        remote(vec_pack.at[1], vec_got.at[1 + 2 * y + x], s_vs.at[1 + j], s_v.at[1 + j], across[j]) for j in range(3)
+    ]
+    vec_got[1 + 2 * y + x] = vec_pack[1]
+    sum_some(1)
     for swap in vec_swaps:
         swap.wait()
-    vec_buf[1] = ((vec_got[0] + vec_got[1]) + (vec_got[2] + vec_got[3])) + (
-        (vec_got[4] + vec_got[5]) + (vec_got[6] + vec_got[7])
-    )
+    vec_pack[2] = (vec_got[1] + vec_got[2]) + (vec_got[3] + vec_got[4])
     vec_swaps = [
-        remote(vec_buf.at[1], vec_got.at[8 + z], s_vs.at[6 + j], s_v.at[6 + j], Z[j]) for j in range(1, 4)
+        remote(vec_pack.at[2], vec_got.at[5 + z], s_vs.at[3 + j], s_v.at[3 + j], Z[j]) for j in range(1, 4)
     ]
-    vec_got[8 + z] = vec_buf[1]
-    sum_end(0)
-    sum_end(1)
+    vec_got[5 + z] = vec_pack[2]
+    sum_some(1)
     for swap in vec_swaps:
         swap.wait()
-    vec_out[...] = (vec_got[8] + vec_got[9]) + (vec_got[10] + vec_got[11])
+    total = (vec_got[5] + vec_got[6]) + (vec_got[7] + vec_got[8])
+    for v in range(4):
+        for t in range(6):
+            vec_out[v : v + 1, 128 * t : 128 * (t + 1)] = total[6 * v + t : 6 * v + t + 1, :]
+    sum_end(0)
+    sum_some(4)
+    sum_end(1)
     sum_end(2)
     out_swaps[1].wait()
     on.wait()
@@ -838,8 +853,9 @@
         VMEM((width, width), bf16),
         VMEM((width, width), bf16),
         VMEM((2, slots, width), bf16),
-        VMEM((2, 8, width), f32),
-        VMEM((12, 8, width), f32),
+        VMEM((8, width), f32),
+        VMEM((3, 24, 128), f32),
+        VMEM((9, 24, 128), f32),
         VMEM((2 * rows, width), bf16),
         VMEM((depth, width), bf16),
         VMEM((16, 128), bf16),
@@ -859,7 +875,7 @@
             jax.ShapeDtypeStruct((depth, width), f32),
             jax.ShapeDtypeStruct((depth, width), f32),
             jax.ShapeDtypeStruct((depth, width), f32),
-            jax.ShapeDtypeStruct((8, width), f32),
+            jax.ShapeDtypeStruct((4, width), f32),
         ],
         in_specs=[here] * 10 + [there, here],
         out_specs=[here, there, there, here, here, here, here],
@@ -872,38 +888,49 @@
     )(w_qkv, w_out, up_own, down_own, norms, valid, classes, *rest)
 
 
-def finish_kernel(block_in, token_in, attn_in, up_in, down_in, block_out, token_out, qkv_out, out_out, up_out, down_out, narrow, wide, held, sems):
-    parts = narrow.shape[0]
-    rows = narrow.shape[1]
-    loads, saves, keeps = [], [], []
+def finish_kernel(*refs):
+    (block_in, token_in, attn_in, up_in, down_in) = refs[:5]
+    (block_out, token_out, qkv_out, out_out, up_out, down_out) = refs[5:11]
+    (narrow, wide, held, mats, qkv, out, sems) = refs[11:]
+    parts, rows = narrow.shape[0], narrow.shape[1]
+    count = iter(range(sems.shape[0]))
+
+    def copy(src, dst):
+        return pltpu.make_async_copy(src, dst, sems.at[next(count)])
+
+    mat_loads = [copy(ref, mats.at[i]) for i, ref in enumerate((attn_in, up_in, down_in))]
+    loads, saves, keep_loads, keep_saves = [], [], [], []
     for i in range(parts):
-        load = pltpu.make_async_copy(block_in.at[pl.ds(i * rows, rows)], held.at[i], sems.at[1 + 2 * parts + i])
+        span = pl.ds(i * rows, rows)
+        loads.append(copy(token_in.at[span], narrow.at[i]))
+        saves.append(copy(wide.at[i], token_out.at[span]))
+        keep_loads.append(copy(block_in.at[span], held.at[i]))
+        keep_saves.append(copy(held.at[i], block_out.at[span]))
+    for load in mat_loads + loads + keep_loads:
         load.start()
-        save = pltpu.make_async_copy(held.at[i], block_out.at[pl.ds(i * rows, rows)], sems.at[1 + 3 * parts + i])
-        keeps.append((load, save))
-    for i in range(parts):
-        loads.append(pltpu.make_async_copy(token_in.at[pl.ds(i * rows, rows)], narrow.at[i], sems.at[1 + i]))
-        loads[i].start()
-        saves.append(pltpu.make_async_copy(wide.at[i], token_out.at[pl.ds(i * rows, rows)], sems.at[1 + parts + i]))
-    up_out[...] = up_in[...]
-    down_out[...] = down_in[...]
+    for load in mat_loads:
+        load.wait()
+    mat_saves = [copy(mats.at[1], up_out), copy(mats.at[2], down_out)]
+    for save in mat_saves:
+        save.start()
     for i, (pair, single) in enumerate(((0, 384), (128, 512), (256, 448))):
-        qkv_out[i] = jnp.concatenate([attn_in[:, pair : pair + 128], attn_in[:, single : single + 64]], axis=1)
-    depth = attn_in.shape[0]
+        qkv[i] = jnp.concatenate([mats[0, :, pair : pair + 128], mats[0, :, single : single + 64]], axis=1)
+    depth = mats.shape[1]
     row = lax.broadcasted_iota(jnp.int32, (depth, depth), 0)
     eye = (row == lax.broadcasted_iota(jnp.int32, (depth, depth), 1)).astype(f32).astype(bf16)
-    mixed = jnp.concatenate([attn_in[:, 640:768], attn_in[:, 576:640]], axis=1)
-    out_out[...] = sum(tn(part, eye) for part in split_three(mixed))
+    mixed = jnp.concatenate([mats[0, :, 640:768], mats[0, :, 576:640]], axis=1)
+    out[...] = sum(tn(part, eye) for part in split_three(mixed))
+    mat_saves += [copy(qkv, qkv_out), copy(out, out_out)]
+    for save in mat_saves[2:]:
+        save.start()
     for i in range(parts):
         loads[i].wait()
         wide[i] = narrow[i].astype(f32)
         saves[i].start()
-    for load, save in keeps:
+    for load, save in zip(keep_loads, keep_saves):
         load.wait()
         save.start()
-    for save in saves:
-        save.wait()
-    for load, save in keeps:
+    for save in mat_saves + saves + keep_saves:
         save.wait()
 
 
@@ -911,7 +938,7 @@
     rows, width = token_grad.shape
     depth = own_up.shape[0]
     parts = 4
-    here, there = pl.BlockSpec(memory_space=VMEM), pl.BlockSpec(memory_space=pltpu.HBM)
+    there = pl.BlockSpec(memory_space=pltpu.HBM)
     return pl.pallas_call(
         finish_kernel,
         out_shape=[
@@ -922,13 +949,16 @@
             jax.ShapeDtypeStruct((depth, width), f32),
             jax.ShapeDtypeStruct((depth, width), f32),
         ],
-        in_specs=[there, there, here, here, here],
-        out_specs=[there, there, here, here, here, here],
+        in_specs=[there] * 5,
+        out_specs=[there] * 6,
         scratch_shapes=[
             VMEM((parts, rows // parts, width), bf16),
             VMEM((parts, rows // parts, width), f32),
             VMEM((parts, rows // parts, width), bf16),
-            DMA((1 + 4 * parts,)),
+            VMEM((3, depth, width), f32),
+            VMEM((3, depth, 192), f32),
+            VMEM((192, depth), f32),
+            DMA((7 + 4 * parts,)),
         ],
         compiler_params=pltpu.CompilerParams(vmem_limit_bytes=63 * 2**20),
         name="finish",

time: 188 us -> 181 us (0.963)
  Pallas kernels: 183 us -> 176 us
    pallas_call x1, Pallas kernels: 175 us -> 169 us  [layer(): pl.pallas_call(functools.partial(layer_kernel, slot_total), out_shape=[ja...]
where the time goes in v4:
time: 181 us
  Pallas kernels  176 us (97%)
  between operations  2.4 us (1%)
    pallas_call x1, Pallas kernels, layer(): pl.pallas_call(functools.partial(layer_kernel, slot_total), out_shape=[ja...  169 us
    pallas_call x1, Pallas kernels, finish(): pl.pallas_call(finish_kernel, out_shape=[jax.ShapeDtypeStruct(block_out.s...  6.54 us

profile of v4, /device:TPU:0, one launch (start us, length us, event | category | flops | bytes accessed | tf_op | source)
XLA Modules:
  0.0 180.9 jit_solution(8820696283795493493)
XLA Ops:
  0.6 1.3 pad_maximum_fusion.refs_4_
  1.9 169.4 %layer.1 = (f32[1,1]{1,0:T(1,128)}, bf16[2048,768]{1,0:T(8,128)(2,1)}, bf16[2048,768]{1,0:T(8,128)(2,1)}, f32[96,768]{1,0:T(8,128)}, f32[96,768]{1,0:T(8,128)}, /*index=5*/f32[96,768]{1,0:T(8,128)}, f32[4,768]{1,0:T(4,128)}) custom-call(bf16[3,96,192]{2,1,0:T(8,128)(2,1)} %refs_0_.1, bf16[192,96]{1,0:T(8,128)(2,1)} %refs_1_.1, bf16[96,768]{1,0:T(8,128)(2,1)} %refs_2_.1, ...), custom_call_target="tpu_custom_call" | custom-call | flops 30000001024 | bytes 40000000 | tf_op jit(solution)/shard_map/layer/pallas_call | solution.py:869
  171.3 0.8 constant_dynamic-slice_fusion
  172.1 0.5 slice_bitcast_fusion
  172.6 6.5 %finish.1 = (bf16[2048,768]{1,0:T(8,128)(2,1)}, f32[2048,768]{1,0:T(8,128)}, f32[3,96,192]{2,1,0:T(8,128)}, f32[192,96]{1,0:T(8,128)}, f32[96,768]{1,0:T(8,128)}, /*index=5*/f32[96,768]{1,0:T(8,128)}) custom-call(bf16[2048,768]{1,0:T(8,128)(2,1)} %get-tuple-element.25.refs_0_, bf16[2048,768]{1,0:T(8,128)(2,1)} %get-tuple-element.26.refs_1_, ...), custom_call_target="tpu_custom_call" | custom-call | tf_op jit(solution)/shard_map/finish/pallas_call | solution.py:942

commit v5 on v4

--- a/solution.py
+++ b/solution.py
@@ -473,14 +473,14 @@
     def slope_of(upper):
         return half_erf(upper) + upper * jnp.exp(-0.5 * upper * upper) * (1.0 / (2.0 * jnp.pi) ** 0.5)
 
-    def group_up():
+    def group_up(start):
         def body(i):
-            upper = nn(ends_two[i], w_up[mp])
-            rows = rows_of(i, end_count)
+            upper = nn(ends_two[start + i], w_up[mp])
+            rows = rows_of(start + i, end_count)
             g_all[rows, :] = (upper * half_erf(upper)).astype(bf16)
             s_all[rows, :] = slope_of(upper)
 
-        loop(4, body)
+        loop(2, body)
 
     def full_down(b):
         rows = slice(256 * b, 256 * (b + 1))
@@ -513,15 +513,11 @@
     second_norm()
     swaps = [remote(ends_two.at[mp], ends_two.at[mp], s_exs.at[j - 1], s_a2.at[j - 1], G[j]) for j in range(1, 4)]
     run("U4")
-    blend(
-        ("D3",),
-        [functools.partial(full_up, m) for m in range(4)] + [functools.partial(project, m, 1) for m in range(4)],
-    )
+    blend(("D3",), [functools.partial(full_up, m) for m in range(4)])
     loop(4, ends_up)
     run("I4")
     for swap in swaps:
         swap.wait()
-    group_up()
     run("D4")
 
     pooled = h_ends[...]
@@ -565,7 +561,7 @@
 
     swaps = [remote(sum_own, sum_got.at[here], s_sums.at[j - 1], s_sum.at[j - 1], PLANE[j - 1]) for j in range(1, 8)]
     sum_got[here] = sum_own[...]
-    full_down(0)
+    group_up(0)
     for swap in swaps:
         swap.wait()
     sum_buf[...] = ((sum_got[0] + sum_got[1]) + (sum_got[2] + sum_got[3])) + (
@@ -573,7 +569,7 @@
     )
     swaps = [remote(sum_buf, sum_got.at[8 + z], s_sums.at[6 + j], s_sum.at[6 + j], Z[j]) for j in range(1, 4)]
     sum_got[8 + z] = sum_buf[...]
-    full_down(1)
+    group_up(2)
     for swap in swaps:
         swap.wait()
     sums = (sum_got[8] + sum_got[9]) + (sum_got[10] + sum_got[11])
@@ -709,7 +705,10 @@
         last = jnp.where(low, made(512, 640), outer[:, 0:128])
         return jnp.concatenate([made(0, 512), last, outer[:, 128:256]], axis=1)
 
+    full_down(0)
+    sum_some(1)
     back_swap.wait()
+    full_down(1)
     own_rows = rows_of(mp, token_rows)
     far_rows = rows_of(ym, token_rows)
     out_swaps = [
@@ -719,24 +718,26 @@
     keep_out = pltpu.make_async_copy(stage_out, block_out.at[own_rows], s_local.at[2])
     keep_out.start()
 
+    def both_back(m, mix=False):
+        project(m, 1)
+        attention_back(m, 0, mix)
+        attention_back(m, 1, mix)
+        sum_some(1)
+
+    sum_some(1)
     m = 2 * y + (1 - c)
-    attention_back(m, 0, True)
-    attention_back(m, 1, True)
+    both_back(m, True)
     attn_send[...] = attn_grad(m).astype(bf16)
     core_swap = remote(attn_send, attn_core, s_exs.at[7], s_core.at[0], C)
     sum_some(1)
     m = 2 * y + c
-    attention_back(m, 0, True)
-    attention_back(m, 1, True)
-    sum_some(1)
+    both_back(m, True)
     made = attn_grad(m)
     core_swap.wait()
     grad_attn[...] = (made + attn_core[...].astype(f32)).astype(bf16)
     sum_some(1)
     for i in range(2):
-        for g in range(2):
-            attention_back(2 * (1 - y) + i, g)
-    sum_some(1)
+        both_back(2 * (1 - y) + i)
 
     def token_end(g):
         def body(b):
@@ -757,7 +758,6 @@
     on = remote(block_out.at[far_rows], block_out.at[far_rows], s_on.at[0], s_on.at[1], C)
     for g in range(2):
         token_back(g)
-        sum_some(g)
         token_end(g)
         if g == 0:
             for v in range(4):
@@ -769,8 +769,7 @@
         grad_swaps.append(remote(ref, spot, s_tg.at[2 * g], s_tg.at[2 * g + 1], C))
         keep_grads.append(pltpu.make_async_copy(ref, spot, s_local.at[3 + g]))
         keep_grads[g].start()
-        if g == 0:
-            sum_some(1)
+        sum_some(1)
     core_vec.wait()
     vec_pack[1] = vec_pack[0] + vec_got[0]
     across = [X, Y, (2 * z + (1 - x), ym)]
@@ -794,7 +793,6 @@
         for t in range(6):
             vec_out[v : v + 1, 128 * t : 128 * (t + 1)] = total[6 * v + t : 6 * v + t + 1, :]
     sum_end(0)
-    sum_some(4)
     sum_end(1)
     sum_end(2)
     out_swaps[1].wait()

time: 181 us -> 169 us (0.934)
  Pallas kernels: 176 us -> 164 us
    pallas_call x1, Pallas kernels: 169 us -> 157 us  [layer(): pl.pallas_call(functools.partial(layer_kernel, slot_total), out_shape=[ja...]
where the time goes in v5:
time: 169 us
  Pallas kernels  164 us (97%)
  between operations  2.4 us (1%)
    pallas_call x1, Pallas kernels, layer(): pl.pallas_call(functools.partial(layer_kernel, slot_total), out_shape=[ja...  157 us
    pallas_call x1, Pallas kernels, finish(): pl.pallas_call(finish_kernel, out_shape=[jax.ShapeDtypeStruct(block_out.s...  6.54 us

profile of v5, /device:TPU:0, one launch (start us, length us, event | category | flops | bytes accessed | tf_op | source)
XLA Modules:
  0.0 168.7 jit_solution(1861829114663435960)
XLA Ops:
  0.6 1.3 pad_maximum_fusion.refs_4_
  1.9 157.1 %layer.1 = (f32[1,1]{1,0:T(1,128)}, bf16[2048,768]{1,0:T(8,128)(2,1)}, bf16[2048,768]{1,0:T(8,128)(2,1)}, f32[96,768]{1,0:T(8,128)}, f32[96,768]{1,0:T(8,128)}, /*index=5*/f32[96,768]{1,0:T(8,128)}, f32[4,768]{1,0:T(4,128)}) custom-call(bf16[3,96,192]{2,1,0:T(8,128)(2,1)} %refs_0_.1, bf16[192,96]{1,0:T(8,128)(2,1)} %refs_1_.1, bf16[96,768]{1,0:T(8,128)(2,1)} %refs_2_.1, ...), custom_call_target="tpu_custom_call" | custom-call | flops 30000001024 | bytes 40000000 | tf_op jit(solution)/shard_map/layer/pallas_call | solution.py:867
  159.1 0.8 constant_dynamic-slice_fusion
  159.8 0.5 slice_bitcast_fusion
  160.4 6.5 %finish.1 = (bf16[2048,768]{1,0:T(8,128)(2,1)}, f32[2048,768]{1,0:T(8,128)}, f32[3,96,192]{2,1,0:T(8,128)}, f32[192,96]{1,0:T(8,128)}, f32[96,768]{1,0:T(8,128)}, /*index=5*/f32[96,768]{1,0:T(8,128)}) custom-call(bf16[2048,768]{1,0:T(8,128)(2,1)} %get-tuple-element.25.refs_0_, bf16[2048,768]{1,0:T(8,128)(2,1)} %get-tuple-element.26.refs_1_, ...), custom_call_target="tpu_custom_call" | custom-call | tf_op jit(solution)/shard_map/finish/pallas_call | solution.py:940

commit v6 on v5

--- a/solution.py
+++ b/solution.py
@@ -82,16 +82,18 @@
 
 
 def layer_kernel(slot_total, *refs):
-    (w_qkv, w_out, up_own, down_own, norms, valid_own, classes, image_gain, image_bias, image_proj, tokens, ids) = refs[:12]
-    (loss_out, block_out, token_out, attn_out, up_out, down_out, vec_out) = refs[12:19]
-    (w_attn, w_up, w_down, images, smalls, x_ref, a_ref, qkv, hidden, a_two, active, stage_out, image_own, vecs) = refs[19:33]
-    (mask_ref, place_ref, member_ref, h_ends, ends_two, ends_grad, u_ends, g_all, s_all, weight_ref, valid_ref) = refs[33:44]
-    (sum_own, sum_buf, sum_got, d_attn, d_far) = refs[44:49]
-    (grad_down, grad_up, grad_attn, step_x, step_z, attn_send, attn_core, ends_back) = refs[49:57]
-    (vec_buf, vec_pack, vec_got, stage_grad, attn_own, small_own, far_mix) = refs[57:64]
-    gsems = refs[64:92]
-    isems = refs[92:101]
-    (s_local, s_bo, s_on, s_send, s_a2, s_dm, s_dh, s_sum, s_sums, s_x, s_z, s_core, s_v, s_vs, s_tg, s_exs) = refs[101:117]
+    (w_qkv, w_out, up_own, down_own) = refs[:4]
+    norms = refs[4:8]
+    (valid_own, classes, image_gain, image_bias, image_proj, tokens, ids) = refs[8:15]
+    (loss_out, block_out, token_out, attn_out, up_out, down_out, vec_out) = refs[15:22]
+    (w_attn, w_up, w_down, images, smalls, x_ref, a_ref, qkv, hidden, a_two, active, stage_out, image_own, vecs) = refs[22:36]
+    (mask_ref, place_ref, member_ref, h_ends, ends_two, ends_grad, u_ends, g_all, s_all, weight_ref, valid_ref) = refs[36:47]
+    (sum_own, sum_buf, sum_got, d_attn, d_far) = refs[47:52]
+    (grad_down, grad_up, grad_attn, step_x, step_z, attn_send, attn_core, ends_back) = refs[52:60]
+    (vec_buf, vec_pack, vec_got, stage_grad, attn_own, small_own, far_mix) = refs[60:67]
+    gsems = refs[67:95]
+    isems = refs[95:104]
+    (s_local, s_bo, s_on, s_send, s_a2, s_dm, s_dh, s_sum, s_sums, s_x, s_z, s_core, s_v, s_vs, s_tg, s_exs) = refs[104:120]
 
     dp = lax.axis_index("dp")
     mp = lax.axis_index("mp")
@@ -353,7 +355,7 @@
 
     def pack_small():
         shift = lax.broadcasted_iota(jnp.int32, (depth, 384), 1) - lax.broadcasted_iota(jnp.int32, (depth, 384), 0)
-        made = nn(norms[...], (shift == depth * lax.rem(dp, 4)).astype(f32).astype(bf16))
+        made = nn(jnp.concatenate([row[...].astype(f32) for row in norms], axis=0).astype(bf16), (shift == depth * lax.rem(dp, 4)).astype(f32).astype(bf16))
         shift = lax.broadcasted_iota(jnp.int32, (slots, 128), 1) - lax.broadcasted_iota(jnp.int32, (slots, 128), 0)
         flags = jnp.broadcast_to(valid_own[...].astype(f32), (8, slots)).astype(bf16)
         flags = nn(flags, (shift == slots * lax.rem(dp, 2)).astype(f32).astype(bf16))
@@ -875,7 +877,7 @@
             jax.ShapeDtypeStruct((depth, width), f32),
             jax.ShapeDtypeStruct((4, width), f32),
         ],
-        in_specs=[here] * 10 + [there, here],
+        in_specs=[here] * 13 + [there, here],
         out_specs=[here, there, there, here, here, here, here],
         scratch_shapes=scratch,
         compiler_params=pltpu.CompilerParams(
@@ -883,7 +885,7 @@
         ),
         cost_estimate=pl.CostEstimate(flops=30 * 10**9, bytes_accessed=40 * 10**6, transcendentals=10**7),
         name="layer",
-    )(w_qkv, w_out, up_own, down_own, norms, valid, classes, *rest)
+    )(w_qkv, w_out, up_own, down_own, *norms, valid, classes, *rest)
 
 
 def finish_kernel(*refs):
@@ -988,7 +990,7 @@
         w_out,
         w_up,
         w_down.T,
-        jnp.stack([ln1_gain, ln1_bias, ln2_gain, ln2_bias]),
+        [row.reshape(1, -1) for row in (ln1_gain, ln1_bias, ln2_gain, ln2_bias)],
         slot_valid.reshape(1, slots),
         class_tokens,
         image_gain,

time: 169 us -> 168 us (level)
  no operation moved by 1% of the time
where the time goes in v6:
time: 168 us
  Pallas kernels  164 us (98%)
  between operations  2.41 us (1%)
    pallas_call x1, Pallas kernels, layer(): pl.pallas_call(functools.partial(layer_kernel, slot_total), out_shape=[ja...  157 us
    pallas_call x1, Pallas kernels, finish(): pl.pallas_call(finish_kernel, out_shape=[jax.ShapeDtypeStruct(block_out.s...  6.54 us

profile of v6, /device:TPU:0, one launch (start us, length us, event | category | flops | bytes accessed | tf_op | source)
XLA Modules:
  0.0 167.6 jit_solution(16448342456525400132)
XLA Ops:
  0.7 157.4 %layer.1 = (f32[1,1]{1,0:T(1,128)}, bf16[2048,768]{1,0:T(8,128)(2,1)}, bf16[2048,768]{1,0:T(8,128)(2,1)}, f32[96,768]{1,0:T(8,128)}, f32[96,768]{1,0:T(8,128)}, /*index=5*/f32[96,768]{1,0:T(8,128)}, f32[4,768]{1,0:T(4,128)}) custom-call(bf16[3,96,192]{2,1,0:T(8,128)(2,1)} %refs_0_.1, bf16[192,96]{1,0:T(8,128)(2,1)} %refs_1_.1, bf16[96,768]{1,0:T(8,128)(2,1)} %refs_2_.1, ...), custom_call_target="tpu_custom_call" | custom-call | flops 30000001024 | bytes 40000000 | tf_op jit(solution)/shard_map/layer/pallas_call | solution.py:869
  158.0 0.8 constant_dynamic-slice_fusion
  158.8 0.5 slice_bitcast_fusion
  159.3 6.5 %finish.1 = (bf16[2048,768]{1,0:T(8,128)(2,1)}, f32[2048,768]{1,0:T(8,128)}, f32[3,96,192]{2,1,0:T(8,128)}, f32[192,96]{1,0:T(8,128)}, f32[96,768]{1,0:T(8,128)}, /*index=5*/f32[96,768]{1,0:T(8,128)}) custom-call(bf16[2048,768]{1,0:T(8,128)(2,1)} %get-tuple-element.25.refs_0_, bf16[2048,768]{1,0:T(8,128)(2,1)} %get-tuple-element.26.refs_1_, ...), custom_call_target="tpu_custom_call" | custom-call | tf_op jit(solution)/shard_map/finish/pallas_call | solution.py:942
